TPU v7x, 512 devices: a whole 4x4x16 slice. The times are simulated.
512 devices in a mesh: grp: 32 (over z_lo, y, core), tp: 16 (over x, z_hi).
Axes of the slice: x: 4, y: 4, z: 16 (z_hi: 4, z_lo: 4; z = z_hi * 4 + z_lo), core: 2. Of those that a mesh axis runs over, the one named last changes fastest.
Arguments:
- grad_top: bfloat16 [96, 128, 4608], P('grp', None, 'tp'), parts along dimension 0, may hold values from -6 to 6
- post_scale: float32 [128], replicated, may hold values from 0.3 to 3
- post_gain: bfloat16 [4608], P('tp'), may hold values from 0.25 to 1.75
- patterns: bfloat16 [32, 128, 128], P('tp'), may hold values from 0 to 1, as said below
- out_proj: bfloat16 [4096, 4608], P('tp'), may hold values from -0.09375 to 0.09375
- value_proj: bfloat16 [2048, 4608], P('tp'), may hold values from -0.125 to 0.125
- pre_scale: float32 [128], replicated, may hold values from 0.3 to 3
- pre_gain: bfloat16 [4608], P('tp'), may hold values from 0.25 to 1.75
- decoder: bfloat16 [2048, 4608], P('tp'), may hold values from -0.09375 to 0.09375
- block_ids: int32 [128, 2], replicated, may hold values from 0 to 15, all different within a row
- feature_acts: bfloat16 [128, 256], P('tp'), may hold values from 0.099609375 to 4
Outputs:
- attribution: float32 [96, 128, 256], P('grp', 'tp'), parts along dimension 0
There are 32 independent parts, one for each index of `grp`. A program takes and returns all parts, laid end to end along the dimension named above; an argument that names none is the same for every part. Nothing has to cross between parts.
Inputs may be any that keep to these rules, and one draw needn't show every extreme that they name: `block_ids`: each token names 2 different blocks. `patterns`: each query row of each head is zero past its own position and sums to one.
All inputs are finite; a program needn't handle non-finite values.
Results may differ from a plain program's by a relative error of at most 0.019.
Values may be sent and summed in bfloat16 or wider, within the bound.
No kernel may reach another device: no remote copies, remote signals or barrier semaphores. Data moves between devices by JAX's collectives and lax.ppermute only.
A program may use at most 64 MiB of HBM per device.

v0:
```python
import jax
import jax.numpy as jnp
from jax import lax
from jax.sharding import PartitionSpec as P

BLK = 128


def contract_cols(left, right):
    return lax.dot_general(
        left, right, (((1,), (1,)), ((), ())), preferred_element_type=jnp.float32
    )


def shards(
    grad_top,
    post_scale,
    post_gain,
    patterns,
    out_proj,
    value_proj,
    pre_scale,
    pre_gain,
    decoder,
    block_ids,
    feature_acts,
):
    targets, seq_len, width_local = grad_top.shape
    rows = targets * seq_len
    head_local = patterns.shape[0]
    head_size = out_proj.shape[0] // head_local
    kv_local = value_proj.shape[0] // head_size
    blocks_local = decoder.shape[0] // BLK
    post_rows = jnp.tile(post_scale, targets)[:, None]
    pre_rows = jnp.tile(pre_scale, targets)[:, None]
    top_local = grad_top.astype(jnp.float32).reshape(rows, width_local)
    scaled = (top_local * post_gain.astype(jnp.float32)[None, :] * post_rows).astype(jnp.bfloat16)
    columns = out_proj
    head_grad = contract_cols(lax.all_gather(scaled, "tp", axis=1, tiled=True), columns)
    grid_heads = head_grad.astype(jnp.bfloat16).reshape(targets, seq_len, head_local, head_size)
    mixed = jnp.einsum("hts,rthj->rshj", patterns, grid_heads, preferred_element_type=jnp.float32)
    paired = mixed.reshape(targets, seq_len, kv_local, head_local // kv_local, head_size).sum(
        axis=3
    )
    value_grad = paired.astype(jnp.bfloat16).reshape(rows, kv_local * head_size)
    columns = value_proj
    attn_local = (
        lax.psum_scatter(
            lax.dot_general(
                columns, value_grad, (((0,), (1,)), ((), ())), preferred_element_type=jnp.float32
            ).astype(jnp.bfloat16),
            "tp",
            scatter_dimension=0,
            tiled=True,
        )
        .astype(jnp.float32)
        .T
    )
    bottom = (top_local + pre_gain.astype(jnp.float32)[None, :] * pre_rows * attn_local).astype(
        jnp.bfloat16
    )
    columns = decoder
    scores = contract_cols(lax.all_gather(bottom, "tp", axis=1, tiled=True), columns)
    token_local = feature_acts.shape[0]
    slots = block_ids.shape[1]
    acts = feature_acts.astype(jnp.float32).reshape(token_local, slots, BLK)
    score_grid = scores.reshape(targets, seq_len, blocks_local * BLK)
    local_ids = block_ids - lax.axis_index("tp") * blocks_local
    grid = score_grid.reshape(targets, seq_len, blocks_local, BLK)
    hit = local_ids[:, :, None] == jnp.arange(blocks_local, dtype=jnp.int32)[None, None, :]
    spread = jnp.sum(
        jnp.where(hit[None, :, :, :, None], grid[:, :, None, :, :], jnp.float32(0.0)), axis=3
    )
    summed = lax.psum_scatter(
        spread.reshape(targets, seq_len, slots * BLK).astype(jnp.bfloat16),
        "tp",
        scatter_dimension=1,
        tiled=True,
    ).astype(jnp.float32)
    picked = summed.reshape(targets, token_local, slots, BLK)
    return (acts[None] * picked).reshape(targets, token_local, slots * BLK)


def solution(mesh):
    in_specs = (
        P("grp", None, "tp"),
        P(),
        P("tp"),
        P("tp", None, None),
        P("tp", None),
        P("tp", None),
        P(),
        P("tp"),
        P("tp", None),
        P(),
        P("tp", None),
    )
    out_specs = P("grp", "tp", None)
    return jax.shard_map(shards, mesh=mesh, in_specs=in_specs, out_specs=out_specs, check_vma=False)
```

profile of v0, /device:TPU:24, one launch (start us, length us, event | category | flops | bytes accessed | tf_op | source)
XLA Modules:
  0.0 533.7 jit_solution(16278853723591861518)
XLA Ops:
  6.5 0.8 broadcast_bitcast_fusion
  7.3 0.7 convert_element_type.46
  8.0 1.7 fusion.3
  9.9 124.9 %all-gather.3.cloned.1.call-done = bf16[384,4608]{0,1:T(8,128)(2,1)} async-done(((bf16[384,288]{0,1:T(8,128)(2,1)}), bf16[384,4608]{0,1:T(8,128)(2,1)}) %all-gather.3.cloned.1.call-update) | async-done | bytes 3538960 | tf_op jit(solution)/shard_map/all_gather | solution.py:39
  134.8 3.8 convolution_convert_fusion.1
  138.6 1.7 reshape.44
  140.2 1.2 fusion.1
  141.4 2.9 fusion
  144.2 5.8 %copy.32 = bf16[4608,384]{1,0:T(8,128)(2,1)} copy(bf16[4608,384]{0,1:T(8,128)(2,1)} %fusion) | data formatting | bytes 7077888
  150.1 0.6 copy-done.4
  150.7 144.3 %reduce-scatter.7.cloned.1.call-done = bf16[288,384]{1,0:T(8,128)(2,1)} async-done(((bf16[4608,384]{1,0:T(8,128)(2,1)}), bf16[288,384]{1,0:T(8,128)(2,1)}) %reduce-scatter.7.cloned.1.call-update) | async-done | bytes 221200 | tf_op jit(solution)/shard_map/reduce_scatter | solution.py:48
  295.0 1.9 fusion.4
  297.0 0.6 broadcast_in_dim.32
  297.6 1.5 copy.24
  299.0 113.8 %all-gather.5.cloned.1.call-done = bf16[384,4608]{0,1:T(8,128)(2,1)} async-done(((bf16[384,288]{0,1:T(8,128)(2,1)}), bf16[384,4608]{0,1:T(8,128)(2,1)}) %all-gather.5.cloned.1.call-update) | async-done | bytes 3538960 | tf_op jit(solution)/shard_map/all_gather | solution.py:63
  412.8 3.1 fusion.7
  415.9 0.1 broadcast_in_dim.36
  416.1 0.1 broadcast_in_dim.37
  416.2 0.8 select_convert_fusion
  417.0 0.2 copy.34
  417.2 0.7 copy.37
  417.9 107.9 %reduce-scatter.9.cloned.1.call-done = bf16[8,768]{1,0:T(8,128)(2,1)} async-done(((bf16[128,768]{1,0:T(8,128)(2,1)}), bf16[8,768]{1,0:T(8,128)(2,1)}) %reduce-scatter.9.cloned.1.call-update) | async-done | bytes 12304
  525.8 0.7 reshape.52
  526.5 0.6 convert_multiply_fusion
  (25 shorter events, 0.2 us)
Async XLA Ops:
  6.5 128.2 %copy-start = (bf16[256,4608]{1,0:T(8,128)(2,1)S(1)}, bf16[256,4608]{1,0:T(8,128)(2,1)}, u32[]{:S(2)}) copy-start(bf16[256,4608]{1,0:T(8,128)(2,1)} %param.15) | copy-start | bytes 7077892
  6.5 128.2 %all-gather.3.cloned.1.call-start = ((), (), s32[]{:S(2)}) async-start(), calls=%async_computation.2 | async-start | bytes 3760128 | tf_op jit(solution)/shard_map/all_gather | solution.py:39
  9.8 131.6 %copy-start.1 = (bf16[128,4608]{1,0:T(8,128)(2,1)S(1)}, bf16[128,4608]{1,0:T(8,128)(2,1)}, u32[]{:S(2)}) copy-start(bf16[128,4608]{1,0:T(8,128)(2,1)} %param.16) | copy-start | bytes 3538948
  9.8 285.2 %reduce-scatter.7.cloned.1.call-start = ((), (), s32[]{:S(2)}) async-start(), calls=%async_computation.4 | async-start | bytes 3760128 | tf_op jit(solution)/shard_map/reduce_scatter | solution.py:48
  150.0 0.7 copy-start.4
  150.0 0.7 copy-start.6
  150.0 146.9 %copy-start.5 = (s32[128,2]{0,1:T(2,128)S(1)}, s32[128,2]{0,1:T(2,128)}, u32[]{:S(2)}) copy-start(s32[128,2]{0,1:T(2,128)} %param.20) | copy-start | bytes 3076
  150.0 262.8 %copy-start.2 = (bf16[128,4608]{1,0:T(8,128)(2,1)S(1)}, bf16[128,4608]{1,0:T(8,128)(2,1)}, u32[]{:S(2)}) copy-start(bf16[128,4608]{1,0:T(8,128)(2,1)} %param.19) | copy-start | bytes 3538948
  150.0 262.8 %all-gather.5.cloned.1.call-start = ((), (), s32[]{:S(2)}) async-start(), calls=%async_computation.3 | async-start | bytes 3760128 | tf_op jit(solution)/shard_map/all_gather | solution.py:63
  296.9 228.9 %reduce-scatter.9.cloned.1.call-start = ((), (), s32[]{:S(2)}) async-start(), calls=%async_computation.5 | async-start | bytes 208896
  299.0 118.9 %copy-start.3 = (bf16[8,256]{1,0:T(8,128)(2,1)S(1)}, bf16[8,256]{1,0:T(8,128)(2,1)}, u32[]{:S(2)}) copy-start(bf16[8,256]{1,0:T(8,128)(2,1)} %param.21) | copy-start | bytes 12292
Sparse Core Ops, SparseCore 0:
  10.4 124.2 all-gather.2
  150.2 144.7 reduce-scatter.6
  298.0 114.7 all-gather.4
  418.0 107.7 reduce-scatter.8
where the time goes:
time: 534 us
  waiting for transfers between devices  491 us (92%)
  between operations  13.2 us (2%)
  local copies, waits for them, and re-layouts  12.7 us (2%)
  matrix products  10.9 us (2%)
  other arithmetic  5.73 us (1%)
    reduce_scatter x1, waiting for transfers between devices, shards(): lax.psum_scatter(lax.dot_general(columns, value_grad, (((0,), (1,)), ((),...  144 us
    all_gather x1, waiting for transfers between devices, shards(): lax.all_gather(scaled, 'tp', axis=1, tiled=True)  125 us
    all_gather x1, waiting for transfers between devices, shards(): lax.all_gather(bottom, 'tp', axis=1, tiled=True)  114 us
    unnamed x5, waiting for transfers between devices  108 us
  transfers between devices with their start and end apart: 4, of which 4 were waited for; matrix products, arithmetic and copies ran while one was open for 0% of the time, Pallas kernels for 0%

commit v1 on v0

v1 whole, which is shorter than its diff:
```python
import functools

import jax
import jax.numpy as jnp
from jax import lax
from jax.experimental import pallas as pl
from jax.experimental.pallas import tpu as pltpu
from jax.sharding import Mesh, PartitionSpec as P

BLK = 128
AXES = ("zl", "y", "c", "x", "zh")
GRP = ("zl", "y", "c")
TP = ("x", "zh")
F32 = jnp.float32
BF16 = jnp.bfloat16
PARAMS = pltpu.CompilerParams(vmem_limit_bytes=40 * 1024 * 1024)


def source_block(zh, zl, n):
    return (zh + (n - 1, n - 2, 0, 1)[zl]) % n


def decoder_moves(sizes):
    nzl, ny, nc, nx, nzh = sizes
    senders = (nzl - 1, 2, 1, 0)
    at = lambda zl, y, c, x, zh: (((zl * ny + y) * nc + c) * nx + x) * nzh + zh
    return [
        (at(senders[zl], y, c, x, source_block(zh, zl, nzh)), at(zl, y, c, x, zh))
        for zl in range(nzl)
        for y in range(ny)
        for c in range(nc)
        for x in range(nx)
        for zh in range(nzh)
    ]


def dot(left, right, dims):
    return lax.dot_general(left, right, (dims, ((), ())), preferred_element_type=F32)


def fold_kernel(rows, dec_ref, gain_ref, value_ref, out_ref, acc_ref):
    step = pl.program_id(0)

    @pl.when(step == 0)
    def _():
        acc_ref[...] = jnp.zeros_like(acc_ref)

    gain = gain_ref[0].astype(F32)[0:1]
    wide = dec_ref.shape[2]
    dec = (dec_ref[...].reshape(-1, wide).astype(F32) * gain).astype(BF16)
    acc_ref[...] += dot(dec, value_ref[...], ((1,), (1,)))

    @pl.when(step == pl.num_programs(0) - 1)
    def _():
        out_ref[...] = acc_ref[...].astype(BF16)


def main_kernel(
    geometry,
    blocks_ref,
    x_ref,
    out_proj_ref,
    dec_ref,
    gain_ref,
    post_ref,
    pre_ref,
    patterns_ref,
    ids_ref,
    folded_ref,
    out_ref,
    acc_ref,
    value_ref,
):
    targets, seq, heads, head, nzl, nx, owners = geometry
    step = pl.program_id(0)
    width = heads * head

    @pl.when(step == 0)
    def _():
        acc_ref[...] = jnp.zeros_like(acc_ref)

    gain = gain_ref[0].astype(F32)[0:1]
    proj = (out_proj_ref[...].astype(F32) * gain).astype(BF16)
    left = jnp.concatenate([proj, dec_ref[...]], axis=0)
    acc_ref[...] += dot(left, x_ref[...], ((1,), (0,)))

    @pl.when(step == pl.num_programs(0) - 1)
    def _():
        head_grad = (acc_ref[0:width, :] * post_ref[...]).astype(BF16)
        for r in range(targets):
            cols = slice(r * seq, (r + 1) * seq)
            mixed = jnp.zeros((head, seq), F32)
            for h in range(heads):
                mixed += dot(
                    head_grad[h * head : (h + 1) * head, cols], patterns_ref[h], ((1,), (0,))
                )
            value_ref[cols, :] = mixed.T.astype(BF16)
        value = value_ref[...]
        ids = ids_ref[...]
        slots = ids.shape[1]
        totals = [jnp.zeros((targets * seq, BLK), F32) for _ in range(slots)]
        for zl in range(nzl):
            for x in range(nx):
                rows = folded_ref[zl, :, x].reshape(BLK, head)
                scores = dot(value, rows, ((1,), (1,)))
                name = blocks_ref[zl * nx + x]
                for k in range(slots):
                    totals[k] += jnp.where(ids[:, k : k + 1] == name, scores, 0.0)
        own = blocks_ref[nzl * nx]
        direct = acc_ref[width:, :].T
        for k in range(slots):
            totals[k] = totals[k] * pre_ref[...] + jnp.where(
                ids[:, k : k + 1] == own, direct, 0.0
            )
        piece = seq // owners
        for i in range(owners):
            for r in range(targets):
                lo = r * seq + i * piece
                both = jnp.concatenate([t[lo : lo + piece] for t in totals], axis=0)
                out_ref[i, :, r * BLK : (r + 1) * BLK] = both.astype(BF16)


def last_kernel(targets, parts_ref, acts_ref, out_ref):
    total = jnp.sum(parts_ref[...].astype(F32), axis=0)
    tokens = acts_ref.shape[0]
    slots = acts_ref.shape[1] // BLK
    for r in range(targets):
        for k in range(slots):
            cols = slice(k * BLK, (k + 1) * BLK)
            out_ref[r, :, cols] = (
                total[k * tokens : (k + 1) * tokens, r * BLK : (r + 1) * BLK] * acts_ref[:, cols]
            )


def shards(
    sizes,
    grad_top,
    post_scale,
    post_gain,
    patterns,
    out_proj,
    value_proj,
    pre_scale,
    pre_gain,
    decoder,
    block_ids,
    feature_acts,
):
    nzl, ny, nc, nx, nzh = sizes
    owners = nx * nzh
    targets, seq, local = grad_top.shape
    rows = targets * seq
    heads, head = patterns.shape[0], out_proj.shape[0] // patterns.shape[0]
    width = out_proj.shape[1]
    chunk = width // nx
    slots = block_ids.shape[1]
    copies = ny * nc
    share = BLK // copies
    tokens = feature_acts.shape[0]
    zl, zh, x = lax.axis_index("zl"), lax.axis_index("zh"), lax.axis_index("x")
    copy = lax.axis_index(("y", "c"))

    mine = lax.dynamic_slice_in_dim(decoder, copy * share, share, axis=0)
    near = lax.ppermute(mine, AXES, decoder_moves(sizes))

    turned = grad_top.transpose(2, 0, 1).reshape(local, rows)
    gains = jnp.pad(jnp.stack([post_gain, pre_gain]), ((0, 14), (0, rows - local)))
    columns = lax.all_gather(
        jnp.concatenate([turned, gains], axis=0), "zh", axis=0, tiled=False
    )
    wide = lax.all_gather(columns[:, :local].reshape(chunk, rows), "x", axis=0, tiled=True)

    both = columns[:, local : local + 2, :local].transpose(1, 0, 2).reshape(1, 2 * chunk)
    both = jnp.pad(both, ((0, 15), (0, width - 2 * chunk)))
    near = lax.all_gather(jnp.concatenate([near, both], axis=0), "x", axis=0, tiled=False)

    folded = pl.pallas_call(
        functools.partial(fold_kernel, nx * share),
        grid=(nx,),
        in_specs=[
            pl.BlockSpec((nx, share, chunk), lambda i: (0, 0, i)),
            pl.BlockSpec((1, 16, chunk), lambda i: (i, share // 16, 1)),
            pl.BlockSpec((head, chunk), lambda i: (0, i)),
        ],
        out_specs=pl.BlockSpec((nx * share, head), lambda i: (0, 0)),
        out_shape=jax.ShapeDtypeStruct((nx * share, head), BF16),
        scratch_shapes=[pltpu.VMEM((nx * share, head), F32)],
        compiler_params=PARAMS,
    )(near, near, value_proj)
    folded = lax.all_gather(folded, ("y", "c"), axis=0, tiled=False)
    folded = lax.all_gather(folded, "zl", axis=0, tiled=False)
    folded = folded.reshape(nzl, copies, nx, share, head)

    names = [
        i * nzh + (zh + (nzh - 1, nzh - 2, 0, 1)[j]) % nzh for j in range(nzl) for i in range(nx)
    ]
    names = jnp.stack(names + [x * nzh + zh]).astype(jnp.int32)
    post_row = jnp.tile(post_scale, targets)[None, :]
    pre_col = jnp.tile(pre_scale, targets)[:, None]
    ids = jnp.tile(block_ids, (targets, 1))

    whole = lambda *dims: pl.BlockSpec(dims, lambda i, s: (0,) * len(dims))
    parts = pl.pallas_call(
        functools.partial(main_kernel, (targets, seq, heads, head, nzl, nx, owners)),
        grid_spec=pltpu.PrefetchScalarGridSpec(
            num_scalar_prefetch=1,
            grid=(nx,),
            in_specs=[
                pl.BlockSpec((chunk, rows), lambda i, s: (i, 0)),
                pl.BlockSpec((heads * head, chunk), lambda i, s: (0, i)),
                pl.BlockSpec((BLK, chunk), lambda i, s: (0, i)),
                pl.BlockSpec((1, 16, chunk), lambda i, s: (i, share // 16, 0)),
                whole(1, rows),
                whole(rows, 1),
                whole(heads, seq, seq),
                whole(rows, slots),
                whole(nzl, copies, nx, share, head),
            ],
            out_specs=whole(owners, slots * tokens, targets * BLK),
            scratch_shapes=[
                pltpu.VMEM((heads * head + BLK, rows), F32),
                pltpu.VMEM((rows, head), BF16),
            ],
        ),
        out_shape=jax.ShapeDtypeStruct((owners, slots * tokens, targets * BLK), BF16),
        compiler_params=PARAMS,
    )(names, wide, out_proj, decoder, near, post_row, pre_col, patterns, ids, folded)

    parts = lax.all_to_all(parts, TP, 0, 0)
    return pl.pallas_call(
        functools.partial(last_kernel, targets),
        out_shape=jax.ShapeDtypeStruct((targets, tokens, slots * BLK), F32),
        compiler_params=PARAMS,
    )(parts, feature_acts.astype(F32))


def solution(mesh):
    sizes = (4, 4, mesh.devices.size // 256, 4, 4)
    mesh = Mesh(mesh.devices.reshape(sizes), AXES)
    in_specs = (
        P(GRP, None, TP),
        P(),
        P(TP),
        P(TP, None, None),
        P(TP, None),
        P(TP, None),
        P(),
        P(TP),
        P(TP, None),
        P(),
        P(TP, None),
    )
    return jax.shard_map(
        functools.partial(shards, sizes),
        mesh=mesh,
        in_specs=in_specs,
        out_specs=P(GRP, TP, None),
        check_vma=False,
    )
```

time: 534 us -> 197 us (0.37)
  waiting for transfers between devices: 491 us -> 66 us
  blocking collectives: 0 us -> 70.9 us
  starting transfers between devices: 0.13 us -> 25.1 us
  matrix products: 10.9 us -> 0 us
  Pallas kernels: 0 us -> 8.17 us
    all_gather x2, waiting for transfers between devices: 239 us -> 47.2 us  [the longest x1 26.6 us: shards(): lax.all_gather(jnp.concatenate([near, both], axis=0), 'x', axis=0, tiled=...]
    reduce_scatter x1 -> x0, waiting for transfers between devices: 144 us -> none  [shards(): lax.psum_scatter(lax.dot_general(columns, value_grad, (((0,), (1,)), ((),...]
    unnamed x5 -> x2, waiting for transfers between devices: 108 us -> 0.03 us
    all_gather x0 -> x3, blocking collectives: none -> 70.9 us  [the longest x1 41.9 us: shards(): lax.all_gather(jnp.concatenate([turned, gains], axis=0), 'zh', axis=0, ti...]
    all_to_all x0 -> x1, waiting for transfers between devices: none -> 18.7 us  [shards(): parts = lax.all_to_all(parts, TP, 0, 0)]
    all_to_all x0 -> x1, starting transfers between devices: none -> 13.7 us  [shards(): parts = lax.all_to_all(parts, TP, 0, 0)]
    ppermute x0 -> x1, starting transfers between devices: none -> 11.4 us  [shards(): near = lax.ppermute(mine, AXES, decoder_moves(sizes))]
    dot_general x4 -> x0, matrix products: 10.9 us -> none  [the longest x2 6.92 us: contract_cols(): lax.dot_general(left, right, (((1,), (1,)), ((), ())), preferred_element_...]
  transfers between devices with their start and end apart: 4 -> 4, of which waited for: 4 -> 3; matrix products, arithmetic and copies ran while one was open for 0% -> 2% of each run, Pallas kernels for 0% -> 1%
where the time goes in v1:
time: 197 us; the launch traced here: 195 us
  blocking collectives  70.9 us (36%)
  waiting for transfers between devices  66 us (34%)
  starting transfers between devices  25.1 us (13%)
  between operations  13.7 us (7%)
  local copies, waits for them, and re-layouts  10.1 us (5%)
  Pallas kernels  8.17 us (4%)
    all_gather x1, blocking collectives, shards(): lax.all_gather(jnp.concatenate([turned, gains], axis=0), 'zh', axis=0, ti...  41.9 us
    all_gather x1, waiting for transfers between devices, shards(): lax.all_gather(jnp.concatenate([near, both], axis=0), 'x', axis=0, tiled=...  26.6 us
    all_gather x1, waiting for transfers between devices, shards(): lax.all_gather(columns[:, :local].reshape(chunk, rows), 'x', axis=0, tile...  20.6 us
    all_to_all x1, waiting for transfers between devices, shards(): parts = lax.all_to_all(parts, TP, 0, 0)  18.7 us
    all_gather x1, blocking collectives, shards(): folded = lax.all_gather(folded, 'zl', axis=0, tiled=False)  16.2 us
    all_to_all x1, starting transfers between devices, shards(): parts = lax.all_to_all(parts, TP, 0, 0)  13.7 us
    all_gather x1, blocking collectives, shards(): folded = lax.all_gather(folded, ('y', 'c'), axis=0, tiled=False)  12.8 us
    ppermute x1, starting transfers between devices, shards(): near = lax.ppermute(mine, AXES, decoder_moves(sizes))  11.4 us
  transfers between devices with their start and end apart: 4, of which 3 were waited for; matrix products, arithmetic and copies ran while one was open for 2% of the time, Pallas kernels for 1%

profile of v1, /device:TPU:24, one launch (start us, length us, event | category | flops | bytes accessed | tf_op | source)
XLA Modules:
  0.0 194.7 jit_solution(14059510714129217325)
XLA Ops:
  6.5 1.0 constant_dynamic-slice_fusion
  7.5 11.4 %collective-permute-start = (bf16[16,4608]{1,0:T(8,128)(2,1)S(1)}, bf16[16,4608]{1,0:T(8,128)(2,1)S(1)}, u32[]{:S(2)}, u32[]{:S(2)}) collective-permute-start(bf16[16,4608]{1,0:T(8,128)(2,1)S(1)} %constant_dynamic-slice_fusion), channel_id=1, source_target_pairs={{387,0},{384,1},{385,2},{386,3},{391,4},{388,5},{389,6},{390,7},{3... | collective-permute-start | bytes 442376 | tf_op jit(solution)/shard_map/ppermute | solution.py:164
  18.9 0.7 stack.82
  19.6 0.7 stack.81
  20.4 41.9 %all-gather = bf16[1216,384]{1,0:T(8,128)(2,1)S(1)} all-gather(bf16[304,384]{1,0:T(8,128)(2,1)S(1)} %pad_maximum_fusion), channel_id=2, replica_groups=mesh['zl'=4,'y'=4,'c'=2,'x'=4,'zh'=4] {'zh'}, dimensions={0}, use_global_device_ids=true | all-gather | bytes 1167360 | tf_op jit(solution)/shard_map/all_gather | solution.py:168
  62.3 0.1 reshape.20
  62.4 0.7 fusion.1
  63.3 1.0 slice.8
  64.4 0.1 copy.25
  64.6 0.1 copy.20
  64.7 0.1 stack.80.blocks_ref
  64.8 26.6 %all-gather.9.cloned.1.call-done = bf16[128,4608]{1,0:T(8,128)(2,1)} async-done(((bf16[32,4608]{1,0:T(8,128)(2,1)}), bf16[128,4608]{1,0:T(8,128)(2,1)}) %all-gather.9.cloned.1.call-update) | async-done | bytes 1179664 | tf_op jit(solution)/shard_map/all_gather | solution.py:175
  91.4 1.3 copy-done.1
  92.7 1.3 copy-done.6
  94.0 1.1 shard_map.109
  95.1 12.8 %all-gather.2 = bf16[512,128]{1,0:T(8,128)(2,1)S(1)} all-gather(bf16[64,128]{1,0:T(8,128)(2,1)S(1)} %shard_map.109), channel_id=4, replica_groups=mesh['zl'=4,'y'=4,'c'=2,'x'=4,'zh'=4] {'y','c'}, dimensions={0}, use_global_device_ids=true | all-gather | bytes 147456 | tf_op jit(solution)/shard_map/all_gather | solution.py:190
  107.9 16.2 %all-gather.3 = bf16[32,64,128]{2,1,0:T(8,128)(2,1)S(1)} all-gather(bf16[8,64,128]{2,1,0:T(8,128)(2,1)S(1)} %bitcast.54), channel_id=5, replica_groups=mesh['zl'=4,'y'=4,'c'=2,'x'=4,'zh'=4] {'zl'}, dimensions={0}, use_global_device_ids=true | all-gather | bytes 655360 | tf_op jit(solution)/shard_map/all_gather | solution.py:191
  124.1 20.6 %all-gather.7.cloned.1.call-done.x_ref = bf16[4608,384]{1,0:T(8,128)(2,1)} async-done(((bf16[1152,384]{1,0:T(8,128)(2,1)}), bf16[4608,384]{1,0:T(8,128)(2,1)}) %all-gather.7.cloned.1.call-update) | async-done | bytes 3538960 | tf_op jit(solution)/shard_map/all_gather | solution.py:171
  144.7 2.0 %copy-done.3 = bf16[4608,384]{1,0:T(8,128)(2,1)S(1)} copy-done((bf16[4608,384]{1,0:T(8,128)(2,1)S(1)}, bf16[4608,384]{1,0:T(8,128)(2,1)}, u32[]{:S(2)}) %copy-start.3) | copy-done | bytes 3538968
  146.7 1.7 copy-done.4
  148.4 6.4 %shard_map.110 = bf16[16,16,384]{2,1,0:T(8,128)(2,1)} custom-call(s32[17]{0:T(128)S(1)} %stack.80.blocks_ref, bf16[4608,384]{1,0:T(8,128)(2,1)S(1)} %copy-done.3, bf16[256,4608]{1,0:T(8,128)(2,1)S(1)} %copy-done.4, bf16[128,4608]{1,0:T(8,128)(2,1)S(1)} %copy-done.5, bf16[4,32,4608]{2,1,0:T(8,128)(2,1)S(1)} %bitcast.46, f32[1,384]{1,0:T(1,128)S(1)} %bitcast.50, ...), custom_call_target="tpu_custom_call" | custom-call | tf_op jit(solution)/shard_map/pallas_call | solution.py:203
  154.8 13.7 %all-to-all-start = ((bf16[16,16,384]{2,1,0:T(8,128)(2,1)}), bf16[16,16,384]{2,1,0:T(8,128)(2,1)S(1)}, u32[]{:S(2)}, u32[]{:S(2)}) async-start(bf16[16,16,384]{2,1,0:T(8,128)(2,1)} %shard_map.110), calls=%async_computation | async-start | bytes 393216 | tf_op jit(solution)/shard_map/all_to_all | solution.py:229
  168.5 18.7 %all-to-all-done.parts_ref = bf16[16,16,384]{2,1,0:T(8,128)(2,1)S(1)} async-done(((bf16[16,16,384]{2,1,0:T(8,128)(2,1)}), bf16[16,16,384]{2,1,0:T(8,128)(2,1)S(1)}, u32[]{:S(2)}, u32[]{:S(2)}) %all-to-all-start) | async-done | bytes 196640 | tf_op jit(solution)/shard_map/all_to_all | solution.py:229
  187.2 0.6 shard_map.111
  (36 shorter events, 0.2 us)
Async XLA Ops:
  6.5 13.7 %copy-start = (bf16[3,128,288]{1,2,0:T(8,128)(2,1)S(1)}, bf16[3,128,288]{1,2,0:T(8,128)(2,1)}, u32[]{:S(2)}) copy-start(bf16[3,128,288]{1,2,0:T(8,128)(2,1)} %param.11) | copy-start | bytes 663556
  6.5 84.9 %all-gather.9.cloned.1.call-start = ((), (), s32[]{:S(2)}) async-start(), calls=%async_computation.2 | async-start | bytes 1474560 | tf_op jit(solution)/shard_map/all_gather | solution.py:175
  7.5 54.9 %collective-permute-start = (bf16[16,4608]{1,0:T(8,128)(2,1)S(1)}, bf16[16,4608]{1,0:T(8,128)(2,1)S(1)}, u32[]{:S(2)}, u32[]{:S(2)}) collective-permute-start(bf16[16,4608]{1,0:T(8,128)(2,1)S(1)} %constant_dynamic-slice_fusion), channel_id=1, source_target_pairs={{387,0},{384,1},{385,2},{386,3},{391,4},{388,5},{389,6},{390,7},{3... | collective-permute-start | bytes 442376 | tf_op jit(solution)/shard_map/ppermute | solution.py:164
  63.2 1.2 copy-start.10
  63.2 1.2 copy-start.11
  63.2 1.4 copy-start.9
  63.2 81.5 %all-gather.7.cloned.1.call-start = ((), (), s32[]{:S(2)}) async-start(), calls=%async_computation.1 | async-start | bytes 4423680 | tf_op jit(solution)/shard_map/all_gather | solution.py:171
  91.4 1.3 copy-start.1
  92.7 1.3 copy-start.6
  94.0 50.7 %copy-start.2 = (bf16[128,4608]{1,0:T(8,128)(2,1)S(1)}, bf16[128,4608]{1,0:T(8,128)(2,1)}, u32[]{:S(2)}) copy-start(bf16[128,4608]{1,0:T(8,128)(2,1)} %all-gather.9.cloned.1.call-done) | copy-start | bytes 3538948
  94.0 50.8 %copy-start.5 = (bf16[128,4608]{1,0:T(8,128)(2,1)S(1)}, bf16[128,4608]{1,0:T(8,128)(2,1)}, u32[]{:S(2)}) copy-start(bf16[128,4608]{1,0:T(8,128)(2,1)} %dec_ref.1) | copy-start | bytes 3538948
  94.0 50.8 %copy-start.7 = (bf16[2,128,128]{2,1,0:T(8,128)(2,1)S(1)}, bf16[2,128,128]{2,1,0:T(8,128)(2,1)}, u32[]{:S(2)}) copy-start(bf16[2,128,128]{2,1,0:T(8,128)(2,1)} %patterns_ref.1) | copy-start | bytes 196612
  144.7 2.0 %copy-start.3 = (bf16[4608,384]{1,0:T(8,128)(2,1)S(1)}, bf16[4608,384]{1,0:T(8,128)(2,1)}, u32[]{:S(2)}) copy-start(bf16[4608,384]{1,0:T(8,128)(2,1)} %all-gather.7.cloned.1.call-done.x_ref) | copy-start | bytes 10616836
  146.7 1.7 copy-start.4
  148.4 20.1 %copy-start.8 = (bf16[8,256]{1,0:T(8,128)(2,1)S(1)}, bf16[8,256]{1,0:T(8,128)(2,1)}, u32[]{:S(2)}) copy-start(bf16[8,256]{1,0:T(8,128)(2,1)} %param.21) | copy-start | bytes 12292
  154.8 32.5 %all-to-all-start = ((bf16[16,16,384]{2,1,0:T(8,128)(2,1)}), bf16[16,16,384]{2,1,0:T(8,128)(2,1)S(1)}, u32[]{:S(2)}, u32[]{:S(2)}) async-start(bf16[16,16,384]{2,1,0:T(8,128)(2,1)} %shard_map.110), calls=%async_computation | async-start | bytes 393216 | tf_op jit(solution)/shard_map/all_to_all | solution.py:229
Sparse Core Ops, SparseCore 0:
  63.3 28.0 all-gather.8
  93.5 51.1 all-gather.6

commit v2 on v1

v2 whole, which is shorter than its diff:
```python
import functools

import jax
import jax.numpy as jnp
from jax import lax
from jax.experimental import pallas as pl
from jax.experimental.pallas import tpu as pltpu
from jax.sharding import Mesh, PartitionSpec as P

BLK = 128
LANES = 128
AXES = ("zl", "y", "c", "x", "zh")
GRP = ("zl", "y", "c")
TP = ("x", "zh")
F32 = jnp.float32
BF16 = jnp.bfloat16
PARAMS = pltpu.CompilerParams(vmem_limit_bytes=40 * 1024 * 1024)
FULL = pltpu.CompilerParams(vmem_limit_bytes=60 * 1024 * 1024)


def source_block(zh, zl, n):
    return (zh + (n - 1, n - 2, 0, 1)[zl]) % n


def decoder_moves(sizes):
    nzl, ny, nc, nx, nzh = sizes
    senders = (nzl - 1, 2, 1, 0)
    at = lambda zl, y, c, x, zh: (((zl * ny + y) * nc + c) * nx + x) * nzh + zh
    return [
        (at(senders[zl], y, c, x, source_block(zh, zl, nzh)), at(zl, y, c, x, zh))
        for zl in range(nzl)
        for y in range(ny)
        for c in range(nc)
        for x in range(nx)
        for zh in range(nzh)
    ]


def ring(size, step):
    return [(i, (i + step) % size) for i in range(size)]


def dot(left, right, dims):
    return lax.dot_general(left, right, (dims, ((), ())), preferred_element_type=F32)


def fold_kernel(dec_ref, value_ref, out_ref, acc_ref):
    step = pl.program_id(0)

    @pl.when(step == 0)
    def _():
        acc_ref[...] = jnp.zeros_like(acc_ref)

    chunk = value_ref.shape[1]
    width = dec_ref.shape[2] - 2 * LANES
    gain = gain_row(dec_ref[step, :, width + LANES : width + 2 * LANES], chunk)
    dec = dec_ref[:, :, pl.ds(pl.multiple_of(step * chunk, LANES), chunk)]
    dec = (dec.reshape(-1, chunk).astype(F32) * gain).astype(BF16)
    acc_ref[...] += dot(dec, value_ref[...], ((1,), (1,)))

    @pl.when(step == pl.num_programs(0) - 1)
    def _():
        out_ref[...] = acc_ref[...].astype(BF16)


def gain_row(tile, chunk):
    tile = tile.astype(F32)
    return jnp.concatenate([tile[i : i + 1] for i in range(chunk // LANES)], axis=1)


def value_kernel(
    geometry,
    order_ref,
    x0,
    x1,
    x2,
    x3,
    out_proj,
    decoder,
    gains_ref,
    post_ref,
    patterns_ref,
    value_ref,
    direct_ref,
    x_buf,
    proj_buf,
    dec_buf,
    sems,
):
    targets, seq, heads, head = geometry
    width = heads * head
    chunk = x_buf.shape[1]
    sources = (x0, x1, x2, x3)
    copies = []
    for n, source in enumerate(sources):
        cols = pl.ds(pl.multiple_of(order_ref[n] * chunk, LANES), chunk)
        group = [
            pltpu.make_async_copy(source, x_buf.at[n], sems.at[0, n]),
            pltpu.make_async_copy(out_proj.at[:, cols], proj_buf.at[n], sems.at[1, n]),
            pltpu.make_async_copy(decoder.at[:, cols], dec_buf.at[n], sems.at[2, n]),
        ]
        for c in group:
            c.start()
        copies.append(group)
    total = None
    for n, group in enumerate(copies):
        for c in group:
            c.wait()
        gain = gain_row(gains_ref[order_ref[n]], chunk)
        proj = (proj_buf[n].astype(F32) * gain).astype(BF16)
        left = jnp.concatenate([proj, dec_buf[n]], axis=0)
        part = dot(left, x_buf[n], ((1,), (0,)))
        total = part if total is None else total + part
    head_grad = (total[0:width] * post_ref[...]).astype(BF16)
    for r in range(targets):
        cols = slice(r * seq, (r + 1) * seq)
        mixed = jnp.zeros((head, seq), F32)
        for h in range(heads):
            mixed += dot(head_grad[h * head : (h + 1) * head, cols], patterns_ref[h], ((1,), (0,)))
        value_ref[cols, :] = mixed.T.astype(BF16)
    direct_ref[...] = total[width:].T


def score_kernel(
    geometry,
    names_ref,
    value_ref,
    direct_ref,
    pre_ref,
    ids_ref,
    m0,
    m1,
    m2,
    m3,
    out_ref,
):
    targets, seq, nx, owners = geometry
    value = value_ref[...]
    head = value.shape[1]
    ids = ids_ref[...]
    slots = ids.shape[1]
    totals = [jnp.zeros((targets * seq, BLK), F32) for _ in range(slots)]
    for n, folded_ref in enumerate((m0, m1, m2, m3)):
        for x in range(nx):
            rows = folded_ref[:, x].reshape(BLK, head)
            scores = dot(value, rows, ((1,), (1,)))
            name = names_ref[n * nx + x]
            for k in range(slots):
                totals[k] += jnp.where(ids[:, k : k + 1] == name, scores, 0.0)
    own = names_ref[4 * nx]
    direct = direct_ref[...]
    for k in range(slots):
        totals[k] = totals[k] * pre_ref[...] + jnp.where(ids[:, k : k + 1] == own, direct, 0.0)
    piece = seq // owners
    for i in range(owners):
        for r in range(targets):
            lo = r * seq + i * piece
            both = jnp.concatenate([t[lo : lo + piece] for t in totals], axis=0)
            out_ref[i, :, r * BLK : (r + 1) * BLK] = both.astype(BF16)


def last_kernel(targets, parts_ref, acts_ref, out_ref):
    total = jnp.sum(parts_ref[...].astype(F32), axis=0)
    tokens = acts_ref.shape[0]
    slots = acts_ref.shape[1] // BLK
    for r in range(targets):
        for k in range(slots):
            cols = slice(k * BLK, (k + 1) * BLK)
            out_ref[r, :, cols] = (
                total[k * tokens : (k + 1) * tokens, r * BLK : (r + 1) * BLK] * acts_ref[:, cols]
            )


def shards(
    sizes,
    grad_top,
    post_scale,
    post_gain,
    patterns,
    out_proj,
    value_proj,
    pre_scale,
    pre_gain,
    decoder,
    block_ids,
    feature_acts,
):
    nzl, ny, nc, nx, nzh = sizes
    owners = nx * nzh
    targets, seq, local = grad_top.shape
    rows = targets * seq
    heads, head = patterns.shape[0], out_proj.shape[0] // patterns.shape[0]
    width = out_proj.shape[1]
    chunk = width // nx
    slots = block_ids.shape[1]
    copies = ny * nc
    share = BLK // copies
    tokens = feature_acts.shape[0]
    zl, zh, x = lax.axis_index("zl"), lax.axis_index("zh"), lax.axis_index("x")
    copy = lax.axis_index(("y", "c"))

    mine = lax.dynamic_slice_in_dim(decoder, copy * share, share, axis=0)
    near = lax.ppermute(mine, AXES, decoder_moves(sizes))

    turned = grad_top.transpose(2, 0, 1).reshape(local, rows)
    gains = jnp.pad(jnp.stack([post_gain, pre_gain]), ((0, 14), (0, rows - local)))
    columns = lax.all_gather(
        jnp.concatenate([turned, gains], axis=0), "zh", axis=0, tiled=False
    )
    tiles = columns[:, local : local + 2, :local].transpose(1, 0, 2).reshape(2, -1, LANES)
    tiles = jnp.pad(tiles, ((0, 0), (0, share - chunk // LANES), (0, 0)))
    near = lax.all_gather(
        jnp.concatenate([near, tiles[0], tiles[1]], axis=1), "x", axis=0, tiled=False
    )
    wide, near = lax.optimization_barrier((columns[:, :local].reshape(chunk, rows), near))
    turns = (0, 1, nx - 1, 2)
    wides = [wide if k == 0 else lax.ppermute(wide, "x", ring(nx, k)) for k in turns]
    order = jnp.stack([(x - k) % nx for k in turns]).astype(jnp.int32)

    folded = pl.pallas_call(
        fold_kernel,
        grid=(nx,),
        in_specs=[
            pl.BlockSpec((nx, share, width + 2 * LANES), lambda i: (0, 0, 0)),
            pl.BlockSpec((head, chunk), lambda i: (0, i)),
        ],
        out_specs=pl.BlockSpec((nx * share, head), lambda i: (0, 0)),
        out_shape=jax.ShapeDtypeStruct((nx * share, head), BF16),
        scratch_shapes=[pltpu.VMEM((nx * share, head), F32)],
        compiler_params=PARAMS,
    )(near, value_proj)
    folded = lax.all_gather(folded, ("y", "c"), axis=0, tiled=False)
    folded = folded.reshape(copies, nx, share, head)
    levels = (0, 1, nzl - 1, 2)
    foldeds = [folded if k == 0 else lax.ppermute(folded, "zl", ring(nzl, k)) for k in levels]
    shifts = jnp.array([nzh - 1, nzh - 2, 0, 1])
    names = [
        i * nzh + (zh + shifts[(zl - k) % nzl]) % nzh for k in levels for i in range(nx)
    ]
    names = jnp.stack(names + [x * nzh + zh]).astype(jnp.int32)
    post_row = jnp.tile(post_scale, targets)[None, :]
    pre_col = jnp.tile(pre_scale, targets)[:, None]
    ids = jnp.tile(block_ids, (targets, 1))

    smem = pl.BlockSpec(memory_space=pltpu.SMEM)
    vmem = pl.BlockSpec(memory_space=pltpu.VMEM)
    hbm = pl.BlockSpec(memory_space=pl.ANY)
    value, direct = pl.pallas_call(
        functools.partial(value_kernel, (targets, seq, heads, head)),
        in_specs=[smem] + [hbm] * 6 + [vmem] * 3,
        out_specs=[vmem, vmem],
        out_shape=[
            jax.ShapeDtypeStruct((rows, head), BF16),
            jax.ShapeDtypeStruct((rows, BLK), F32),
        ],
        scratch_shapes=[
            pltpu.VMEM((nx, chunk, rows), BF16),
            pltpu.VMEM((nx, heads * head, chunk), BF16),
            pltpu.VMEM((nx, BLK, chunk), BF16),
            pltpu.SemaphoreType.DMA((3, nx)),
        ],
        compiler_params=FULL,
    )(
        order,
        *wides,
        out_proj,
        decoder,
        near[:, :, width : width + LANES],
        post_row,
        patterns,
    )
    parts = pl.pallas_call(
        functools.partial(score_kernel, (targets, seq, nx, owners)),
        in_specs=[smem] + [vmem] * 8,
        out_specs=vmem,
        out_shape=jax.ShapeDtypeStruct((owners, slots * tokens, targets * BLK), BF16),
        compiler_params=PARAMS,
    )(names, value, direct, pre_col, ids, *foldeds)

    parts = lax.all_to_all(parts, TP, 0, 0)
    return pl.pallas_call(
        functools.partial(last_kernel, targets),
        out_shape=jax.ShapeDtypeStruct((targets, tokens, slots * BLK), F32),
        compiler_params=PARAMS,
    )(parts, feature_acts.astype(F32))


def solution(mesh):
    sizes = (4, 4, mesh.devices.size // 256, 4, 4)
    mesh = Mesh(mesh.devices.reshape(sizes), AXES)
    in_specs = (
        P(GRP, None, TP),
        P(),
        P(TP),
        P(TP, None, None),
        P(TP, None),
        P(TP, None),
        P(),
        P(TP),
        P(TP, None),
        P(),
        P(TP, None),
    )
    return jax.shard_map(
        functools.partial(shards, sizes),
        mesh=mesh,
        in_specs=in_specs,
        out_specs=P(GRP, TP, None),
        check_vma=False,
    )
```

time: 197 us -> 159 us (0.81)
  waiting for transfers between devices: 66 us -> 27.6 us
  starting transfers between devices: 25.1 us -> 38.6 us
  between operations: 13.7 us -> 3.09 us
  Pallas kernels: 8.17 us -> 11.3 us
  blocking collectives: 70.9 us -> 68.1 us
  local copies, waits for them, and re-layouts: 10.1 us -> 7.6 us
    all_gather x2 -> x0, waiting for transfers between devices: 47.2 us -> none  [the longest x1 26.6 us: shards(): lax.all_gather(jnp.concatenate([near, both], axis=0), 'x', axis=0, tiled=...]
    ppermute x0 -> x6, starting transfers between devices: none -> 20 us  [the longest x3 10.4 us: shards(): lax.ppermute(wide, 'x', ring(nx, k))]
    ppermute x0 -> x6, waiting for transfers between devices: none -> 9.98 us  [the longest x3 9.98 us: shards(): lax.ppermute(wide, 'x', ring(nx, k))]
    all_to_all x1, starting transfers between devices: 13.7 us -> 7.27 us  [shards(): parts = lax.all_to_all(parts, TP, 0, 0)]
    pallas_call x2 -> x3, Pallas kernels: 7.52 us -> 10.6 us  [the longest x1 6.33 us: shards(): pl.pallas_call(functools.partial(value_kernel, (targets, seq, heads, head...]
    unnamed x30 -> x29, local copies, waits for them, and re-layouts: 6.5 us -> 3.66 us
    all_gather x1, blocking collectives: 16.2 us -> 13.5 us  [shards(): lax.all_gather(jnp.concatenate([near, tiles[0], tiles[1]], axis=1), 'x',...]
  transfers between devices with their start and end apart: 4 -> 8, of which waited for: 3 -> 2; matrix products, arithmetic and copies ran while one was open for 2% -> 3% of each run, Pallas kernels for 1% -> 5%
where the time goes in v2:
time: 159 us; the launch traced here: 157 us
  blocking collectives  68.1 us (43%)
  starting transfers between devices  38.6 us (24%)
  waiting for transfers between devices  27.6 us (17%)
  Pallas kernels  11.3 us (7%)
  local copies, waits for them, and re-layouts  7.6 us (5%)
  between operations  3.09 us (2%)
    all_gather x1, blocking collectives, shards(): lax.all_gather(jnp.concatenate([turned, gains], axis=0), 'zh', axis=0, ti...  41.9 us
    all_to_all x1, waiting for transfers between devices, shards(): parts = lax.all_to_all(parts, TP, 0, 0)  17.6 us
    all_gather x1, blocking collectives, shards(): lax.all_gather(jnp.concatenate([near, tiles[0], tiles[1]], axis=1), 'x',...  13.5 us
    all_gather x1, blocking collectives, shards(): folded = lax.all_gather(folded, ('y', 'c'), axis=0, tiled=False)  12.8 us
    ppermute x1, starting transfers between devices, shards(): near = lax.ppermute(mine, AXES, decoder_moves(sizes))  11.4 us
    ppermute x3, starting transfers between devices, shards(): lax.ppermute(wide, 'x', ring(nx, k))  10.4 us
    ppermute x3, waiting for transfers between devices, shards(): lax.ppermute(wide, 'x', ring(nx, k))  9.98 us
    ppermute x3, starting transfers between devices, shards(): lax.ppermute(folded, 'zl', ring(nzl, k))  9.54 us
  transfers between devices with their start and end apart: 8, of which 2 were waited for; matrix products, arithmetic and copies ran while one was open for 3% of the time, Pallas kernels for 5%

profile of v2, /device:TPU:24, one launch (start us, length us, event | category | flops | bytes accessed | tf_op | source)
XLA Modules:
  0.0 157.0 jit_solution(4734559644932203154)
XLA Ops:
  0.0 1.0 constant_dynamic-slice_fusion
  1.0 11.4 %collective-permute-start = (bf16[16,4608]{1,0:T(8,128)(2,1)S(1)}, bf16[16,4608]{1,0:T(8,128)(2,1)S(1)}, u32[]{:S(2)}, u32[]{:S(2)}) collective-permute-start(bf16[16,4608]{1,0:T(8,128)(2,1)S(1)} %constant_dynamic-slice_fusion), channel_id=1, source_target_pairs={{387,0},{384,1},{385,2},{386,3},{391,4},{388,5},{389,6},{390,7},{3... | collective-permute-start | bytes 442376 | tf_op jit(solution)/shard_map/ppermute | solution.py:203
  12.4 0.7 stack.102
  13.1 0.7 stack.101
  13.8 41.9 %all-gather = bf16[1216,384]{1,0:T(8,128)(2,1)S(1)} all-gather(bf16[304,384]{1,0:T(8,128)(2,1)S(1)} %pad_maximum_fusion), channel_id=2, replica_groups=mesh['zl'=4,'y'=4,'c'=2,'x'=4,'zh'=4] {'zh'}, dimensions={0}, use_global_device_ids=true | all-gather | bytes 1167360 | tf_op jit(solution)/shard_map/all_gather | solution.py:207
  56.0 13.5 %all-gather.1 = bf16[64,4864]{1,0:T(8,128)(2,1)S(1)} all-gather(bf16[16,4864]{1,0:T(8,128)(2,1)S(1)} %pad_maximum_fusion.1), channel_id=3, replica_groups=mesh['zl'=4,'y'=4,'c'=2,'x'=4,'zh'=4] {'x'}, dimensions={0}, use_global_device_ids=true | all-gather | bytes 778240 | tf_op jit(solution)/shard_map/all_gather | solution.py:212
  69.5 3.9 %collective-permute-start.1 = (bf16[1152,384]{1,0:T(8,128)(2,1)S(1)}, bf16[1152,384]{1,0:T(8,128)(2,1)S(1)}, u32[]{:S(2)}, u32[]{:S(2)}) collective-permute-start(bf16[1152,384]{1,0:T(8,128)(2,1)S(1)} %bitcast.66), channel_id=1, source_target_pairs={{0,4},{4,8},{8,12},{12,0},{1,5},{5,9},{9,13},{13,1},{2,6},{6,10},{... | collective-permute-start | bytes 2654216 | tf_op jit(solution)/shard_map/ppermute | solution.py:217
  73.4 3.3 %collective-permute-start.2 = (bf16[1152,384]{1,0:T(8,128)(2,1)S(1)}, bf16[1152,384]{1,0:T(8,128)(2,1)}, u32[]{:S(2)}, u32[]{:S(2)}) collective-permute-start(bf16[1152,384]{1,0:T(8,128)(2,1)S(1)} %bitcast.67), channel_id=1, source_target_pairs={{0,12},{4,0},{8,4},{12,8},{1,13},{5,1},{9,5},{13,9},{2,14},{6,2},{... | collective-permute-start | bytes 2654216 | tf_op jit(solution)/shard_map/ppermute | solution.py:217
  76.7 3.2 %collective-permute-start.3 = (bf16[1152,384]{1,0:T(8,128)(2,1)S(1)}, bf16[1152,384]{1,0:T(8,128)(2,1)}, u32[]{:S(2)}, u32[]{:S(2)}) collective-permute-start(bf16[1152,384]{1,0:T(8,128)(2,1)S(1)} %bitcast.68), channel_id=1, source_target_pairs={{0,8},{4,12},{8,0},{12,4},{1,9},{5,13},{9,1},{13,5},{2,10},{6,14},... | collective-permute-start | bytes 2654216 | tf_op jit(solution)/shard_map/ppermute | solution.py:217
  80.0 1.1 shard_map.119
  81.1 12.8 %all-gather.2 = bf16[512,128]{1,0:T(8,128)(2,1)S(1)} all-gather(bf16[64,128]{1,0:T(8,128)(2,1)S(1)} %shard_map.119), channel_id=4, replica_groups=mesh['zl'=4,'y'=4,'c'=2,'x'=4,'zh'=4] {'y','c'}, dimensions={0}, use_global_device_ids=true | all-gather | bytes 147456 | tf_op jit(solution)/shard_map/all_gather | solution.py:232
  93.8 1.9 %collective-permute-start.4 = (bf16[8,4,16,128]{3,2,1,0:T(8,128)(2,1)S(1)}, bf16[8,4,16,128]{3,2,1,0:T(8,128)(2,1)S(1)}, u32[]{:S(2)}, u32[]{:S(2)}) collective-permute-start(bf16[8,4,16,128]{3,2,1,0:T(8,128)(2,1)S(1)} %bitcast.60), channel_id=1, source_target_pairs={{0,128},{128,256},{256,384},{384,0},{1,129},{129,257},{257,385},{3... | collective-permute-start | bytes 393224 | tf_op jit(solution)/shard_map/ppermute | solution.py:235
  95.8 5.7 %collective-permute-start.5 = (bf16[8,4,16,128]{3,2,1,0:T(8,128)(2,1)S(1)}, bf16[8,4,16,128]{3,2,1,0:T(8,128)(2,1)S(1)}, u32[]{:S(2)}, u32[]{:S(2)}) collective-permute-start(bf16[8,4,16,128]{3,2,1,0:T(8,128)(2,1)S(1)} %bitcast.61), channel_id=1, source_target_pairs={{0,384},{128,0},{256,128},{384,256},{1,385},{129,1},{257,129},{385... | collective-permute-start | bytes 393224 | tf_op jit(solution)/shard_map/ppermute | solution.py:235
  101.5 10.0 %collective-permute-done.1.x1 = bf16[1152,384]{1,0:T(8,128)(2,1)S(1)} collective-permute-done((bf16[1152,384]{1,0:T(8,128)(2,1)S(1)}, bf16[1152,384]{1,0:T(8,128)(2,1)S(1)}, u32[]{:S(2)}, u32[]{:S(2)}) %collective-permute-start.1) | collective-permute-done | bytes 884768 | tf_op jit(solution)/shard_map/ppermute | solution.py:217
  111.5 1.0 copy-done.5
  112.4 1.9 %collective-permute-start.6 = (bf16[8,4,16,128]{3,2,1,0:T(8,128)(2,1)S(1)}, bf16[8,4,16,128]{3,2,1,0:T(8,128)(2,1)S(1)}, u32[]{:S(2)}, u32[]{:S(2)}) collective-permute-start(bf16[8,4,16,128]{3,2,1,0:T(8,128)(2,1)S(1)} %bitcast.62), channel_id=1, source_target_pairs={{0,256},{128,384},{256,0},{384,128},{1,257},{129,385},{257,1},{385... | collective-permute-start | bytes 393224 | tf_op jit(solution)/shard_map/ppermute | solution.py:235
  114.4 0.7 fusion.8
  120.0 6.3 %shard_map.118 = (bf16[384,128]{1,0:T(8,128)(2,1)}, f32[384,128]{1,0:T(8,128)}) custom-call(s32[4]{0:T(128)} %pad_add_fusion.order_ref, bf16[1152,384]{1,0:T(8,128)(2,1)} %bitcast.69, bf16[1152,384]{1,0:T(8,128)(2,1)} %copy-done.5, bf16[1152,384]{1,0:T(8,128)(2,1)} %collective-permute-done.2.x2, bf16[1152,384]{1,0:T(8,128)(2,1)} %collective-permute-done.3.x3, ...), custom_call_target="tpu_custom_call" | custom-call | tf_op jit(solution)/shard_map/pallas_call | solution.py:248
  126.4 0.9 copy-done.2
  127.4 0.9 copy-done.3
  128.2 3.2 %shard_map.120 = bf16[16,16,384]{2,1,0:T(8,128)(2,1)} custom-call(s32[17]{0:T(128)S(1)} %stack.95.names_ref, bf16[384,128]{1,0:T(8,128)(2,1)S(1)} %copy-done.3, f32[384,128]{1,0:T(8,128)S(1)} %copy-done.2, f32[384,1]{1,0:T(8,128)S(1)} %bitcast.58, s32[384,2]{1,0:T(8,128)S(1)} %bitcast.59, bf16[8,4,16,128]{3,2,1,0:T(8,128)(2,1)S(1)} %bitcast.63, ...), custom_call_target="tpu_custom_call" | custom-call | tf_op jit(solution)/shard_map/pallas_call | solution.py:272
  131.5 7.3 %all-to-all-start = ((bf16[16,16,384]{2,1,0:T(8,128)(2,1)}), bf16[16,16,384]{2,1,0:T(8,128)(2,1)S(1)}, u32[]{:S(2)}, u32[]{:S(2)}) async-start(bf16[16,16,384]{2,1,0:T(8,128)(2,1)} %shard_map.120), calls=%async_computation | async-start | bytes 393216 | tf_op jit(solution)/shard_map/all_to_all | solution.py:280
  138.8 17.6 %all-to-all-done.parts_ref = bf16[16,16,384]{2,1,0:T(8,128)(2,1)S(1)} async-done(((bf16[16,16,384]{2,1,0:T(8,128)(2,1)}), bf16[16,16,384]{2,1,0:T(8,128)(2,1)S(1)}, u32[]{:S(2)}, u32[]{:S(2)}) %all-to-all-start) | async-done | bytes 196640 | tf_op jit(solution)/shard_map/all_to_all | solution.py:280
  156.4 0.6 shard_map.121
  (45 shorter events, 2.5 us)
Async XLA Ops:
  0.0 13.7 %copy-start = (bf16[3,128,288]{1,2,0:T(8,128)(2,1)S(1)}, bf16[3,128,288]{1,2,0:T(8,128)(2,1)}, u32[]{:S(2)}) copy-start(bf16[3,128,288]{1,2,0:T(8,128)(2,1)} %param.12) | copy-start | bytes 663556
  1.0 55.0 %collective-permute-start = (bf16[16,4608]{1,0:T(8,128)(2,1)S(1)}, bf16[16,4608]{1,0:T(8,128)(2,1)S(1)}, u32[]{:S(2)}, u32[]{:S(2)}) collective-permute-start(bf16[16,4608]{1,0:T(8,128)(2,1)S(1)} %constant_dynamic-slice_fusion), channel_id=1, source_target_pairs={{387,0},{384,1},{385,2},{386,3},{391,4},{388,5},{389,6},{390,7},{3... | collective-permute-start | bytes 442376 | tf_op jit(solution)/shard_map/ppermute | solution.py:203
  55.8 24.2 %copy-start.9 = (f32[128]{0:T(128)S(1)}, f32[128]{0:T(128)}, u32[]{:S(2)}) copy-start(f32[128]{0:T(128)} %param.13) | copy-start | bytes 1540
  55.8 24.2 %copy-start.1 = (bf16[128,4608]{1,0:T(8,128)(2,1)S(1)}, bf16[128,4608]{1,0:T(8,128)(2,1)}, u32[]{:S(2)}) copy-start(bf16[128,4608]{1,0:T(8,128)(2,1)} %value_ref.1) | copy-start | bytes 3538948
  55.9 25.2 %copy-start.4 = (bf16[4,288,384]{2,1,0:T(8,128)(2,1)}, bf16[4,288,384]{2,1,0:T(8,128)(2,1)S(1)}, u32[]{:S(2)}) copy-start(bf16[4,288,384]{2,1,0:T(8,128)(2,1)S(1)} %slice.20) | copy-start | bytes 2654212
  69.5 44.9 %copy-start.10 = (f32[128]{0:T(128)S(1)}, f32[128]{0:T(128)}, u32[]{:S(2)}) copy-start(f32[128]{0:T(128)} %param.18) | copy-start | bytes 1540
  69.5 44.9 %copy-start.6 = (s32[4]{0:T(128)S(1)}, s32[4]{0:T(128)}, u32[]{:S(2)}) copy-start(s32[4]{0:T(128)} %constant.152.clone) | copy-start | bytes 52
  69.5 42.0 %collective-permute-start.1 = (bf16[1152,384]{1,0:T(8,128)(2,1)S(1)}, bf16[1152,384]{1,0:T(8,128)(2,1)S(1)}, u32[]{:S(2)}, u32[]{:S(2)}) collective-permute-start(bf16[1152,384]{1,0:T(8,128)(2,1)S(1)} %bitcast.66), channel_id=1, source_target_pairs={{0,4},{4,8},{8,12},{12,0},{1,5},{5,9},{9,13},{13,1},{2,6},{6,10},{... | collective-permute-start | bytes 2654216 | tf_op jit(solution)/shard_map/ppermute | solution.py:217
  73.4 46.6 %collective-permute-start.2 = (bf16[1152,384]{1,0:T(8,128)(2,1)S(1)}, bf16[1152,384]{1,0:T(8,128)(2,1)}, u32[]{:S(2)}, u32[]{:S(2)}) collective-permute-start(bf16[1152,384]{1,0:T(8,128)(2,1)S(1)} %bitcast.67), channel_id=1, source_target_pairs={{0,12},{4,0},{8,4},{12,8},{1,13},{5,1},{9,5},{13,9},{2,14},{6,2},{... | collective-permute-start | bytes 2654216 | tf_op jit(solution)/shard_map/ppermute | solution.py:217
  76.7 43.3 %collective-permute-start.3 = (bf16[1152,384]{1,0:T(8,128)(2,1)S(1)}, bf16[1152,384]{1,0:T(8,128)(2,1)}, u32[]{:S(2)}, u32[]{:S(2)}) collective-permute-start(bf16[1152,384]{1,0:T(8,128)(2,1)S(1)} %bitcast.68), channel_id=1, source_target_pairs={{0,8},{4,12},{8,0},{12,4},{1,9},{5,13},{9,1},{13,5},{2,10},{6,14},... | collective-permute-start | bytes 2654216 | tf_op jit(solution)/shard_map/ppermute | solution.py:217
  80.0 38.6 %copy-start.8 = (s32[128,2]{0,1:T(2,128)S(1)}, s32[128,2]{0,1:T(2,128)}, u32[]{:S(2)}) copy-start(s32[128,2]{0,1:T(2,128)} %param.21) | copy-start | bytes 3076
  93.8 32.5 %collective-permute-start.4 = (bf16[8,4,16,128]{3,2,1,0:T(8,128)(2,1)S(1)}, bf16[8,4,16,128]{3,2,1,0:T(8,128)(2,1)S(1)}, u32[]{:S(2)}, u32[]{:S(2)}) collective-permute-start(bf16[8,4,16,128]{3,2,1,0:T(8,128)(2,1)S(1)} %bitcast.60), channel_id=1, source_target_pairs={{0,128},{128,256},{256,384},{384,0},{1,129},{129,257},{257,385},{3... | collective-permute-start | bytes 393224 | tf_op jit(solution)/shard_map/ppermute | solution.py:235
  95.8 30.6 %collective-permute-start.5 = (bf16[8,4,16,128]{3,2,1,0:T(8,128)(2,1)S(1)}, bf16[8,4,16,128]{3,2,1,0:T(8,128)(2,1)S(1)}, u32[]{:S(2)}, u32[]{:S(2)}) collective-permute-start(bf16[8,4,16,128]{3,2,1,0:T(8,128)(2,1)S(1)} %bitcast.61), channel_id=1, source_target_pairs={{0,384},{128,0},{256,128},{384,256},{1,385},{129,1},{257,129},{385... | collective-permute-start | bytes 393224 | tf_op jit(solution)/shard_map/ppermute | solution.py:235
  111.5 1.0 copy-start.5
  112.4 14.0 %collective-permute-start.6 = (bf16[8,4,16,128]{3,2,1,0:T(8,128)(2,1)S(1)}, bf16[8,4,16,128]{3,2,1,0:T(8,128)(2,1)S(1)}, u32[]{:S(2)}, u32[]{:S(2)}) collective-permute-start(bf16[8,4,16,128]{3,2,1,0:T(8,128)(2,1)S(1)} %bitcast.62), channel_id=1, source_target_pairs={{0,256},{128,384},{256,0},{384,128},{1,257},{129,385},{257,1},{385... | collective-permute-start | bytes 393224 | tf_op jit(solution)/shard_map/ppermute | solution.py:235
  126.4 12.4 %copy-start.7 = (bf16[8,256]{1,0:T(8,128)(2,1)S(1)}, bf16[8,256]{1,0:T(8,128)(2,1)}, u32[]{:S(2)}) copy-start(bf16[8,256]{1,0:T(8,128)(2,1)} %param.22) | copy-start | bytes 12292
  126.4 0.9 copy-start.2
  127.4 0.9 copy-start.3
  131.5 24.9 %all-to-all-start = ((bf16[16,16,384]{2,1,0:T(8,128)(2,1)}), bf16[16,16,384]{2,1,0:T(8,128)(2,1)S(1)}, u32[]{:S(2)}, u32[]{:S(2)}) async-start(bf16[16,16,384]{2,1,0:T(8,128)(2,1)} %shard_map.120), calls=%async_computation | async-start | bytes 393216 | tf_op jit(solution)/shard_map/all_to_all | solution.py:280

commit v3 on v2

v3 whole, which is shorter than its diff:
```python
import functools

import jax
import jax.numpy as jnp
from jax import lax
from jax.experimental import pallas as pl
from jax.experimental.pallas import tpu as pltpu
from jax.sharding import Mesh, PartitionSpec as P

BLK = 128
LANES = 128
AXES = ("zl", "y", "c", "x", "zh")
GRP = ("zl", "y", "c")
TP = ("x", "zh")
TURNS = (0, 2, 1, 3)
F32 = jnp.float32
BF16 = jnp.bfloat16
PARAMS = pltpu.CompilerParams(vmem_limit_bytes=40 * 1024 * 1024)


def source_block(zh, zl, n):
    return (zh + (n - 1, n - 2, 0, 1)[zl]) % n


def decoder_moves(sizes):
    nzl, ny, nc, nx, nzh = sizes
    senders = (nzl - 1, 2, 1, 0)
    at = lambda zl, y, c, x, zh: (((zl * ny + y) * nc + c) * nx + x) * nzh + zh
    return [
        (at(senders[zl], y, c, x, source_block(zh, zl, nzh)), at(zl, y, c, x, zh))
        for zl in range(nzl)
        for y in range(ny)
        for c in range(nc)
        for x in range(nx)
        for zh in range(nzh)
    ]


def ring(size, step):
    return [(i, (i + step) % size) for i in range(size)]


def dot(left, right, dims):
    return lax.dot_general(left, right, (dims, ((), ())), preferred_element_type=F32)


def pack_kernel(top_ref, post_ref, pre_ref, out_ref):
    targets, local, seq = top_ref.shape
    wide = targets * seq
    for r in range(targets):
        out_ref[0:local, r * seq : (r + 1) * seq] = top_ref[r]
    zh = lax.axis_index("zh")
    lane = lax.broadcasted_iota(jnp.int32, (8, wide), 1)
    line = lax.broadcasted_iota(jnp.int32, (8, wide), 0)
    both = []
    for ref in (post_ref, pre_ref):
        flat = jnp.concatenate([ref[...].astype(F32), jnp.zeros((1, wide - local), F32)], axis=1)
        full = jnp.broadcast_to(flat, (8, wide))
        moved = full
        for z in range(1, 4):
            moved = jnp.where(zh == z, pltpu.roll(full, (z * local) % wide, 1), moved)
        place = line * wide + lane - zh * local
        both.append(jnp.where((place >= 0) & (place < local), moved, 0.0))
    out_ref[local:, :] = jnp.concatenate(both, axis=0).astype(BF16)


def join_kernel(columns_ref, wide_ref, gain_ref):
    zone, tall, rows = columns_ref.shape
    local = tall - 16
    total = None
    for z in range(zone):
        wide_ref[z * local : (z + 1) * local] = columns_ref[z, 0:local]
        tail = columns_ref[z, local:].astype(F32)
        total = tail if total is None else total + tail
    gain_ref[...] = total.astype(BF16)


def gain_row(tile, first, count):
    tile = tile.astype(F32)
    return jnp.concatenate([tile[first + i : first + i + 1] for i in range(count)], axis=1)


def fold_kernel(dec_ref, gains_ref, value_ref, out_ref, acc_ref):
    step = pl.program_id(0)

    @pl.when(step == 0)
    def _():
        acc_ref[...] = jnp.zeros_like(acc_ref)

    chunk = value_ref.shape[1]
    gain = gain_row(gains_ref[0], 8, chunk // gains_ref.shape[2])
    dec = (dec_ref[...].reshape(-1, chunk).astype(F32) * gain).astype(BF16)
    acc_ref[...] += dot(dec, value_ref[...], ((1,), (1,)))

    @pl.when(step == pl.num_programs(0) - 1)
    def _():
        out_ref[...] = acc_ref[...].astype(BF16)


def value_kernel(
    geometry,
    own,
    left,
    right,
    low,
    high,
    out_proj,
    decoder,
    near,
    post_ref,
    patterns_ref,
    value_ref,
    direct_ref,
    gains_ref,
    proj_buf,
    dec_buf,
    sem,
    sems,
):
    targets, seq, heads, head = geometry
    width = heads * head
    chunk = proj_buf.shape[2]
    size = 4
    mine = lax.axis_index("x")
    places = [lax.rem(mine + size - turn, size) for turn in (0, 1, 3, 2)]
    tail = pl.ds(decoder.shape[1], gains_ref.shape[2])
    fetch = pltpu.make_async_copy(near.at[:, pl.ds(0, 16), tail], gains_ref, sem)
    fetch.start()
    copies = []
    for n, place in enumerate(places):
        cols = pl.ds(pl.multiple_of(place * chunk, LANES), chunk)
        group = [
            pltpu.make_async_copy(out_proj.at[:, cols], proj_buf.at[n], sems.at[0, n]),
            pltpu.make_async_copy(decoder.at[:, cols], dec_buf.at[n], sems.at[1, n]),
        ]
        for c in group:
            c.start()
        copies.append(group)
    fetch.wait()
    total = None
    for n, sources in enumerate(((own,), (left,), (right,), (low, high))):
        for c in copies[n]:
            c.wait()
        gain = gain_row(gains_ref[places[n]], 0, chunk // gains_ref.shape[2])
        proj = proj_buf[n] * gain.astype(BF16)
        weights = jnp.concatenate([proj, dec_buf[n]], axis=0)
        first = 0
        for source in sources:
            last = first + source.shape[0]
            part = dot(weights[:, first:last], source[...], ((1,), (0,)))
            total = part if total is None else total + part
            first = last
    post = jnp.concatenate([post_ref[...]] * targets, axis=1)
    head_grad = (total[0:width] * post).astype(BF16)
    for r in range(targets):
        cols = slice(r * seq, (r + 1) * seq)
        mixed = jnp.zeros((head, seq), F32)
        for h in range(heads):
            mixed += dot(head_grad[h * head : (h + 1) * head, cols], patterns_ref[h], ((1,), (0,)))
        value_ref[cols, :] = mixed.T.astype(BF16)
    direct_ref[...] = total[width:].T


def score_kernel(geometry, value_ref, direct_ref, pre_ref, ids_ref, m0, m1, m2, m3, out_ref):
    targets, seq, nx, nzh, owners = geometry
    zh, zl = lax.axis_index("zh"), lax.axis_index("zl")
    value = value_ref[...]
    head = value.shape[1]
    slots = ids_ref.shape[0]
    lines = [ids_ref[...].astype(F32), pre_ref[...], jnp.zeros((7 - slots, seq), F32)]
    columns = jnp.concatenate(lines, axis=0).T
    ids = [columns[:, k : k + 1] for k in range(slots)]
    pre = columns[:, slots : slots + 1]
    totals = [[jnp.zeros((seq, BLK), F32) for _ in range(targets)] for _ in range(slots)]
    for turn, folded_ref in zip(TURNS, (m0, m1, m2, m3)):
        other = lax.rem(zl + 4 - turn, 4)
        shift = jnp.where(
            other == 0, nzh - 1, jnp.where(other == 1, nzh - 2, jnp.where(other == 2, 0, 1))
        )
        block = lax.rem(zh + shift, nzh)
        for x in range(nx):
            rows = folded_ref[:, x].reshape(BLK, head)
            scores = dot(value, rows, ((1,), (1,)))
            name = (x * nzh + block).astype(F32)
            for k in range(slots):
                hit = ids[k] == name
                for r in range(targets):
                    totals[k][r] += jnp.where(hit, scores[r * seq : (r + 1) * seq], 0.0)
    own = (lax.axis_index("x") * nzh + zh).astype(F32)
    direct = direct_ref[...]
    for k in range(slots):
        hit = ids[k] == own
        for r in range(targets):
            picked = jnp.where(hit, direct[r * seq : (r + 1) * seq], 0.0)
            totals[k][r] = totals[k][r] * pre + picked
    piece = seq // owners
    for i in range(owners):
        for r in range(targets):
            both = [totals[k][r][i * piece : (i + 1) * piece] for k in range(slots)]
            out_ref[i, :, r * BLK : (r + 1) * BLK] = jnp.concatenate(both, axis=0).astype(BF16)


def last_kernel(targets, parts_ref, acts_ref, out_ref):
    total = jnp.sum(parts_ref[...].astype(F32), axis=0)
    acts = acts_ref[...].astype(F32)
    tokens = acts.shape[0]
    slots = acts.shape[1] // BLK
    for r in range(targets):
        for k in range(slots):
            cols = slice(k * BLK, (k + 1) * BLK)
            out_ref[r, :, cols] = (
                total[k * tokens : (k + 1) * tokens, r * BLK : (r + 1) * BLK] * acts[:, cols]
            )


def shards(
    sizes,
    grad_top,
    post_scale,
    post_gain,
    patterns,
    out_proj,
    value_proj,
    pre_scale,
    pre_gain,
    decoder,
    block_ids,
    feature_acts,
):
    nzl, ny, nc, nx, nzh = sizes
    owners = nx * nzh
    targets, seq, local = grad_top.shape
    rows = targets * seq
    heads, head = patterns.shape[0], out_proj.shape[0] // patterns.shape[0]
    width = out_proj.shape[1]
    chunk = width // nx
    slots = block_ids.shape[1]
    copies = ny * nc
    share = BLK // copies
    tokens = feature_acts.shape[0]
    vmem = pl.BlockSpec(memory_space=pltpu.VMEM)
    hbm = pl.BlockSpec(memory_space=pl.ANY)

    cut = chunk // 2 // LANES * LANES + LANES

    copy = lax.axis_index(("y", "c"))
    near = lax.dynamic_slice_in_dim(decoder, copy * share, share, axis=0)
    near = lax.ppermute(near, AXES, decoder_moves(sizes))
    packed = pl.pallas_call(
        pack_kernel,
        out_shape=jax.ShapeDtypeStruct((local + 16, rows), BF16),
        compiler_params=PARAMS,
    )(grad_top.transpose(0, 2, 1), post_gain[None, :], pre_gain[None, :])
    columns = lax.all_gather(packed, "zh", axis=0, tiled=False)
    wide, gains = pl.pallas_call(
        join_kernel,
        out_shape=[
            jax.ShapeDtypeStruct((chunk, rows), BF16),
            jax.ShapeDtypeStruct((16, rows), BF16),
        ],
        compiler_params=PARAMS,
    )(columns)
    gains = jnp.pad(gains, ((0, share - 16), (0, 0)))
    near = lax.all_gather(jnp.concatenate([near, gains], axis=1), "x", axis=0, tiled=False)
    wide, near = lax.optimization_barrier((wide, near))
    left = lax.ppermute(wide, "x", ring(nx, 1))
    right = lax.ppermute(wide, "x", ring(nx, nx - 1))
    folded = pl.pallas_call(
        fold_kernel,
        grid=(nx,),
        in_specs=[
            pl.BlockSpec((nx, share, chunk), lambda i: (0, 0, i)),
            pl.BlockSpec((1, 16, rows), lambda i: (i, 0, width // rows)),
            pl.BlockSpec((head, chunk), lambda i: (0, i)),
        ],
        out_specs=pl.BlockSpec((nx * share, head), lambda i: (0, 0)),
        out_shape=jax.ShapeDtypeStruct((nx * share, head), BF16),
        scratch_shapes=[pltpu.VMEM((nx * share, head), F32)],
        compiler_params=PARAMS,
    )(near, near, value_proj)
    folded = lax.all_gather(folded, ("y", "c"), axis=0, tiled=False)
    left, right, folded = lax.optimization_barrier((left, right, folded))
    low = lax.ppermute(left[:cut], "x", ring(nx, 1))
    high = lax.ppermute(right[cut:], "x", ring(nx, nx - 1))
    folded = folded.reshape(copies, nx, share, head)
    foldeds = [folded if k == 0 else lax.ppermute(folded, "zl", ring(nzl, k)) for k in TURNS]

    value, direct = pl.pallas_call(
        functools.partial(value_kernel, (targets, seq, heads, head)),
        in_specs=[vmem] * 5 + [hbm] * 3 + [vmem] * 2,
        out_specs=[vmem, vmem],
        out_shape=[
            jax.ShapeDtypeStruct((rows, head), BF16),
            jax.ShapeDtypeStruct((rows, BLK), F32),
        ],
        scratch_shapes=[
            pltpu.VMEM((nx, 16, rows), BF16),
            pltpu.VMEM((nx, heads * head, chunk), BF16),
            pltpu.VMEM((nx, BLK, chunk), BF16),
            pltpu.SemaphoreType.DMA,
            pltpu.SemaphoreType.DMA((2, nx)),
        ],
        compiler_params=PARAMS,
    )(wide, left, right, low, high, out_proj, decoder, near, post_scale[None, :], patterns)
    parts = pl.pallas_call(
        functools.partial(score_kernel, (targets, seq, nx, nzh, owners)),
        out_shape=jax.ShapeDtypeStruct((owners, slots * tokens, targets * BLK), BF16),
        compiler_params=PARAMS,
    )(value, direct, pre_scale[None, :], block_ids.T, *foldeds)

    parts = lax.all_to_all(parts, TP, 0, 0)
    return pl.pallas_call(
        functools.partial(last_kernel, targets),
        out_shape=jax.ShapeDtypeStruct((targets, tokens, slots * BLK), F32),
        compiler_params=PARAMS,
    )(parts, feature_acts)


def solution(mesh):
    sizes = (4, 4, mesh.devices.size // 256, 4, 4)
    mesh = Mesh(mesh.devices.reshape(sizes), AXES)
    in_specs = (
        P(GRP, None, TP),
        P(),
        P(TP),
        P(TP, None, None),
        P(TP, None),
        P(TP, None),
        P(),
        P(TP),
        P(TP, None),
        P(),
        P(TP, None),
    )
    return jax.shard_map(
        functools.partial(shards, sizes),
        mesh=mesh,
        in_specs=in_specs,
        out_specs=P(GRP, TP, None),
        check_vma=False,
    )
```

time: 159 us -> 144 us (0.906)
  blocking collectives: 68.1 us -> 92.3 us
  waiting for transfers between devices: 27.6 us -> 4.35 us
  Pallas kernels: 11.3 us -> 6.41 us
  local copies, waits for them, and re-layouts: 7.6 us -> 3.36 us
  between operations: 3.09 us -> 0.26 us
  starting transfers between devices: 38.6 us -> 35.9 us
    all_to_all x0 -> x1, blocking collectives: none -> 25.6 us  [shards(): parts = lax.all_to_all(parts, TP, 0, 0)]
    all_to_all x1 -> x0, waiting for transfers between devices: 17.6 us -> none  [shards(): parts = lax.all_to_all(parts, TP, 0, 0)]
    all_to_all x1 -> x0, starting transfers between devices: 7.27 us -> none  [shards(): parts = lax.all_to_all(parts, TP, 0, 0)]
    ppermute x4 -> x5, waiting for transfers between devices: 9.98 us -> 2.82 us  [the longest x1 1.64 us: shards(): left = lax.ppermute(wide, 'x', ring(nx, 1))]
    ppermute x4 -> x5, starting transfers between devices: 21.8 us -> 26 us  [the longest x1 11.4 us: shards(): near = lax.ppermute(near, AXES, decoder_moves(sizes))]
    pallas_call x1, Pallas kernels: 6.33 us -> 3.29 us  [shards(): pl.pallas_call(functools.partial(value_kernel, (targets, seq, heads, head...]
    unnamed x29 -> x18, local copies, waits for them, and re-layouts: 3.66 us -> 0.98 us
    pallas_call x1 -> x3, Pallas kernels: 3.22 us -> 1.2 us  [the longest x1 1.03 us: shards(): pl.pallas_call(functools.partial(score_kernel, (targets, seq, nx, nzh, ow...]
  transfers between devices with their start and end apart: 8 -> 8, of which waited for: 2 -> 3; matrix products, arithmetic and copies ran while one was open for 3% -> 1% of each run, Pallas kernels for 5% -> 3%
where the time goes in v3:
time: 144 us; the launch traced here: 143 us
  blocking collectives  92.3 us (64%)
  starting transfers between devices  35.9 us (25%)
  Pallas kernels  6.41 us (4%)
  waiting for transfers between devices  4.35 us (3%)
  local copies, waits for them, and re-layouts  3.36 us (2%)
    all_gather x1, blocking collectives, shards(): columns = lax.all_gather(packed, 'zh', axis=0, tiled=False)  40.3 us
    all_to_all x1, blocking collectives, shards(): parts = lax.all_to_all(parts, TP, 0, 0)  25.6 us
    all_gather x1, blocking collectives, shards(): lax.all_gather(jnp.concatenate([near, gains], axis=1), 'x', axis=0, tiled...  13.5 us
    all_gather x1, blocking collectives, shards(): folded = lax.all_gather(folded, ('y', 'c'), axis=0, tiled=False)  12.9 us
    ppermute x1, starting transfers between devices, shards(): near = lax.ppermute(near, AXES, decoder_moves(sizes))  11.4 us
    ppermute x3, starting transfers between devices, shards(): lax.ppermute(folded, 'zl', ring(nzl, k))  9.92 us
    ppermute x1, starting transfers between devices, shards(): high = lax.ppermute(right[cut:], 'x', ring(nx, nx - 1))  4.95 us
    ppermute x1, starting transfers between devices, shards(): left = lax.ppermute(wide, 'x', ring(nx, 1))  3.83 us
  transfers between devices with their start and end apart: 8, of which 3 were waited for; matrix products, arithmetic and copies ran while one was open for 1% of the time, Pallas kernels for 3%

profile of v3, /device:TPU:24, one launch (start us, length us, event | category | flops | bytes accessed | tf_op | source)
XLA Modules:
  0.0 142.5 jit_solution(15226476224885613308)
XLA Ops:
  0.0 0.9 constant_dynamic-slice_fusion
  0.9 11.4 %collective-permute-start = (bf16[16,4608]{1,0:T(8,128)(2,1)S(1)}, bf16[16,4608]{1,0:T(8,128)(2,1)S(1)}, u32[]{:S(2)}, u32[]{:S(2)}) collective-permute-start(bf16[16,4608]{1,0:T(8,128)(2,1)S(1)} %constant_dynamic-slice_fusion), channel_id=1, source_target_pairs={{387,0},{384,1},{385,2},{386,3},{391,4},{388,5},{389,6},{390,7},{3... | collective-permute-start | bytes 442376 | tf_op jit(solution)/shard_map/ppermute | solution.py:248
  12.3 0.7 broadcast_in_dim.12.post_ref
  13.0 0.7 broadcast_in_dim.13.pre_ref
  13.7 0.9 copy-done.3
  14.7 40.3 %all-gather = bf16[1216,384]{1,0:T(8,128)(2,1)S(1)} all-gather(bf16[304,384]{1,0:T(8,128)(2,1)S(1)} %shard_map.109), channel_id=2, replica_groups=mesh['zl'=4,'y'=4,'c'=2,'x'=4,'zh'=4] {'zh'}, dimensions={0}, use_global_device_ids=true | all-gather | bytes 1167360 | tf_op jit(solution)/shard_map/all_gather | solution.py:254
  55.0 0.1 shard_map.110
  55.1 13.5 %all-gather.1 = bf16[64,4992]{1,0:T(8,128)(2,1)S(1)} all-gather(bf16[16,4992]{1,0:T(8,128)(2,1)S(1)} %pad_maximum_fusion), channel_id=3, replica_groups=mesh['zl'=4,'y'=4,'c'=2,'x'=4,'zh'=4] {'x'}, dimensions={0}, use_global_device_ids=true | all-gather | bytes 798720 | tf_op jit(solution)/shard_map/all_gather | solution.py:264
  68.6 3.8 %collective-permute-start.1 = (bf16[1152,384]{1,0:T(8,128)(2,1)S(1)}, bf16[1152,384]{1,0:T(8,128)(2,1)S(1)}, u32[]{:S(2)}, u32[]{:S(2)}) collective-permute-start(bf16[1152,384]{1,0:T(8,128)(2,1)S(1)} %get-tuple-element.16.own), channel_id=1, source_target_pairs={{0,4},{4,8},{8,12},{12,0},{1,5},{5,9},{9,13},{13,1},{2,6},{6,10},{... | collective-permute-start | bytes 2654216 | tf_op jit(solution)/shard_map/ppermute | solution.py:266
  72.4 3.2 %collective-permute-start.2 = (bf16[1152,384]{1,0:T(8,128)(2,1)S(1)}, bf16[1152,384]{1,0:T(8,128)(2,1)S(1)}, u32[]{:S(2)}, u32[]{:S(2)}) collective-permute-start(bf16[1152,384]{1,0:T(8,128)(2,1)S(1)} %get-tuple-element.16.own), channel_id=1, source_target_pairs={{0,12},{4,0},{8,4},{12,8},{1,13},{5,1},{9,5},{13,9},{2,14},{6,2},{... | collective-permute-start | bytes 2654216 | tf_op jit(solution)/shard_map/ppermute | solution.py:267
  75.7 1.3 shard_map.111
  77.0 12.9 %all-gather.2 = bf16[512,128]{1,0:T(8,128)(2,1)S(1)} all-gather(bf16[64,128]{1,0:T(8,128)(2,1)S(1)} %shard_map.111), channel_id=4, replica_groups=mesh['zl'=4,'y'=4,'c'=2,'x'=4,'zh'=4] {'y','c'}, dimensions={0}, use_global_device_ids=true | all-gather | bytes 147456 | tf_op jit(solution)/shard_map/all_gather | solution.py:281
  89.9 1.6 %collective-permute-done.1.left = bf16[1152,384]{1,0:T(8,128)(2,1)S(1)} collective-permute-done((bf16[1152,384]{1,0:T(8,128)(2,1)S(1)}, bf16[1152,384]{1,0:T(8,128)(2,1)S(1)}, u32[]{:S(2)}, u32[]{:S(2)}) %collective-permute-start.1) | collective-permute-done | bytes 884768 | tf_op jit(solution)/shard_map/ppermute | solution.py:266
  91.5 1.2 collective-permute-done.2.right
  92.8 2.6 %collective-permute-start.3 = (bf16[640,384]{1,0:T(8,128)(2,1)S(1)}, bf16[640,384]{1,0:T(8,128)(2,1)S(1)}, u32[]{:S(2)}, u32[]{:S(2)}) collective-permute-start(bf16[640,384]{1,0:T(8,128)(2,1)S(1)} %slice.6), channel_id=1, source_target_pairs={{0,4},{4,8},{8,12},{12,0},{1,5},{5,9},{9,13},{13,1},{2,6},{6,10},{... | collective-permute-start | bytes 1474568 | tf_op jit(solution)/shard_map/ppermute | solution.py:283
  95.4 4.9 %collective-permute-start.4 = (bf16[512,384]{1,0:T(8,128)(2,1)S(1)}, bf16[512,384]{1,0:T(8,128)(2,1)S(1)}, u32[]{:S(2)}, u32[]{:S(2)}) collective-permute-start(bf16[512,384]{1,0:T(8,128)(2,1)S(1)} %slice.7), channel_id=1, source_target_pairs={{0,12},{4,0},{8,4},{12,8},{1,13},{5,1},{9,5},{13,9},{2,14},{6,2},{... | collective-permute-start | bytes 1179656 | tf_op jit(solution)/shard_map/ppermute | solution.py:284
  100.3 1.9 %collective-permute-start.5 = (bf16[8,4,16,128]{3,2,1,0:T(8,128)(2,1)S(1)}, bf16[8,4,16,128]{3,2,1,0:T(8,128)(2,1)S(1)}, u32[]{:S(2)}, u32[]{:S(2)}) collective-permute-start(bf16[8,4,16,128]{3,2,1,0:T(8,128)(2,1)S(1)} %bitcast.12), channel_id=1, source_target_pairs={{0,256},{128,384},{256,0},{384,128},{1,257},{129,385},{257,1},{385... | collective-permute-start | bytes 393224 | tf_op jit(solution)/shard_map/ppermute | solution.py:286
  102.3 6.1 %collective-permute-start.6 = (bf16[8,4,16,128]{3,2,1,0:T(8,128)(2,1)S(1)}, bf16[8,4,16,128]{3,2,1,0:T(8,128)(2,1)S(1)}, u32[]{:S(2)}, u32[]{:S(2)}) collective-permute-start(bf16[8,4,16,128]{3,2,1,0:T(8,128)(2,1)S(1)} %bitcast.13), channel_id=1, source_target_pairs={{0,128},{128,256},{256,384},{384,0},{1,129},{129,257},{257,385},{3... | collective-permute-start | bytes 393224 | tf_op jit(solution)/shard_map/ppermute | solution.py:286
  108.4 1.9 %collective-permute-start.7 = (bf16[8,4,16,128]{3,2,1,0:T(8,128)(2,1)S(1)}, bf16[8,4,16,128]{3,2,1,0:T(8,128)(2,1)S(1)}, u32[]{:S(2)}, u32[]{:S(2)}) collective-permute-start(bf16[8,4,16,128]{3,2,1,0:T(8,128)(2,1)S(1)} %bitcast.14), channel_id=1, source_target_pairs={{0,384},{128,0},{256,128},{384,256},{1,385},{129,1},{257,129},{385... | collective-permute-start | bytes 393224 | tf_op jit(solution)/shard_map/ppermute | solution.py:286
  110.4 3.3 %shard_map.112 = (bf16[384,128]{1,0:T(8,128)(2,1)S(1)}, f32[384,128]{1,0:T(8,128)S(1)}) custom-call(bf16[1152,384]{1,0:T(8,128)(2,1)S(1)} %get-tuple-element.16.own, bf16[1152,384]{1,0:T(8,128)(2,1)S(1)} %collective-permute-done.1.left, bf16[1152,384]{1,0:T(8,128)(2,1)S(1)} %collective-permute-done.2.right, bf16[640,384]{1,0:T(8,128)(2,1)S(1)} %collective-permute-done.3.low, ...), custom_call_target="tpu_custom_call" | custom-call | tf_op jit(solution)/shard_map/pallas_call | solution.py:288
  113.7 1.5 %collective-permute-done.7.m3 = bf16[8,4,16,128]{3,2,1,0:T(8,128)(2,1)S(1)} collective-permute-done((bf16[8,4,16,128]{3,2,1,0:T(8,128)(2,1)S(1)}, bf16[8,4,16,128]{3,2,1,0:T(8,128)(2,1)S(1)}, u32[]{:S(2)}, u32[]{:S(2)}) %collective-permute-start.7) | collective-permute-done | bytes 131104 | tf_op jit(solution)/shard_map/ppermute | solution.py:286
  115.2 1.0 shard_map.113
  116.3 25.6 %all_to_all.5.parts_ref = bf16[16,16,384]{2,1,0:T(8,128)(2,1)S(1)} all-to-all(bf16[16,16,384]{2,1,0:T(8,128)(2,1)S(1)} %shard_map.113), channel_id=1, replica_groups=mesh['zl'=4,'y'=4,'c'=2,'x'=4,'zh'=4] {'x','zh'}, dimensions={0} | all-to-all | bytes 393216 | tf_op jit(solution)/shard_map/all_to_all | solution.py:311
  141.9 0.6 shard_map.114
  (26 shorter events, 0.3 us)
Async XLA Ops:
  0.9 54.2 %collective-permute-start = (bf16[16,4608]{1,0:T(8,128)(2,1)S(1)}, bf16[16,4608]{1,0:T(8,128)(2,1)S(1)}, u32[]{:S(2)}, u32[]{:S(2)}) collective-permute-start(bf16[16,4608]{1,0:T(8,128)(2,1)S(1)} %constant_dynamic-slice_fusion), channel_id=1, source_target_pairs={{387,0},{384,1},{385,2},{386,3},{391,4},{388,5},{389,6},{390,7},{3... | collective-permute-start | bytes 442376 | tf_op jit(solution)/shard_map/ppermute | solution.py:248
  13.7 0.9 copy-start.3
  55.0 20.7 %copy-start.2 = (bf16[128,4608]{1,0:T(8,128)(2,1)S(1)}, bf16[128,4608]{1,0:T(8,128)(2,1)}, u32[]{:S(2)}) copy-start(bf16[128,4608]{1,0:T(8,128)(2,1)} %value_ref.1) | copy-start | bytes 3538948
  68.6 22.9 %collective-permute-start.1 = (bf16[1152,384]{1,0:T(8,128)(2,1)S(1)}, bf16[1152,384]{1,0:T(8,128)(2,1)S(1)}, u32[]{:S(2)}, u32[]{:S(2)}) collective-permute-start(bf16[1152,384]{1,0:T(8,128)(2,1)S(1)} %get-tuple-element.16.own), channel_id=1, source_target_pairs={{0,4},{4,8},{8,12},{12,0},{1,5},{5,9},{9,13},{13,1},{2,6},{6,10},{... | collective-permute-start | bytes 2654216 | tf_op jit(solution)/shard_map/ppermute | solution.py:266
  72.4 20.3 %collective-permute-start.2 = (bf16[1152,384]{1,0:T(8,128)(2,1)S(1)}, bf16[1152,384]{1,0:T(8,128)(2,1)S(1)}, u32[]{:S(2)}, u32[]{:S(2)}) collective-permute-start(bf16[1152,384]{1,0:T(8,128)(2,1)S(1)} %get-tuple-element.16.own), channel_id=1, source_target_pairs={{0,12},{4,0},{8,4},{12,8},{1,13},{5,1},{9,5},{13,9},{2,14},{6,2},{... | collective-permute-start | bytes 2654216 | tf_op jit(solution)/shard_map/ppermute | solution.py:267
  75.7 34.6 %copy-start = (bf16[256,4608]{1,0:T(8,128)(2,1)S(1)}, bf16[256,4608]{1,0:T(8,128)(2,1)}, u32[]{:S(2)}) copy-start(bf16[256,4608]{1,0:T(8,128)(2,1)} %out_proj.1) | copy-start | bytes 7077892
  77.0 33.3 %copy-start.1 = (bf16[128,4608]{1,0:T(8,128)(2,1)S(1)}, bf16[128,4608]{1,0:T(8,128)(2,1)}, u32[]{:S(2)}) copy-start(bf16[128,4608]{1,0:T(8,128)(2,1)} %decoder.1) | copy-start | bytes 3538948
  77.0 33.3 %copy-start.4 = (bf16[2,128,128]{2,1,0:T(8,128)(2,1)S(1)}, bf16[2,128,128]{2,1,0:T(8,128)(2,1)}, u32[]{:S(2)}) copy-start(bf16[2,128,128]{2,1,0:T(8,128)(2,1)} %patterns_ref.1) | copy-start | bytes 196612
  77.0 33.3 %copy-start.7 = (f32[128]{0:T(128)S(1)}, f32[128]{0:T(128)}, u32[]{:S(2)}) copy-start(f32[128]{0:T(128)} %param.12) | copy-start | bytes 1540
  92.8 17.5 %collective-permute-start.3 = (bf16[640,384]{1,0:T(8,128)(2,1)S(1)}, bf16[640,384]{1,0:T(8,128)(2,1)S(1)}, u32[]{:S(2)}, u32[]{:S(2)}) collective-permute-start(bf16[640,384]{1,0:T(8,128)(2,1)S(1)} %slice.6), channel_id=1, source_target_pairs={{0,4},{4,8},{8,12},{12,0},{1,5},{5,9},{9,13},{13,1},{2,6},{6,10},{... | collective-permute-start | bytes 1474568 | tf_op jit(solution)/shard_map/ppermute | solution.py:283
  95.4 14.9 %collective-permute-start.4 = (bf16[512,384]{1,0:T(8,128)(2,1)S(1)}, bf16[512,384]{1,0:T(8,128)(2,1)S(1)}, u32[]{:S(2)}, u32[]{:S(2)}) collective-permute-start(bf16[512,384]{1,0:T(8,128)(2,1)S(1)} %slice.7), channel_id=1, source_target_pairs={{0,12},{4,0},{8,4},{12,8},{1,13},{5,1},{9,5},{13,9},{2,14},{6,2},{... | collective-permute-start | bytes 1179656 | tf_op jit(solution)/shard_map/ppermute | solution.py:284
  100.3 13.3 %collective-permute-start.5 = (bf16[8,4,16,128]{3,2,1,0:T(8,128)(2,1)S(1)}, bf16[8,4,16,128]{3,2,1,0:T(8,128)(2,1)S(1)}, u32[]{:S(2)}, u32[]{:S(2)}) collective-permute-start(bf16[8,4,16,128]{3,2,1,0:T(8,128)(2,1)S(1)} %bitcast.12), channel_id=1, source_target_pairs={{0,256},{128,384},{256,0},{384,128},{1,257},{129,385},{257,1},{385... | collective-permute-start | bytes 393224 | tf_op jit(solution)/shard_map/ppermute | solution.py:286
  102.3 11.4 %collective-permute-start.6 = (bf16[8,4,16,128]{3,2,1,0:T(8,128)(2,1)S(1)}, bf16[8,4,16,128]{3,2,1,0:T(8,128)(2,1)S(1)}, u32[]{:S(2)}, u32[]{:S(2)}) collective-permute-start(bf16[8,4,16,128]{3,2,1,0:T(8,128)(2,1)S(1)} %bitcast.13), channel_id=1, source_target_pairs={{0,128},{128,256},{256,384},{384,0},{1,129},{129,257},{257,385},{3... | collective-permute-start | bytes 393224 | tf_op jit(solution)/shard_map/ppermute | solution.py:286
  108.4 6.9 %collective-permute-start.7 = (bf16[8,4,16,128]{3,2,1,0:T(8,128)(2,1)S(1)}, bf16[8,4,16,128]{3,2,1,0:T(8,128)(2,1)S(1)}, u32[]{:S(2)}, u32[]{:S(2)}) collective-permute-start(bf16[8,4,16,128]{3,2,1,0:T(8,128)(2,1)S(1)} %bitcast.14), channel_id=1, source_target_pairs={{0,384},{128,0},{256,128},{384,256},{1,385},{129,1},{257,129},{385... | collective-permute-start | bytes 393224 | tf_op jit(solution)/shard_map/ppermute | solution.py:286
  110.3 4.9 %copy-start.6 = (s32[128,2]{0,1:T(2,128)S(1)}, s32[128,2]{0,1:T(2,128)}, u32[]{:S(2)}) copy-start(s32[128,2]{0,1:T(2,128)} %param.20) | copy-start | bytes 3076
  110.4 4.9 %copy-start.8 = (f32[128]{0:T(128)S(1)}, f32[128]{0:T(128)}, u32[]{:S(2)}) copy-start(f32[128]{0:T(128)} %param.17) | copy-start | bytes 1540
  113.7 28.2 %copy-start.5 = (bf16[8,256]{1,0:T(8,128)(2,1)S(1)}, bf16[8,256]{1,0:T(8,128)(2,1)}, u32[]{:S(2)}) copy-start(bf16[8,256]{1,0:T(8,128)(2,1)} %acts_ref.1) | copy-start | bytes 12292

commit v4 on v3

--- a/solution.py
+++ b/solution.py
@@ -94,7 +94,7 @@
 
     @pl.when(step == pl.num_programs(0) - 1)
     def _():
-        out_ref[...] = acc_ref[...].astype(BF16)
+        out_ref[...] = jnp.broadcast_to(acc_ref[...].astype(BF16)[None], out_ref.shape)
 
 
 def value_kernel(
@@ -273,12 +273,12 @@
             pl.BlockSpec((1, 16, rows), lambda i: (i, 0, width // rows)),
             pl.BlockSpec((head, chunk), lambda i: (0, i)),
         ],
-        out_specs=pl.BlockSpec((nx * share, head), lambda i: (0, 0)),
-        out_shape=jax.ShapeDtypeStruct((nx * share, head), BF16),
+        out_specs=pl.BlockSpec((copies, nx * share, head), lambda i: (0, 0, 0)),
+        out_shape=jax.ShapeDtypeStruct((copies, nx * share, head), BF16),
         scratch_shapes=[pltpu.VMEM((nx * share, head), F32)],
         compiler_params=PARAMS,
     )(near, near, value_proj)
-    folded = lax.all_gather(folded, ("y", "c"), axis=0, tiled=False)
+    folded = lax.all_to_all(folded, ("y", "c"), 0, 0)
     left, right, folded = lax.optimization_barrier((left, right, folded))
     low = lax.ppermute(left[:cut], "x", ring(nx, 1))
     high = lax.ppermute(right[cut:], "x", ring(nx, nx - 1))

time: 144 us -> 142 us (0.986)
  blocking collectives: 92.3 us -> 86.6 us
  waiting for transfers between devices: 4.35 us -> 8.51 us
    all_gather x1 -> x0, blocking collectives: 12.9 us -> none  [shards(): folded = lax.all_gather(folded, ('y', 'c'), axis=0, tiled=False)]
    all_to_all x0 -> x1, blocking collectives: none -> 8.69 us  [shards(): folded = lax.all_to_all(folded, ('y', 'c'), 0, 0)]
    ppermute x1, waiting for transfers between devices: 1.64 us -> 5.8 us  [shards(): left = lax.ppermute(wide, 'x', ring(nx, 1))]
where the time goes in v4:
time: 142 us; the launch traced here: 141 us
  blocking collectives  86.6 us (61%)
  starting transfers between devices  35.9 us (25%)
  waiting for transfers between devices  8.51 us (6%)
  Pallas kernels  6.44 us (5%)
  local copies, waits for them, and re-layouts  3.36 us (2%)
    all_gather x1, blocking collectives, shards(): columns = lax.all_gather(packed, 'zh', axis=0, tiled=False)  40.3 us
    all_to_all x1, blocking collectives, shards(): parts = lax.all_to_all(parts, TP, 0, 0)  24.2 us
    all_gather x1, blocking collectives, shards(): lax.all_gather(jnp.concatenate([near, gains], axis=1), 'x', axis=0, tiled...  13.5 us
    ppermute x1, starting transfers between devices, shards(): near = lax.ppermute(near, AXES, decoder_moves(sizes))  11.4 us
    ppermute x3, starting transfers between devices, shards(): lax.ppermute(folded, 'zl', ring(nzl, k))  9.92 us
    all_to_all x1, blocking collectives, shards(): folded = lax.all_to_all(folded, ('y', 'c'), 0, 0)  8.69 us
    ppermute x1, waiting for transfers between devices, shards(): left = lax.ppermute(wide, 'x', ring(nx, 1))  5.8 us
    ppermute x1, starting transfers between devices, shards(): high = lax.ppermute(right[cut:], 'x', ring(nx, nx - 1))  4.95 us
  transfers between devices with their start and end apart: 8, of which 3 were waited for; matrix products, arithmetic and copies ran while one was open for 1% of the time, Pallas kernels for 3%

profile of v4, /device:TPU:24, one launch (start us, length us, event | category | flops | bytes accessed | tf_op | source)
XLA Modules:
  0.0 141.1 jit_solution(4785174068313901547)
XLA Ops:
  0.0 0.9 constant_dynamic-slice_fusion
  0.9 11.4 %collective-permute-start = (bf16[16,4608]{1,0:T(8,128)(2,1)S(1)}, bf16[16,4608]{1,0:T(8,128)(2,1)S(1)}, u32[]{:S(2)}, u32[]{:S(2)}) collective-permute-start(bf16[16,4608]{1,0:T(8,128)(2,1)S(1)} %constant_dynamic-slice_fusion), channel_id=1, source_target_pairs={{387,0},{384,1},{385,2},{386,3},{391,4},{388,5},{389,6},{390,7},{3... | collective-permute-start | bytes 442376 | tf_op jit(solution)/shard_map/ppermute | solution.py:248
  12.3 0.7 broadcast_in_dim.12.post_ref
  13.0 0.7 broadcast_in_dim.13.pre_ref
  13.7 0.9 copy-done.3
  14.7 40.3 %all-gather = bf16[1216,384]{1,0:T(8,128)(2,1)S(1)} all-gather(bf16[304,384]{1,0:T(8,128)(2,1)S(1)} %shard_map.109), channel_id=2, replica_groups=mesh['zl'=4,'y'=4,'c'=2,'x'=4,'zh'=4] {'zh'}, dimensions={0}, use_global_device_ids=true | all-gather | bytes 1167360 | tf_op jit(solution)/shard_map/all_gather | solution.py:254
  55.0 0.1 shard_map.110
  55.1 13.5 %all-gather.1 = bf16[64,4992]{1,0:T(8,128)(2,1)S(1)} all-gather(bf16[16,4992]{1,0:T(8,128)(2,1)S(1)} %pad_maximum_fusion), channel_id=3, replica_groups=mesh['zl'=4,'y'=4,'c'=2,'x'=4,'zh'=4] {'x'}, dimensions={0}, use_global_device_ids=true | all-gather | bytes 798720 | tf_op jit(solution)/shard_map/all_gather | solution.py:264
  68.6 3.8 %collective-permute-start.1 = (bf16[1152,384]{1,0:T(8,128)(2,1)S(1)}, bf16[1152,384]{1,0:T(8,128)(2,1)S(1)}, u32[]{:S(2)}, u32[]{:S(2)}) collective-permute-start(bf16[1152,384]{1,0:T(8,128)(2,1)S(1)} %get-tuple-element.16.own), channel_id=1, source_target_pairs={{0,4},{4,8},{8,12},{12,0},{1,5},{5,9},{9,13},{13,1},{2,6},{6,10},{... | collective-permute-start | bytes 2654216 | tf_op jit(solution)/shard_map/ppermute | solution.py:266
  72.4 3.2 %collective-permute-start.2 = (bf16[1152,384]{1,0:T(8,128)(2,1)S(1)}, bf16[1152,384]{1,0:T(8,128)(2,1)S(1)}, u32[]{:S(2)}, u32[]{:S(2)}) collective-permute-start(bf16[1152,384]{1,0:T(8,128)(2,1)S(1)} %get-tuple-element.16.own), channel_id=1, source_target_pairs={{0,12},{4,0},{8,4},{12,8},{1,13},{5,1},{9,5},{13,9},{2,14},{6,2},{... | collective-permute-start | bytes 2654216 | tf_op jit(solution)/shard_map/ppermute | solution.py:267
  75.7 1.3 shard_map.111
  77.0 8.7 %all_to_all.10 = bf16[8,64,128]{2,1,0:T(8,128)(2,1)S(1)} all-to-all(bf16[8,64,128]{2,1,0:T(8,128)(2,1)S(1)} %shard_map.111), channel_id=1, replica_groups=mesh['zl'=4,'y'=4,'c'=2,'x'=4,'zh'=4] {'y','c'}, dimensions={0} | all-to-all | bytes 262144 | tf_op jit(solution)/shard_map/all_to_all | solution.py:281
  85.7 5.8 %collective-permute-done.1.left = bf16[1152,384]{1,0:T(8,128)(2,1)S(1)} collective-permute-done((bf16[1152,384]{1,0:T(8,128)(2,1)S(1)}, bf16[1152,384]{1,0:T(8,128)(2,1)S(1)}, u32[]{:S(2)}, u32[]{:S(2)}) %collective-permute-start.1) | collective-permute-done | bytes 884768 | tf_op jit(solution)/shard_map/ppermute | solution.py:266
  91.5 1.2 collective-permute-done.2.right
  92.8 2.6 %collective-permute-start.3 = (bf16[640,384]{1,0:T(8,128)(2,1)S(1)}, bf16[640,384]{1,0:T(8,128)(2,1)S(1)}, u32[]{:S(2)}, u32[]{:S(2)}) collective-permute-start(bf16[640,384]{1,0:T(8,128)(2,1)S(1)} %slice.6), channel_id=1, source_target_pairs={{0,4},{4,8},{8,12},{12,0},{1,5},{5,9},{9,13},{13,1},{2,6},{6,10},{... | collective-permute-start | bytes 1474568 | tf_op jit(solution)/shard_map/ppermute | solution.py:283
  95.4 4.9 %collective-permute-start.4 = (bf16[512,384]{1,0:T(8,128)(2,1)S(1)}, bf16[512,384]{1,0:T(8,128)(2,1)S(1)}, u32[]{:S(2)}, u32[]{:S(2)}) collective-permute-start(bf16[512,384]{1,0:T(8,128)(2,1)S(1)} %slice.7), channel_id=1, source_target_pairs={{0,12},{4,0},{8,4},{12,8},{1,13},{5,1},{9,5},{13,9},{2,14},{6,2},{... | collective-permute-start | bytes 1179656 | tf_op jit(solution)/shard_map/ppermute | solution.py:284
  100.3 1.9 %collective-permute-start.5 = (bf16[8,4,16,128]{3,2,1,0:T(8,128)(2,1)S(1)}, bf16[8,4,16,128]{3,2,1,0:T(8,128)(2,1)S(1)}, u32[]{:S(2)}, u32[]{:S(2)}) collective-permute-start(bf16[8,4,16,128]{3,2,1,0:T(8,128)(2,1)S(1)} %bitcast.11), channel_id=1, source_target_pairs={{0,256},{128,384},{256,0},{384,128},{1,257},{129,385},{257,1},{385... | collective-permute-start | bytes 393224 | tf_op jit(solution)/shard_map/ppermute | solution.py:286
  102.3 6.1 %collective-permute-start.6 = (bf16[8,4,16,128]{3,2,1,0:T(8,128)(2,1)S(1)}, bf16[8,4,16,128]{3,2,1,0:T(8,128)(2,1)S(1)}, u32[]{:S(2)}, u32[]{:S(2)}) collective-permute-start(bf16[8,4,16,128]{3,2,1,0:T(8,128)(2,1)S(1)} %bitcast.12), channel_id=1, source_target_pairs={{0,128},{128,256},{256,384},{384,0},{1,129},{129,257},{257,385},{3... | collective-permute-start | bytes 393224 | tf_op jit(solution)/shard_map/ppermute | solution.py:286
  108.4 1.9 %collective-permute-start.7 = (bf16[8,4,16,128]{3,2,1,0:T(8,128)(2,1)S(1)}, bf16[8,4,16,128]{3,2,1,0:T(8,128)(2,1)S(1)}, u32[]{:S(2)}, u32[]{:S(2)}) collective-permute-start(bf16[8,4,16,128]{3,2,1,0:T(8,128)(2,1)S(1)} %bitcast.13), channel_id=1, source_target_pairs={{0,384},{128,0},{256,128},{384,256},{1,385},{129,1},{257,129},{385... | collective-permute-start | bytes 393224 | tf_op jit(solution)/shard_map/ppermute | solution.py:286
  110.4 3.3 %shard_map.112 = (bf16[384,128]{1,0:T(8,128)(2,1)S(1)}, f32[384,128]{1,0:T(8,128)S(1)}) custom-call(bf16[1152,384]{1,0:T(8,128)(2,1)S(1)} %get-tuple-element.16.own, bf16[1152,384]{1,0:T(8,128)(2,1)S(1)} %collective-permute-done.1.left, bf16[1152,384]{1,0:T(8,128)(2,1)S(1)} %collective-permute-done.2.right, bf16[640,384]{1,0:T(8,128)(2,1)S(1)} %collective-permute-done.3.low, ...), custom_call_target="tpu_custom_call" | custom-call | tf_op jit(solution)/shard_map/pallas_call | solution.py:288
  113.7 1.5 %collective-permute-done.7.m3 = bf16[8,4,16,128]{3,2,1,0:T(8,128)(2,1)S(1)} collective-permute-done((bf16[8,4,16,128]{3,2,1,0:T(8,128)(2,1)S(1)}, bf16[8,4,16,128]{3,2,1,0:T(8,128)(2,1)S(1)}, u32[]{:S(2)}, u32[]{:S(2)}) %collective-permute-start.7) | collective-permute-done | bytes 131104 | tf_op jit(solution)/shard_map/ppermute | solution.py:286
  115.2 1.0 shard_map.113
  116.3 24.2 %all_to_all.11.parts_ref = bf16[16,16,384]{2,1,0:T(8,128)(2,1)S(1)} all-to-all(bf16[16,16,384]{2,1,0:T(8,128)(2,1)S(1)} %shard_map.113), channel_id=1, replica_groups=mesh['zl'=4,'y'=4,'c'=2,'x'=4,'zh'=4] {'x','zh'}, dimensions={0} | all-to-all | bytes 393216 | tf_op jit(solution)/shard_map/all_to_all | solution.py:311
  140.5 0.6 shard_map.114
  (26 shorter events, 0.3 us)
Async XLA Ops:
  0.9 54.2 %collective-permute-start = (bf16[16,4608]{1,0:T(8,128)(2,1)S(1)}, bf16[16,4608]{1,0:T(8,128)(2,1)S(1)}, u32[]{:S(2)}, u32[]{:S(2)}) collective-permute-start(bf16[16,4608]{1,0:T(8,128)(2,1)S(1)} %constant_dynamic-slice_fusion), channel_id=1, source_target_pairs={{387,0},{384,1},{385,2},{386,3},{391,4},{388,5},{389,6},{390,7},{3... | collective-permute-start | bytes 442376 | tf_op jit(solution)/shard_map/ppermute | solution.py:248
  13.7 0.9 copy-start.3
  55.0 20.7 %copy-start.2 = (bf16[128,4608]{1,0:T(8,128)(2,1)S(1)}, bf16[128,4608]{1,0:T(8,128)(2,1)}, u32[]{:S(2)}) copy-start(bf16[128,4608]{1,0:T(8,128)(2,1)} %value_ref.1) | copy-start | bytes 3538948
  68.6 22.9 %collective-permute-start.1 = (bf16[1152,384]{1,0:T(8,128)(2,1)S(1)}, bf16[1152,384]{1,0:T(8,128)(2,1)S(1)}, u32[]{:S(2)}, u32[]{:S(2)}) collective-permute-start(bf16[1152,384]{1,0:T(8,128)(2,1)S(1)} %get-tuple-element.16.own), channel_id=1, source_target_pairs={{0,4},{4,8},{8,12},{12,0},{1,5},{5,9},{9,13},{13,1},{2,6},{6,10},{... | collective-permute-start | bytes 2654216 | tf_op jit(solution)/shard_map/ppermute | solution.py:266
  72.4 20.3 %collective-permute-start.2 = (bf16[1152,384]{1,0:T(8,128)(2,1)S(1)}, bf16[1152,384]{1,0:T(8,128)(2,1)S(1)}, u32[]{:S(2)}, u32[]{:S(2)}) collective-permute-start(bf16[1152,384]{1,0:T(8,128)(2,1)S(1)} %get-tuple-element.16.own), channel_id=1, source_target_pairs={{0,12},{4,0},{8,4},{12,8},{1,13},{5,1},{9,5},{13,9},{2,14},{6,2},{... | collective-permute-start | bytes 2654216 | tf_op jit(solution)/shard_map/ppermute | solution.py:267
  75.7 34.6 %copy-start = (bf16[256,4608]{1,0:T(8,128)(2,1)S(1)}, bf16[256,4608]{1,0:T(8,128)(2,1)}, u32[]{:S(2)}) copy-start(bf16[256,4608]{1,0:T(8,128)(2,1)} %out_proj.1) | copy-start | bytes 7077892
  77.0 33.3 %copy-start.1 = (bf16[128,4608]{1,0:T(8,128)(2,1)S(1)}, bf16[128,4608]{1,0:T(8,128)(2,1)}, u32[]{:S(2)}) copy-start(bf16[128,4608]{1,0:T(8,128)(2,1)} %decoder.1) | copy-start | bytes 3538948
  77.0 33.3 %copy-start.4 = (bf16[2,128,128]{2,1,0:T(8,128)(2,1)S(1)}, bf16[2,128,128]{2,1,0:T(8,128)(2,1)}, u32[]{:S(2)}) copy-start(bf16[2,128,128]{2,1,0:T(8,128)(2,1)} %patterns_ref.1) | copy-start | bytes 196612
  77.0 33.3 %copy-start.7 = (f32[128]{0:T(128)S(1)}, f32[128]{0:T(128)}, u32[]{:S(2)}) copy-start(f32[128]{0:T(128)} %param.12) | copy-start | bytes 1540
  92.8 17.5 %collective-permute-start.3 = (bf16[640,384]{1,0:T(8,128)(2,1)S(1)}, bf16[640,384]{1,0:T(8,128)(2,1)S(1)}, u32[]{:S(2)}, u32[]{:S(2)}) collective-permute-start(bf16[640,384]{1,0:T(8,128)(2,1)S(1)} %slice.6), channel_id=1, source_target_pairs={{0,4},{4,8},{8,12},{12,0},{1,5},{5,9},{9,13},{13,1},{2,6},{6,10},{... | collective-permute-start | bytes 1474568 | tf_op jit(solution)/shard_map/ppermute | solution.py:283
  95.4 14.9 %collective-permute-start.4 = (bf16[512,384]{1,0:T(8,128)(2,1)S(1)}, bf16[512,384]{1,0:T(8,128)(2,1)S(1)}, u32[]{:S(2)}, u32[]{:S(2)}) collective-permute-start(bf16[512,384]{1,0:T(8,128)(2,1)S(1)} %slice.7), channel_id=1, source_target_pairs={{0,12},{4,0},{8,4},{12,8},{1,13},{5,1},{9,5},{13,9},{2,14},{6,2},{... | collective-permute-start | bytes 1179656 | tf_op jit(solution)/shard_map/ppermute | solution.py:284
  100.3 13.3 %collective-permute-start.5 = (bf16[8,4,16,128]{3,2,1,0:T(8,128)(2,1)S(1)}, bf16[8,4,16,128]{3,2,1,0:T(8,128)(2,1)S(1)}, u32[]{:S(2)}, u32[]{:S(2)}) collective-permute-start(bf16[8,4,16,128]{3,2,1,0:T(8,128)(2,1)S(1)} %bitcast.11), channel_id=1, source_target_pairs={{0,256},{128,384},{256,0},{384,128},{1,257},{129,385},{257,1},{385... | collective-permute-start | bytes 393224 | tf_op jit(solution)/shard_map/ppermute | solution.py:286
  102.3 11.4 %collective-permute-start.6 = (bf16[8,4,16,128]{3,2,1,0:T(8,128)(2,1)S(1)}, bf16[8,4,16,128]{3,2,1,0:T(8,128)(2,1)S(1)}, u32[]{:S(2)}, u32[]{:S(2)}) collective-permute-start(bf16[8,4,16,128]{3,2,1,0:T(8,128)(2,1)S(1)} %bitcast.12), channel_id=1, source_target_pairs={{0,128},{128,256},{256,384},{384,0},{1,129},{129,257},{257,385},{3... | collective-permute-start | bytes 393224 | tf_op jit(solution)/shard_map/ppermute | solution.py:286
  108.4 6.9 %collective-permute-start.7 = (bf16[8,4,16,128]{3,2,1,0:T(8,128)(2,1)S(1)}, bf16[8,4,16,128]{3,2,1,0:T(8,128)(2,1)S(1)}, u32[]{:S(2)}, u32[]{:S(2)}) collective-permute-start(bf16[8,4,16,128]{3,2,1,0:T(8,128)(2,1)S(1)} %bitcast.13), channel_id=1, source_target_pairs={{0,384},{128,0},{256,128},{384,256},{1,385},{129,1},{257,129},{385... | collective-permute-start | bytes 393224 | tf_op jit(solution)/shard_map/ppermute | solution.py:286
  110.3 4.9 %copy-start.6 = (s32[128,2]{0,1:T(2,128)S(1)}, s32[128,2]{0,1:T(2,128)}, u32[]{:S(2)}) copy-start(s32[128,2]{0,1:T(2,128)} %param.20) | copy-start | bytes 3076
  110.4 4.9 %copy-start.8 = (f32[128]{0:T(128)S(1)}, f32[128]{0:T(128)}, u32[]{:S(2)}) copy-start(f32[128]{0:T(128)} %param.17) | copy-start | bytes 1540
  113.7 26.8 %copy-start.5 = (bf16[8,256]{1,0:T(8,128)(2,1)S(1)}, bf16[8,256]{1,0:T(8,128)(2,1)}, u32[]{:S(2)}) copy-start(bf16[8,256]{1,0:T(8,128)(2,1)} %acts_ref.1) | copy-start | bytes 12292

commit v5 on v4

--- a/solution.py
+++ b/solution.py
@@ -12,10 +12,12 @@
 AXES = ("zl", "y", "c", "x", "zh")
 GRP = ("zl", "y", "c")
 TP = ("x", "zh")
-TURNS = (0, 2, 1, 3)
+TURNS = (0, 1, 3, 2)
+ORDER = (2, 3, 0, 1)
 F32 = jnp.float32
 BF16 = jnp.bfloat16
 PARAMS = pltpu.CompilerParams(vmem_limit_bytes=40 * 1024 * 1024)
+FULL = pltpu.CompilerParams(vmem_limit_bytes=60 * 1024 * 1024)
 
 
 def source_block(zh, zl, n):
@@ -44,17 +46,34 @@
     return lax.dot_general(left, right, (dims, ((), ())), preferred_element_type=F32)
 
 
-def pack_kernel(top_ref, post_ref, pre_ref, out_ref):
-    targets, local, seq = top_ref.shape
+def front_kernel(share, top, out_proj, dec, post, pre, out_ref, far_ref, near_ref, flat0, flat1, sems):
+    targets, local, seq = top.shape
     wide = targets * seq
+    height, chunk = out_proj.shape[0], far_ref.shape[1]
+    first = pl.multiple_of(lax.rem(lax.axis_index("x") + 2, 4) * chunk, LANES)
+    cols = pl.ds(first, chunk)
+    copies = [
+        pltpu.make_async_copy(post, flat0, sems.at[0]),
+        pltpu.make_async_copy(pre, flat1, sems.at[1]),
+        pltpu.make_async_copy(out_proj.at[:, cols], far_ref.at[pl.ds(0, height), :], sems.at[2]),
+        pltpu.make_async_copy(dec.at[:, cols], far_ref.at[pl.ds(height, BLK), :], sems.at[3]),
+    ]
+    rows = pl.ds(pl.multiple_of(lax.axis_index(("y", "c")) * share, share), share)
+    copies.append(pltpu.make_async_copy(dec.at[rows, :], near_ref, sems.at[4 + targets]))
     for r in range(targets):
-        out_ref[0:local, r * seq : (r + 1) * seq] = top_ref[r]
+        place = out_ref.at[pl.ds(0, local), pl.ds(r * seq, seq)]
+        copies.append(pltpu.make_async_copy(top.at[r], place, sems.at[4 + r]))
+    for c in copies:
+        c.start()
+    for c in copies[:2]:
+        c.wait()
     zh = lax.axis_index("zh")
     lane = lax.broadcasted_iota(jnp.int32, (8, wide), 1)
     line = lax.broadcasted_iota(jnp.int32, (8, wide), 0)
     both = []
-    for ref in (post_ref, pre_ref):
-        flat = jnp.concatenate([ref[...].astype(F32), jnp.zeros((1, wide - local), F32)], axis=1)
+    for ref in (flat0, flat1):
+        flat = ref[...].astype(F32).reshape(1, local)
+        flat = jnp.concatenate([flat, jnp.zeros((1, wide - local), F32)], axis=1)
         full = jnp.broadcast_to(flat, (8, wide))
         moved = full
         for z in range(1, 4):
@@ -62,6 +81,15 @@
         place = line * wide + lane - zh * local
         both.append(jnp.where((place >= 0) & (place < local), moved, 0.0))
     out_ref[local:, :] = jnp.concatenate(both, axis=0).astype(BF16)
+    for c in copies[2:]:
+        c.wait()
+
+
+def far_kernel(width, wide_ref, weights_ref, gain_ref, out_ref):
+    gain = gain_row(gain_ref[...], 0, weights_ref.shape[1] // gain_ref.shape[1])
+    proj = weights_ref[0:width] * gain.astype(BF16)
+    weights = jnp.concatenate([proj, weights_ref[width:]], axis=0)
+    out_ref[...] = dot(weights, wide_ref[...], ((1,), (0,))).astype(BF16)
 
 
 def join_kernel(columns_ref, wide_ref, gain_ref):
@@ -102,8 +130,7 @@
     own,
     left,
     right,
-    low,
-    high,
+    far,
     out_proj,
     decoder,
     near,
@@ -122,7 +149,7 @@
     chunk = proj_buf.shape[2]
     size = 4
     mine = lax.axis_index("x")
-    places = [lax.rem(mine + size - turn, size) for turn in (0, 1, 3, 2)]
+    places = [lax.rem(mine + size - turn, size) for turn in (0, 1, 3)]
     tail = pl.ds(decoder.shape[1], gains_ref.shape[2])
     fetch = pltpu.make_async_copy(near.at[:, pl.ds(0, 16), tail], gains_ref, sem)
     fetch.start()
@@ -137,19 +164,14 @@
             c.start()
         copies.append(group)
     fetch.wait()
-    total = None
-    for n, sources in enumerate(((own,), (left,), (right,), (low, high))):
+    total = far[...].astype(F32)
+    for n, source in enumerate((own, left, right)):
         for c in copies[n]:
             c.wait()
         gain = gain_row(gains_ref[places[n]], 0, chunk // gains_ref.shape[2])
         proj = proj_buf[n] * gain.astype(BF16)
         weights = jnp.concatenate([proj, dec_buf[n]], axis=0)
-        first = 0
-        for source in sources:
-            last = first + source.shape[0]
-            part = dot(weights[:, first:last], source[...], ((1,), (0,)))
-            total = part if total is None else total + part
-            first = last
+        total += dot(weights, source[...], ((1,), (0,)))
     post = jnp.concatenate([post_ref[...]] * targets, axis=1)
     head_grad = (total[0:width] * post).astype(BF16)
     for r in range(targets):
@@ -195,9 +217,10 @@
             totals[k][r] = totals[k][r] * pre + picked
     piece = seq // owners
     for i in range(owners):
+        place = ORDER.index(i // nzh) * nzh + ORDER.index(i % nzh)
         for r in range(targets):
             both = [totals[k][r][i * piece : (i + 1) * piece] for k in range(slots)]
-            out_ref[i, :, r * BLK : (r + 1) * BLK] = jnp.concatenate(both, axis=0).astype(BF16)
+            out_ref[place, :, r * BLK : (r + 1) * BLK] = jnp.concatenate(both, axis=0).astype(BF16)
 
 
 def last_kernel(targets, parts_ref, acts_ref, out_ref):
@@ -241,16 +264,23 @@
     vmem = pl.BlockSpec(memory_space=pltpu.VMEM)
     hbm = pl.BlockSpec(memory_space=pl.ANY)
 
-    cut = chunk // 2 // LANES * LANES + LANES
-
-    copy = lax.axis_index(("y", "c"))
-    near = lax.dynamic_slice_in_dim(decoder, copy * share, share, axis=0)
+    packed, weights, near = pl.pallas_call(
+        functools.partial(front_kernel, share),
+        in_specs=[hbm] * 5,
+        out_shape=[
+            jax.ShapeDtypeStruct((local + 16, rows), BF16),
+            jax.ShapeDtypeStruct((heads * head + BLK, chunk), BF16),
+            jax.ShapeDtypeStruct((share, width), BF16),
+        ],
+        scratch_shapes=[
+            pltpu.VMEM((local,), BF16),
+            pltpu.VMEM((local,), BF16),
+            pltpu.SemaphoreType.DMA((5 + targets,)),
+        ],
+        compiler_params=FULL,
+    )(grad_top.transpose(0, 2, 1), out_proj, decoder, post_gain, pre_gain)
     near = lax.ppermute(near, AXES, decoder_moves(sizes))
-    packed = pl.pallas_call(
-        pack_kernel,
-        out_shape=jax.ShapeDtypeStruct((local + 16, rows), BF16),
-        compiler_params=PARAMS,
-    )(grad_top.transpose(0, 2, 1), post_gain[None, :], pre_gain[None, :])
+    weights = lax.ppermute(weights, "x", ring(nx, 2))
     columns = lax.all_gather(packed, "zh", axis=0, tiled=False)
     wide, gains = pl.pallas_call(
         join_kernel,
@@ -260,11 +290,17 @@
         ],
         compiler_params=PARAMS,
     )(columns)
-    gains = jnp.pad(gains, ((0, share - 16), (0, 0)))
-    near = lax.all_gather(jnp.concatenate([near, gains], axis=1), "x", axis=0, tiled=False)
+    tail = jnp.pad(gains, ((0, share - 16), (0, 0)))
+    near = lax.all_gather(jnp.concatenate([near, tail], axis=1), "x", axis=0, tiled=False)
     wide, near = lax.optimization_barrier((wide, near))
     left = lax.ppermute(wide, "x", ring(nx, 1))
     right = lax.ppermute(wide, "x", ring(nx, nx - 1))
+    far = pl.pallas_call(
+        functools.partial(far_kernel, heads * head),
+        out_shape=jax.ShapeDtypeStruct((heads * head + BLK, rows), BF16),
+        compiler_params=PARAMS,
+    )(wide, weights, gains)
+    far = lax.ppermute(far, "x", ring(nx, 2))
     folded = pl.pallas_call(
         fold_kernel,
         grid=(nx,),
@@ -279,15 +315,12 @@
         compiler_params=PARAMS,
     )(near, near, value_proj)
     folded = lax.all_to_all(folded, ("y", "c"), 0, 0)
-    left, right, folded = lax.optimization_barrier((left, right, folded))
-    low = lax.ppermute(left[:cut], "x", ring(nx, 1))
-    high = lax.ppermute(right[cut:], "x", ring(nx, nx - 1))
     folded = folded.reshape(copies, nx, share, head)
     foldeds = [folded if k == 0 else lax.ppermute(folded, "zl", ring(nzl, k)) for k in TURNS]
 
     value, direct = pl.pallas_call(
         functools.partial(value_kernel, (targets, seq, heads, head)),
-        in_specs=[vmem] * 5 + [hbm] * 3 + [vmem] * 2,
+        in_specs=[vmem] * 4 + [hbm] * 3 + [vmem] * 2,
         out_specs=[vmem, vmem],
         out_shape=[
             jax.ShapeDtypeStruct((rows, head), BF16),
@@ -295,20 +328,21 @@
         ],
         scratch_shapes=[
             pltpu.VMEM((nx, 16, rows), BF16),
-            pltpu.VMEM((nx, heads * head, chunk), BF16),
-            pltpu.VMEM((nx, BLK, chunk), BF16),
+            pltpu.VMEM((3, heads * head, chunk), BF16),
+            pltpu.VMEM((3, BLK, chunk), BF16),
             pltpu.SemaphoreType.DMA,
-            pltpu.SemaphoreType.DMA((2, nx)),
-        ],
-        compiler_params=PARAMS,
-    )(wide, left, right, low, high, out_proj, decoder, near, post_scale[None, :], patterns)
+            pltpu.SemaphoreType.DMA((2, 3)),
+        ],
+        compiler_params=PARAMS,
+    )(wide, left, right, far, out_proj, decoder, near, post_scale[None, :], patterns)
     parts = pl.pallas_call(
         functools.partial(score_kernel, (targets, seq, nx, nzh, owners)),
         out_shape=jax.ShapeDtypeStruct((owners, slots * tokens, targets * BLK), BF16),
         compiler_params=PARAMS,
     )(value, direct, pre_scale[None, :], block_ids.T, *foldeds)
 
-    parts = lax.all_to_all(parts, TP, 0, 0)
+    group = [i * nzh + z for i in ORDER for z in ORDER]
+    parts = lax.all_to_all(parts, TP, 0, 0, axis_index_groups=[group])
     return pl.pallas_call(
         functools.partial(last_kernel, targets),
         out_shape=jax.ShapeDtypeStruct((targets, tokens, slots * BLK), F32),

time: 142 us -> 136 us (0.958); the launches traced: 141 us -> 134 us
  waiting for transfers between devices: 8.51 us -> 4.9 us
  local copies, waits for them, and re-layouts: 3.36 us -> 0.05 us
  Pallas kernels: 6.44 us -> 8.67 us
  blocking collectives: 86.6 us -> 84.4 us
    ppermute x1, waiting for transfers between devices: 5.8 us -> 0.01 us  [shards(): left = lax.ppermute(wide, 'x', ring(nx, 1))]
    ppermute x3, waiting for transfers between devices: 1.52 us -> 4.89 us  [shards(): lax.ppermute(folded, 'zl', ring(nzl, k))]
    pallas_call x1 -> x2, Pallas kernels: 0.09 us -> 3.04 us  [the longest x1 2.4 us: shards(): pl.pallas_call(functools.partial(front_kernel, share), in_specs=[hbm] * 5...]
    all_to_all x1, blocking collectives: 24.2 us -> 21.3 us  [shards(): parts = lax.all_to_all(parts, TP, 0, 0, axis_index_groups=[group])]
    ppermute x1, starting transfers between devices: 3.21 us -> 5.13 us  [shards(): right = lax.ppermute(wide, 'x', ring(nx, nx - 1))]
    ppermute x1, starting transfers between devices: 3.83 us -> 2.04 us  [shards(): left = lax.ppermute(wide, 'x', ring(nx, 1))]
  transfers between devices with their start and end apart: 8 -> 8, of which waited for: 3 -> 1; matrix products, arithmetic and copies ran while one was open for 1% -> 0% of each run, Pallas kernels for 3% -> 3%
where the time goes in v5:
time: 136 us; the launch traced here: 134 us
  blocking collectives  84.4 us (62%)
  starting transfers between devices  35.3 us (26%)
  Pallas kernels  8.67 us (6%)
  waiting for transfers between devices  4.9 us (4%)
    all_gather x1, blocking collectives, shards(): columns = lax.all_gather(packed, 'zh', axis=0, tiled=False)  40.7 us
    all_to_all x1, blocking collectives, shards(): parts = lax.all_to_all(parts, TP, 0, 0, axis_index_groups=[group])  21.3 us
    all_gather x1, blocking collectives, shards(): lax.all_gather(jnp.concatenate([near, tail], axis=1), 'x', axis=0, tiled=...  13.8 us
    ppermute x1, starting transfers between devices, shards(): near = lax.ppermute(near, AXES, decoder_moves(sizes))  11.4 us
    ppermute x3, starting transfers between devices, shards(): lax.ppermute(folded, 'zl', ring(nzl, k))  9.55 us
    all_to_all x1, blocking collectives, shards(): folded = lax.all_to_all(folded, ('y', 'c'), 0, 0)  8.56 us
    ppermute x1, starting transfers between devices, shards(): right = lax.ppermute(wide, 'x', ring(nx, nx - 1))  5.13 us
    ppermute x1, starting transfers between devices, shards(): weights = lax.ppermute(weights, 'x', ring(nx, 2))  4.93 us
  transfers between devices with their start and end apart: 8, of which 1 were waited for; matrix products, arithmetic and copies ran while one was open for 0% of the time, Pallas kernels for 3%

profile of v5, /device:TPU:24, one launch (start us, length us, event | category | flops | bytes accessed | tf_op | source)
XLA Modules:
  0.0 133.6 jit_solution(9888350609527778808)
XLA Ops:
  0.0 2.4 %shard_map.109 = (bf16[304,384]{1,0:T(8,128)(2,1)}, bf16[384,1152]{1,0:T(8,128)(2,1)}, bf16[16,4608]{1,0:T(8,128)(2,1)}) custom-call(bf16[3,288,128]{2,1,0:T(8,128)(2,1)} %bitcast.18, bf16[256,4608]{1,0:T(8,128)(2,1)} %out_proj.3, bf16[128,4608]{1,0:T(8,128)(2,1)} %decoder.1, bf16[288]{0:T(512)(128)(2,1)} %post.1, bf16[288]{0:T(512)(128)(2,1)} %pre.1), custom_call_target="tpu_custom_call" | custom-call | tf_op jit(solution)/shard_map/pallas_call | solution.py:267
  2.4 11.4 %collective-permute-start = (bf16[16,4608]{1,0:T(8,128)(2,1)}, bf16[16,4608]{1,0:T(8,128)(2,1)S(1)}, u32[]{:S(2)}, u32[]{:S(2)}) collective-permute-start(bf16[16,4608]{1,0:T(8,128)(2,1)} %get-tuple-element.16), channel_id=1, source_target_pairs={{387,0},{384,1},{385,2},{386,3},{391,4},{388,5},{389,6},{390,7},{3... | collective-permute-start | bytes 442376 | tf_op jit(solution)/shard_map/ppermute | solution.py:282
  13.8 4.9 %collective-permute-start.3 = (bf16[384,1152]{1,0:T(8,128)(2,1)}, bf16[384,1152]{1,0:T(8,128)(2,1)S(1)}, u32[]{:S(2)}, u32[]{:S(2)}) collective-permute-start(bf16[384,1152]{1,0:T(8,128)(2,1)} %get-tuple-element.19), channel_id=1, source_target_pairs={{0,8},{4,12},{8,0},{12,4},{1,9},{5,13},{9,1},{13,5},{2,10},{6,14},... | collective-permute-start | bytes 2654216 | tf_op jit(solution)/shard_map/ppermute | solution.py:283
  18.8 40.7 %all-gather = bf16[1216,384]{1,0:T(8,128)(2,1)S(1)} all-gather(bf16[304,384]{1,0:T(8,128)(2,1)} %get-tuple-element.14), channel_id=2, replica_groups=mesh['zl'=4,'y'=4,'c'=2,'x'=4,'zh'=4] {'zh'}, dimensions={0}, use_global_device_ids=true | all-gather | bytes 1167360 | tf_op jit(solution)/shard_map/all_gather | solution.py:284
  59.4 0.1 shard_map.110
  59.6 13.8 %all-gather.1 = bf16[64,4992]{1,0:T(8,128)(2,1)S(1)} all-gather(bf16[16,4992]{1,0:T(8,128)(2,1)S(1)} %pad_maximum_fusion), channel_id=3, replica_groups=mesh['zl'=4,'y'=4,'c'=2,'x'=4,'zh'=4] {'x'}, dimensions={0}, use_global_device_ids=true | all-gather | bytes 798720 | tf_op jit(solution)/shard_map/all_gather | solution.py:294
  73.4 2.0 %collective-permute-start.1 = (bf16[1152,384]{1,0:T(8,128)(2,1)S(1)}, bf16[1152,384]{1,0:T(8,128)(2,1)S(1)}, u32[]{:S(2)}, u32[]{:S(2)}) collective-permute-start(bf16[1152,384]{1,0:T(8,128)(2,1)S(1)} %get-tuple-element.18.wide_ref.own), channel_id=1, source_target_pairs={{0,4},{4,8},{8,12},{12,0},{1,5},{5,9},{9,13},{13,1},{2,6},{6,10},{... | collective-permute-start | bytes 2654216 | tf_op jit(solution)/shard_map/ppermute | solution.py:296
  75.5 5.1 %collective-permute-start.2 = (bf16[1152,384]{1,0:T(8,128)(2,1)S(1)}, bf16[1152,384]{1,0:T(8,128)(2,1)S(1)}, u32[]{:S(2)}, u32[]{:S(2)}) collective-permute-start(bf16[1152,384]{1,0:T(8,128)(2,1)S(1)} %get-tuple-element.18.wide_ref.own), channel_id=1, source_target_pairs={{0,12},{4,0},{8,4},{12,8},{1,13},{5,1},{9,5},{13,9},{2,14},{6,2},{... | collective-permute-start | bytes 2654216 | tf_op jit(solution)/shard_map/ppermute | solution.py:297
  80.6 0.0 copy-start.1
  80.6 0.6 shard_map.111
  81.3 0.0 copy-start
  81.3 0.0 copy-start.3
  81.3 0.0 copy-start.6
  81.3 2.3 %collective-permute-start.4 = (bf16[384,384]{1,0:T(8,128)(2,1)S(1)}, bf16[384,384]{1,0:T(8,128)(2,1)S(1)}, u32[]{:S(2)}, u32[]{:S(2)}) collective-permute-start(bf16[384,384]{1,0:T(8,128)(2,1)S(1)} %shard_map.111), channel_id=1, source_target_pairs={{0,8},{4,12},{8,0},{12,4},{1,9},{5,13},{9,1},{13,5},{2,10},{6,14},... | collective-permute-start | bytes 884744 | tf_op jit(solution)/shard_map/ppermute | solution.py:303
  83.6 1.3 shard_map.113
  84.9 8.6 %all_to_all.10 = bf16[8,64,128]{2,1,0:T(8,128)(2,1)S(1)} all-to-all(bf16[8,64,128]{2,1,0:T(8,128)(2,1)S(1)} %shard_map.113), channel_id=1, replica_groups=mesh['zl'=4,'y'=4,'c'=2,'x'=4,'zh'=4] {'y','c'}, dimensions={0} | all-to-all | bytes 262144 | tf_op jit(solution)/shard_map/all_to_all | solution.py:317
  93.5 1.9 %collective-permute-start.5 = (bf16[8,4,16,128]{3,2,1,0:T(8,128)(2,1)S(1)}, bf16[8,4,16,128]{3,2,1,0:T(8,128)(2,1)S(1)}, u32[]{:S(2)}, u32[]{:S(2)}) collective-permute-start(bf16[8,4,16,128]{3,2,1,0:T(8,128)(2,1)S(1)} %bitcast.11), channel_id=1, source_target_pairs={{0,128},{128,256},{256,384},{384,0},{1,129},{129,257},{257,385},{3... | collective-permute-start | bytes 393224 | tf_op jit(solution)/shard_map/ppermute | solution.py:319
  95.4 5.7 %collective-permute-start.6 = (bf16[8,4,16,128]{3,2,1,0:T(8,128)(2,1)S(1)}, bf16[8,4,16,128]{3,2,1,0:T(8,128)(2,1)S(1)}, u32[]{:S(2)}, u32[]{:S(2)}) collective-permute-start(bf16[8,4,16,128]{3,2,1,0:T(8,128)(2,1)S(1)} %bitcast.12), channel_id=1, source_target_pairs={{0,384},{128,0},{256,128},{384,256},{1,385},{129,1},{257,129},{385... | collective-permute-start | bytes 393224 | tf_op jit(solution)/shard_map/ppermute | solution.py:319
  101.1 1.9 %collective-permute-start.7 = (bf16[8,4,16,128]{3,2,1,0:T(8,128)(2,1)S(1)}, bf16[8,4,16,128]{3,2,1,0:T(8,128)(2,1)S(1)}, u32[]{:S(2)}, u32[]{:S(2)}) collective-permute-start(bf16[8,4,16,128]{3,2,1,0:T(8,128)(2,1)S(1)} %bitcast.13), channel_id=1, source_target_pairs={{0,256},{128,384},{256,0},{384,128},{1,257},{129,385},{257,1},{385... | collective-permute-start | bytes 393224 | tf_op jit(solution)/shard_map/ppermute | solution.py:319
  103.1 2.6 %shard_map.112 = (bf16[384,128]{1,0:T(8,128)(2,1)S(1)}, f32[384,128]{1,0:T(8,128)S(1)}) custom-call(bf16[1152,384]{1,0:T(8,128)(2,1)S(1)} %get-tuple-element.18.wide_ref.own, bf16[1152,384]{1,0:T(8,128)(2,1)S(1)} %collective-permute-done.1.left, bf16[1152,384]{1,0:T(8,128)(2,1)S(1)} %collective-permute-done.2.right, ...), custom_call_target="tpu_custom_call" | custom-call | tf_op jit(solution)/shard_map/pallas_call | solution.py:321
  105.7 4.9 %collective-permute-done.7.m3 = bf16[8,4,16,128]{3,2,1,0:T(8,128)(2,1)S(1)} collective-permute-done((bf16[8,4,16,128]{3,2,1,0:T(8,128)(2,1)S(1)}, bf16[8,4,16,128]{3,2,1,0:T(8,128)(2,1)S(1)}, u32[]{:S(2)}, u32[]{:S(2)}) %collective-permute-start.7) | collective-permute-done | bytes 131104 | tf_op jit(solution)/shard_map/ppermute | solution.py:319
  110.6 1.0 shard_map.114
  111.7 21.3 %all_to_all.11.parts_ref = bf16[16,16,384]{2,1,0:T(8,128)(2,1)S(1)} all-to-all(bf16[16,16,384]{2,1,0:T(8,128)(2,1)S(1)} %shard_map.114), channel_id=1, replica_groups={{10,11,8,9,14,15,12,13,2,3,0,1,6,7,4,5},{26,27,24,25,30,31,28,29,18,19,..., dimensions={0} | all-to-all | bytes 393216 | tf_op jit(solution)/shard_map/all_to_all | solution.py:345
  133.0 0.6 shard_map.115
  (20 shorter events, 0.1 us)
Async XLA Ops:
  2.4 57.1 %collective-permute-start = (bf16[16,4608]{1,0:T(8,128)(2,1)}, bf16[16,4608]{1,0:T(8,128)(2,1)S(1)}, u32[]{:S(2)}, u32[]{:S(2)}) collective-permute-start(bf16[16,4608]{1,0:T(8,128)(2,1)} %get-tuple-element.16), channel_id=1, source_target_pairs={{387,0},{384,1},{385,2},{386,3},{391,4},{388,5},{389,6},{390,7},{3... | collective-permute-start | bytes 442376 | tf_op jit(solution)/shard_map/ppermute | solution.py:282
  13.8 66.8 %collective-permute-start.3 = (bf16[384,1152]{1,0:T(8,128)(2,1)}, bf16[384,1152]{1,0:T(8,128)(2,1)S(1)}, u32[]{:S(2)}, u32[]{:S(2)}) collective-permute-start(bf16[384,1152]{1,0:T(8,128)(2,1)} %get-tuple-element.19), channel_id=1, source_target_pairs={{0,8},{4,12},{8,0},{12,4},{1,9},{5,13},{9,1},{13,5},{2,10},{6,14},... | collective-permute-start | bytes 2654216 | tf_op jit(solution)/shard_map/ppermute | solution.py:283
  73.4 10.2 %copy-start.2 = (bf16[128,4608]{1,0:T(8,128)(2,1)S(1)}, bf16[128,4608]{1,0:T(8,128)(2,1)}, u32[]{:S(2)}) copy-start(bf16[128,4608]{1,0:T(8,128)(2,1)} %value_ref.1) | copy-start | bytes 3538948
  73.4 27.7 %collective-permute-start.1 = (bf16[1152,384]{1,0:T(8,128)(2,1)S(1)}, bf16[1152,384]{1,0:T(8,128)(2,1)S(1)}, u32[]{:S(2)}, u32[]{:S(2)}) collective-permute-start(bf16[1152,384]{1,0:T(8,128)(2,1)S(1)} %get-tuple-element.18.wide_ref.own), channel_id=1, source_target_pairs={{0,4},{4,8},{8,12},{12,0},{1,5},{5,9},{9,13},{13,1},{2,6},{6,10},{... | collective-permute-start | bytes 2654216 | tf_op jit(solution)/shard_map/ppermute | solution.py:296
  75.5 27.6 %collective-permute-start.2 = (bf16[1152,384]{1,0:T(8,128)(2,1)S(1)}, bf16[1152,384]{1,0:T(8,128)(2,1)S(1)}, u32[]{:S(2)}, u32[]{:S(2)}) collective-permute-start(bf16[1152,384]{1,0:T(8,128)(2,1)S(1)} %get-tuple-element.18.wide_ref.own), channel_id=1, source_target_pairs={{0,12},{4,0},{8,4},{12,8},{1,13},{5,1},{9,5},{13,9},{2,14},{6,2},{... | collective-permute-start | bytes 2654216 | tf_op jit(solution)/shard_map/ppermute | solution.py:297
  80.6 22.5 %copy-start.1 = (bf16[128,4608]{1,0:T(8,128)(2,1)S(1)}, bf16[128,4608]{1,0:T(8,128)(2,1)}, u32[]{:S(2)}) copy-start(bf16[128,4608]{1,0:T(8,128)(2,1)} %decoder.1) | copy-start | bytes 3538948
  81.3 21.8 %copy-start = (bf16[256,4608]{1,0:T(8,128)(2,1)S(1)}, bf16[256,4608]{1,0:T(8,128)(2,1)}, u32[]{:S(2)}) copy-start(bf16[256,4608]{1,0:T(8,128)(2,1)} %out_proj.3) | copy-start | bytes 7077892
  81.3 21.8 %copy-start.3 = (bf16[2,128,128]{2,1,0:T(8,128)(2,1)S(1)}, bf16[2,128,128]{2,1,0:T(8,128)(2,1)}, u32[]{:S(2)}) copy-start(bf16[2,128,128]{2,1,0:T(8,128)(2,1)} %patterns_ref.1) | copy-start | bytes 196612
  81.3 21.8 %copy-start.6 = (f32[128]{0:T(128)S(1)}, f32[128]{0:T(128)}, u32[]{:S(2)}) copy-start(f32[128]{0:T(128)} %param.12) | copy-start | bytes 1540
  81.3 21.8 %collective-permute-start.4 = (bf16[384,384]{1,0:T(8,128)(2,1)S(1)}, bf16[384,384]{1,0:T(8,128)(2,1)S(1)}, u32[]{:S(2)}, u32[]{:S(2)}) collective-permute-start(bf16[384,384]{1,0:T(8,128)(2,1)S(1)} %shard_map.111), channel_id=1, source_target_pairs={{0,8},{4,12},{8,0},{12,4},{1,9},{5,13},{9,1},{13,5},{2,10},{6,14},... | collective-permute-start | bytes 884744 | tf_op jit(solution)/shard_map/ppermute | solution.py:303
  93.5 12.3 %collective-permute-start.5 = (bf16[8,4,16,128]{3,2,1,0:T(8,128)(2,1)S(1)}, bf16[8,4,16,128]{3,2,1,0:T(8,128)(2,1)S(1)}, u32[]{:S(2)}, u32[]{:S(2)}) collective-permute-start(bf16[8,4,16,128]{3,2,1,0:T(8,128)(2,1)S(1)} %bitcast.11), channel_id=1, source_target_pairs={{0,128},{128,256},{256,384},{384,0},{1,129},{129,257},{257,385},{3... | collective-permute-start | bytes 393224 | tf_op jit(solution)/shard_map/ppermute | solution.py:319
  95.4 10.3 %collective-permute-start.6 = (bf16[8,4,16,128]{3,2,1,0:T(8,128)(2,1)S(1)}, bf16[8,4,16,128]{3,2,1,0:T(8,128)(2,1)S(1)}, u32[]{:S(2)}, u32[]{:S(2)}) collective-permute-start(bf16[8,4,16,128]{3,2,1,0:T(8,128)(2,1)S(1)} %bitcast.12), channel_id=1, source_target_pairs={{0,384},{128,0},{256,128},{384,256},{1,385},{129,1},{257,129},{385... | collective-permute-start | bytes 393224 | tf_op jit(solution)/shard_map/ppermute | solution.py:319
  101.1 9.5 %collective-permute-start.7 = (bf16[8,4,16,128]{3,2,1,0:T(8,128)(2,1)S(1)}, bf16[8,4,16,128]{3,2,1,0:T(8,128)(2,1)S(1)}, u32[]{:S(2)}, u32[]{:S(2)}) collective-permute-start(bf16[8,4,16,128]{3,2,1,0:T(8,128)(2,1)S(1)} %bitcast.13), channel_id=1, source_target_pairs={{0,256},{128,384},{256,0},{384,128},{1,257},{129,385},{257,1},{385... | collective-permute-start | bytes 393224 | tf_op jit(solution)/shard_map/ppermute | solution.py:319
  103.1 7.5 %copy-start.5 = (s32[128,2]{0,1:T(2,128)S(1)}, s32[128,2]{0,1:T(2,128)}, u32[]{:S(2)}) copy-start(s32[128,2]{0,1:T(2,128)} %param.20) | copy-start | bytes 3076
  103.1 7.5 %copy-start.7 = (f32[128]{0:T(128)S(1)}, f32[128]{0:T(128)}, u32[]{:S(2)}) copy-start(f32[128]{0:T(128)} %param.17) | copy-start | bytes 1540
  105.7 27.3 %copy-start.4 = (bf16[8,256]{1,0:T(8,128)(2,1)S(1)}, bf16[8,256]{1,0:T(8,128)(2,1)}, u32[]{:S(2)}) copy-start(bf16[8,256]{1,0:T(8,128)(2,1)} %acts_ref.1) | copy-start | bytes 12292

commit v6 on v5

--- a/solution.py
+++ b/solution.py
@@ -21,7 +21,7 @@
 
 
 def source_block(zh, zl, n):
-    return (zh + (n - 1, n - 2, 0, 1)[zl]) % n
+    return (zh + (n - 1, 0, 2, 1)[zl]) % n
 
 
 def decoder_moves(sizes):
@@ -197,7 +197,7 @@
     for turn, folded_ref in zip(TURNS, (m0, m1, m2, m3)):
         other = lax.rem(zl + 4 - turn, 4)
         shift = jnp.where(
-            other == 0, nzh - 1, jnp.where(other == 1, nzh - 2, jnp.where(other == 2, 0, 1))
+            other == 0, nzh - 1, jnp.where(other == 1, 0, jnp.where(other == 2, 2, 1))
         )
         block = lax.rem(zh + shift, nzh)
         for x in range(nx):

time: 136 us -> 135 us (level)
  no operation moved by 1% of the time
where the time goes in v6:
time: 135 us; the launch traced here: 133 us
  blocking collectives  83.4 us (62%)
  starting transfers between devices  35.3 us (26%)
  Pallas kernels  8.67 us (6%)
  waiting for transfers between devices  4.9 us (4%)
    all_gather x1, blocking collectives, shards(): columns = lax.all_gather(packed, 'zh', axis=0, tiled=False)  39.8 us
    all_to_all x1, blocking collectives, shards(): parts = lax.all_to_all(parts, TP, 0, 0, axis_index_groups=[group])  21.4 us
    all_gather x1, blocking collectives, shards(): lax.all_gather(jnp.concatenate([near, tail], axis=1), 'x', axis=0, tiled=...  13.7 us
    ppermute x1, starting transfers between devices, shards(): near = lax.ppermute(near, AXES, decoder_moves(sizes))  11.4 us
    ppermute x3, starting transfers between devices, shards(): lax.ppermute(folded, 'zl', ring(nzl, k))  9.55 us
    all_to_all x1, blocking collectives, shards(): folded = lax.all_to_all(folded, ('y', 'c'), 0, 0)  8.56 us
    ppermute x1, starting transfers between devices, shards(): right = lax.ppermute(wide, 'x', ring(nx, nx - 1))  4.97 us
    ppermute x1, starting transfers between devices, shards(): weights = lax.ppermute(weights, 'x', ring(nx, 2))  4.93 us
  transfers between devices with their start and end apart: 8, of which 1 were waited for; matrix products, arithmetic and copies ran while one was open for 0% of the time, Pallas kernels for 3%

profile of v6, /device:TPU:24, one launch (start us, length us, event | category | flops | bytes accessed | tf_op | source)
XLA Modules:
  0.0 132.7 jit_solution(9361104278459461865)
XLA Ops:
  0.0 2.4 %shard_map.109 = (bf16[304,384]{1,0:T(8,128)(2,1)}, bf16[384,1152]{1,0:T(8,128)(2,1)}, bf16[16,4608]{1,0:T(8,128)(2,1)}) custom-call(bf16[3,288,128]{2,1,0:T(8,128)(2,1)} %bitcast.18, bf16[256,4608]{1,0:T(8,128)(2,1)} %out_proj.3, bf16[128,4608]{1,0:T(8,128)(2,1)} %decoder.1, bf16[288]{0:T(512)(128)(2,1)} %post.1, bf16[288]{0:T(512)(128)(2,1)} %pre.1), custom_call_target="tpu_custom_call" | custom-call | tf_op jit(solution)/shard_map/pallas_call | solution.py:267
  2.4 11.4 %collective-permute-start = (bf16[16,4608]{1,0:T(8,128)(2,1)}, bf16[16,4608]{1,0:T(8,128)(2,1)S(1)}, u32[]{:S(2)}, u32[]{:S(2)}) collective-permute-start(bf16[16,4608]{1,0:T(8,128)(2,1)} %get-tuple-element.16), channel_id=1, source_target_pairs={{387,0},{384,1},{385,2},{386,3},{391,4},{388,5},{389,6},{390,7},{3... | collective-permute-start | bytes 442376 | tf_op jit(solution)/shard_map/ppermute | solution.py:282
  13.8 4.9 %collective-permute-start.3 = (bf16[384,1152]{1,0:T(8,128)(2,1)}, bf16[384,1152]{1,0:T(8,128)(2,1)S(1)}, u32[]{:S(2)}, u32[]{:S(2)}) collective-permute-start(bf16[384,1152]{1,0:T(8,128)(2,1)} %get-tuple-element.19), channel_id=1, source_target_pairs={{0,8},{4,12},{8,0},{12,4},{1,9},{5,13},{9,1},{13,5},{2,10},{6,14},... | collective-permute-start | bytes 2654216 | tf_op jit(solution)/shard_map/ppermute | solution.py:283
  18.8 39.8 %all-gather = bf16[1216,384]{1,0:T(8,128)(2,1)S(1)} all-gather(bf16[304,384]{1,0:T(8,128)(2,1)} %get-tuple-element.14), channel_id=2, replica_groups=mesh['zl'=4,'y'=4,'c'=2,'x'=4,'zh'=4] {'zh'}, dimensions={0}, use_global_device_ids=true | all-gather | bytes 1167360 | tf_op jit(solution)/shard_map/all_gather | solution.py:284
  58.6 0.1 shard_map.110
  58.7 13.7 %all-gather.1 = bf16[64,4992]{1,0:T(8,128)(2,1)S(1)} all-gather(bf16[16,4992]{1,0:T(8,128)(2,1)S(1)} %pad_maximum_fusion), channel_id=3, replica_groups=mesh['zl'=4,'y'=4,'c'=2,'x'=4,'zh'=4] {'x'}, dimensions={0}, use_global_device_ids=true | all-gather | bytes 798720 | tf_op jit(solution)/shard_map/all_gather | solution.py:294
  72.4 2.2 %collective-permute-start.1 = (bf16[1152,384]{1,0:T(8,128)(2,1)S(1)}, bf16[1152,384]{1,0:T(8,128)(2,1)S(1)}, u32[]{:S(2)}, u32[]{:S(2)}) collective-permute-start(bf16[1152,384]{1,0:T(8,128)(2,1)S(1)} %get-tuple-element.18.wide_ref.own), channel_id=1, source_target_pairs={{0,4},{4,8},{8,12},{12,0},{1,5},{5,9},{9,13},{13,1},{2,6},{6,10},{... | collective-permute-start | bytes 2654216 | tf_op jit(solution)/shard_map/ppermute | solution.py:296
  74.6 5.0 %collective-permute-start.2 = (bf16[1152,384]{1,0:T(8,128)(2,1)S(1)}, bf16[1152,384]{1,0:T(8,128)(2,1)S(1)}, u32[]{:S(2)}, u32[]{:S(2)}) collective-permute-start(bf16[1152,384]{1,0:T(8,128)(2,1)S(1)} %get-tuple-element.18.wide_ref.own), channel_id=1, source_target_pairs={{0,12},{4,0},{8,4},{12,8},{1,13},{5,1},{9,5},{13,9},{2,14},{6,2},{... | collective-permute-start | bytes 2654216 | tf_op jit(solution)/shard_map/ppermute | solution.py:297
  79.6 0.0 copy-start.1
  79.6 0.6 shard_map.111
  80.3 0.0 copy-start.6
  80.3 2.3 %collective-permute-start.4 = (bf16[384,384]{1,0:T(8,128)(2,1)S(1)}, bf16[384,384]{1,0:T(8,128)(2,1)S(1)}, u32[]{:S(2)}, u32[]{:S(2)}) collective-permute-start(bf16[384,384]{1,0:T(8,128)(2,1)S(1)} %shard_map.111), channel_id=1, source_target_pairs={{0,8},{4,12},{8,0},{12,4},{1,9},{5,13},{9,1},{13,5},{2,10},{6,14},... | collective-permute-start | bytes 884744 | tf_op jit(solution)/shard_map/ppermute | solution.py:303
  82.6 1.3 shard_map.113
  83.9 8.6 %all_to_all.10 = bf16[8,64,128]{2,1,0:T(8,128)(2,1)S(1)} all-to-all(bf16[8,64,128]{2,1,0:T(8,128)(2,1)S(1)} %shard_map.113), channel_id=1, replica_groups=mesh['zl'=4,'y'=4,'c'=2,'x'=4,'zh'=4] {'y','c'}, dimensions={0} | all-to-all | bytes 262144 | tf_op jit(solution)/shard_map/all_to_all | solution.py:317
  92.5 2.9 %collective-permute-start.5 = (bf16[8,4,16,128]{3,2,1,0:T(8,128)(2,1)S(1)}, bf16[8,4,16,128]{3,2,1,0:T(8,128)(2,1)S(1)}, u32[]{:S(2)}, u32[]{:S(2)}) collective-permute-start(bf16[8,4,16,128]{3,2,1,0:T(8,128)(2,1)S(1)} %bitcast.11), channel_id=1, source_target_pairs={{0,128},{128,256},{256,384},{384,0},{1,129},{129,257},{257,385},{3... | collective-permute-start | bytes 393224 | tf_op jit(solution)/shard_map/ppermute | solution.py:319
  95.4 4.7 %collective-permute-start.6 = (bf16[8,4,16,128]{3,2,1,0:T(8,128)(2,1)S(1)}, bf16[8,4,16,128]{3,2,1,0:T(8,128)(2,1)S(1)}, u32[]{:S(2)}, u32[]{:S(2)}) collective-permute-start(bf16[8,4,16,128]{3,2,1,0:T(8,128)(2,1)S(1)} %bitcast.12), channel_id=1, source_target_pairs={{0,384},{128,0},{256,128},{384,256},{1,385},{129,1},{257,129},{385... | collective-permute-start | bytes 393224 | tf_op jit(solution)/shard_map/ppermute | solution.py:319
  100.1 1.9 %collective-permute-start.7 = (bf16[8,4,16,128]{3,2,1,0:T(8,128)(2,1)S(1)}, bf16[8,4,16,128]{3,2,1,0:T(8,128)(2,1)S(1)}, u32[]{:S(2)}, u32[]{:S(2)}) collective-permute-start(bf16[8,4,16,128]{3,2,1,0:T(8,128)(2,1)S(1)} %bitcast.13), channel_id=1, source_target_pairs={{0,256},{128,384},{256,0},{384,128},{1,257},{129,385},{257,1},{385... | collective-permute-start | bytes 393224 | tf_op jit(solution)/shard_map/ppermute | solution.py:319
  102.1 0.0 copy-start.5
  102.1 0.0 copy-start.7
  102.1 2.6 %shard_map.112 = (bf16[384,128]{1,0:T(8,128)(2,1)S(1)}, f32[384,128]{1,0:T(8,128)S(1)}) custom-call(bf16[1152,384]{1,0:T(8,128)(2,1)S(1)} %get-tuple-element.18.wide_ref.own, bf16[1152,384]{1,0:T(8,128)(2,1)S(1)} %collective-permute-done.1.left, bf16[1152,384]{1,0:T(8,128)(2,1)S(1)} %collective-permute-done.2.right, ...), custom_call_target="tpu_custom_call" | custom-call | tf_op jit(solution)/shard_map/pallas_call | solution.py:321
  104.7 4.9 %collective-permute-done.7.m3 = bf16[8,4,16,128]{3,2,1,0:T(8,128)(2,1)S(1)} collective-permute-done((bf16[8,4,16,128]{3,2,1,0:T(8,128)(2,1)S(1)}, bf16[8,4,16,128]{3,2,1,0:T(8,128)(2,1)S(1)}, u32[]{:S(2)}, u32[]{:S(2)}) %collective-permute-start.7) | collective-permute-done | bytes 131104 | tf_op jit(solution)/shard_map/ppermute | solution.py:319
  109.6 1.0 shard_map.114
  110.7 21.4 %all_to_all.11.parts_ref = bf16[16,16,384]{2,1,0:T(8,128)(2,1)S(1)} all-to-all(bf16[16,16,384]{2,1,0:T(8,128)(2,1)S(1)} %shard_map.114), channel_id=1, replica_groups={{10,11,8,9,14,15,12,13,2,3,0,1,6,7,4,5},{26,27,24,25,30,31,28,29,18,19,..., dimensions={0} | all-to-all | bytes 393216 | tf_op jit(solution)/shard_map/all_to_all | solution.py:345
  132.0 0.6 shard_map.115
  (20 shorter events, 0.1 us)
Async XLA Ops:
  2.4 56.2 %collective-permute-start = (bf16[16,4608]{1,0:T(8,128)(2,1)}, bf16[16,4608]{1,0:T(8,128)(2,1)S(1)}, u32[]{:S(2)}, u32[]{:S(2)}) collective-permute-start(bf16[16,4608]{1,0:T(8,128)(2,1)} %get-tuple-element.16), channel_id=1, source_target_pairs={{387,0},{384,1},{385,2},{386,3},{391,4},{388,5},{389,6},{390,7},{3... | collective-permute-start | bytes 442376 | tf_op jit(solution)/shard_map/ppermute | solution.py:282
  13.8 65.8 %collective-permute-start.3 = (bf16[384,1152]{1,0:T(8,128)(2,1)}, bf16[384,1152]{1,0:T(8,128)(2,1)S(1)}, u32[]{:S(2)}, u32[]{:S(2)}) collective-permute-start(bf16[384,1152]{1,0:T(8,128)(2,1)} %get-tuple-element.19), channel_id=1, source_target_pairs={{0,8},{4,12},{8,0},{12,4},{1,9},{5,13},{9,1},{13,5},{2,10},{6,14},... | collective-permute-start | bytes 2654216 | tf_op jit(solution)/shard_map/ppermute | solution.py:283
  72.4 10.2 %copy-start.2 = (bf16[128,4608]{1,0:T(8,128)(2,1)S(1)}, bf16[128,4608]{1,0:T(8,128)(2,1)}, u32[]{:S(2)}) copy-start(bf16[128,4608]{1,0:T(8,128)(2,1)} %value_ref.1) | copy-start | bytes 3538948
  72.4 27.7 %collective-permute-start.1 = (bf16[1152,384]{1,0:T(8,128)(2,1)S(1)}, bf16[1152,384]{1,0:T(8,128)(2,1)S(1)}, u32[]{:S(2)}, u32[]{:S(2)}) collective-permute-start(bf16[1152,384]{1,0:T(8,128)(2,1)S(1)} %get-tuple-element.18.wide_ref.own), channel_id=1, source_target_pairs={{0,4},{4,8},{8,12},{12,0},{1,5},{5,9},{9,13},{13,1},{2,6},{6,10},{... | collective-permute-start | bytes 2654216 | tf_op jit(solution)/shard_map/ppermute | solution.py:296
  74.6 27.4 %collective-permute-start.2 = (bf16[1152,384]{1,0:T(8,128)(2,1)S(1)}, bf16[1152,384]{1,0:T(8,128)(2,1)S(1)}, u32[]{:S(2)}, u32[]{:S(2)}) collective-permute-start(bf16[1152,384]{1,0:T(8,128)(2,1)S(1)} %get-tuple-element.18.wide_ref.own), channel_id=1, source_target_pairs={{0,12},{4,0},{8,4},{12,8},{1,13},{5,1},{9,5},{13,9},{2,14},{6,2},{... | collective-permute-start | bytes 2654216 | tf_op jit(solution)/shard_map/ppermute | solution.py:297
  79.6 22.5 %copy-start.1 = (bf16[128,4608]{1,0:T(8,128)(2,1)S(1)}, bf16[128,4608]{1,0:T(8,128)(2,1)}, u32[]{:S(2)}) copy-start(bf16[128,4608]{1,0:T(8,128)(2,1)} %decoder.1) | copy-start | bytes 3538948
  80.3 21.8 %copy-start = (bf16[256,4608]{1,0:T(8,128)(2,1)S(1)}, bf16[256,4608]{1,0:T(8,128)(2,1)}, u32[]{:S(2)}) copy-start(bf16[256,4608]{1,0:T(8,128)(2,1)} %out_proj.3) | copy-start | bytes 7077892
  80.3 21.8 %copy-start.3 = (bf16[2,128,128]{2,1,0:T(8,128)(2,1)S(1)}, bf16[2,128,128]{2,1,0:T(8,128)(2,1)}, u32[]{:S(2)}) copy-start(bf16[2,128,128]{2,1,0:T(8,128)(2,1)} %patterns_ref.1) | copy-start | bytes 196612
  80.3 21.8 %copy-start.6 = (f32[128]{0:T(128)S(1)}, f32[128]{0:T(128)}, u32[]{:S(2)}) copy-start(f32[128]{0:T(128)} %param.12) | copy-start | bytes 1540
  80.3 21.8 %collective-permute-start.4 = (bf16[384,384]{1,0:T(8,128)(2,1)S(1)}, bf16[384,384]{1,0:T(8,128)(2,1)S(1)}, u32[]{:S(2)}, u32[]{:S(2)}) collective-permute-start(bf16[384,384]{1,0:T(8,128)(2,1)S(1)} %shard_map.111), channel_id=1, source_target_pairs={{0,8},{4,12},{8,0},{12,4},{1,9},{5,13},{9,1},{13,5},{2,10},{6,14},... | collective-permute-start | bytes 884744 | tf_op jit(solution)/shard_map/ppermute | solution.py:303
  92.5 12.2 %collective-permute-start.5 = (bf16[8,4,16,128]{3,2,1,0:T(8,128)(2,1)S(1)}, bf16[8,4,16,128]{3,2,1,0:T(8,128)(2,1)S(1)}, u32[]{:S(2)}, u32[]{:S(2)}) collective-permute-start(bf16[8,4,16,128]{3,2,1,0:T(8,128)(2,1)S(1)} %bitcast.11), channel_id=1, source_target_pairs={{0,128},{128,256},{256,384},{384,0},{1,129},{129,257},{257,385},{3... | collective-permute-start | bytes 393224 | tf_op jit(solution)/shard_map/ppermute | solution.py:319
  95.4 9.3 %collective-permute-start.6 = (bf16[8,4,16,128]{3,2,1,0:T(8,128)(2,1)S(1)}, bf16[8,4,16,128]{3,2,1,0:T(8,128)(2,1)S(1)}, u32[]{:S(2)}, u32[]{:S(2)}) collective-permute-start(bf16[8,4,16,128]{3,2,1,0:T(8,128)(2,1)S(1)} %bitcast.12), channel_id=1, source_target_pairs={{0,384},{128,0},{256,128},{384,256},{1,385},{129,1},{257,129},{385... | collective-permute-start | bytes 393224 | tf_op jit(solution)/shard_map/ppermute | solution.py:319
  100.1 9.5 %collective-permute-start.7 = (bf16[8,4,16,128]{3,2,1,0:T(8,128)(2,1)S(1)}, bf16[8,4,16,128]{3,2,1,0:T(8,128)(2,1)S(1)}, u32[]{:S(2)}, u32[]{:S(2)}) collective-permute-start(bf16[8,4,16,128]{3,2,1,0:T(8,128)(2,1)S(1)} %bitcast.13), channel_id=1, source_target_pairs={{0,256},{128,384},{256,0},{384,128},{1,257},{129,385},{257,1},{385... | collective-permute-start | bytes 393224 | tf_op jit(solution)/shard_map/ppermute | solution.py:319
  102.1 7.5 %copy-start.5 = (s32[128,2]{0,1:T(2,128)S(1)}, s32[128,2]{0,1:T(2,128)}, u32[]{:S(2)}) copy-start(s32[128,2]{0,1:T(2,128)} %param.20) | copy-start | bytes 3076
  102.1 7.5 %copy-start.7 = (f32[128]{0:T(128)S(1)}, f32[128]{0:T(128)}, u32[]{:S(2)}) copy-start(f32[128]{0:T(128)} %param.17) | copy-start | bytes 1540
  104.7 27.3 %copy-start.4 = (bf16[8,256]{1,0:T(8,128)(2,1)S(1)}, bf16[8,256]{1,0:T(8,128)(2,1)}, u32[]{:S(2)}) copy-start(bf16[8,256]{1,0:T(8,128)(2,1)} %acts_ref.1) | copy-start | bytes 12292

commit v7 on v6

--- a/solution.py
+++ b/solution.py
@@ -58,7 +58,7 @@
         pltpu.make_async_copy(out_proj.at[:, cols], far_ref.at[pl.ds(0, height), :], sems.at[2]),
         pltpu.make_async_copy(dec.at[:, cols], far_ref.at[pl.ds(height, BLK), :], sems.at[3]),
     ]
-    rows = pl.ds(pl.multiple_of(lax.axis_index(("y", "c")) * share, share), share)
+    rows = pl.ds(pl.multiple_of(lax.axis_index(("c", "y")) * share, share), share)
     copies.append(pltpu.make_async_copy(dec.at[rows, :], near_ref, sems.at[4 + targets]))
     for r in range(targets):
         place = out_ref.at[pl.ds(0, local), pl.ds(r * seq, seq)]
@@ -295,12 +295,6 @@
     wide, near = lax.optimization_barrier((wide, near))
     left = lax.ppermute(wide, "x", ring(nx, 1))
     right = lax.ppermute(wide, "x", ring(nx, nx - 1))
-    far = pl.pallas_call(
-        functools.partial(far_kernel, heads * head),
-        out_shape=jax.ShapeDtypeStruct((heads * head + BLK, rows), BF16),
-        compiler_params=PARAMS,
-    )(wide, weights, gains)
-    far = lax.ppermute(far, "x", ring(nx, 2))
     folded = pl.pallas_call(
         fold_kernel,
         grid=(nx,),
@@ -314,7 +308,14 @@
         scratch_shapes=[pltpu.VMEM((nx * share, head), F32)],
         compiler_params=PARAMS,
     )(near, near, value_proj)
-    folded = lax.all_to_all(folded, ("y", "c"), 0, 0)
+    wide, folded = lax.optimization_barrier((wide, folded))
+    folded = lax.all_to_all(folded, ("c", "y"), 0, 0)
+    far = pl.pallas_call(
+        functools.partial(far_kernel, heads * head),
+        out_shape=jax.ShapeDtypeStruct((heads * head + BLK, rows), BF16),
+        compiler_params=PARAMS,
+    )(wide, weights, gains)
+    far = lax.ppermute(far, "x", ring(nx, 2))
     folded = folded.reshape(copies, nx, share, head)
     foldeds = [folded if k == 0 else lax.ppermute(folded, "zl", ring(nzl, k)) for k in TURNS]
 

time: 135 us -> 135 us (level)
  no operation moved by 1% of the time
where the time goes in v7:
time: 135 us; the launch traced here: 133 us
  blocking collectives  83.6 us (62%)
  starting transfers between devices  35.1 us (26%)
  Pallas kernels  8.68 us (6%)
  waiting for transfers between devices  4.9 us (4%)
    all_gather x1, blocking collectives, shards(): columns = lax.all_gather(packed, 'zh', axis=0, tiled=False)  39.8 us
    all_to_all x1, blocking collectives, shards(): parts = lax.all_to_all(parts, TP, 0, 0, axis_index_groups=[group])  21.4 us
    all_gather x1, blocking collectives, shards(): lax.all_gather(jnp.concatenate([near, tail], axis=1), 'x', axis=0, tiled=...  13.9 us
    ppermute x1, starting transfers between devices, shards(): near = lax.ppermute(near, AXES, decoder_moves(sizes))  11.4 us
    ppermute x3, starting transfers between devices, shards(): lax.ppermute(folded, 'zl', ring(nzl, k))  9.55 us
    all_to_all x1, blocking collectives, shards(): folded = lax.all_to_all(folded, ('c', 'y'), 0, 0)  8.56 us
    ppermute x1, starting transfers between devices, shards(): right = lax.ppermute(wide, 'x', ring(nx, nx - 1))  4.97 us
    ppermute x1, starting transfers between devices, shards(): weights = lax.ppermute(weights, 'x', ring(nx, 2))  4.93 us
  transfers between devices with their start and end apart: 8, of which 1 were waited for; matrix products, arithmetic and copies ran while one was open for 0% of the time, Pallas kernels for 3%

profile of v7, /device:TPU:24, one launch (start us, length us, event | category | flops | bytes accessed | tf_op | source)
XLA Modules:
  0.0 132.6 jit_solution(12291977271535207427)
XLA Ops:
  0.0 2.4 %shard_map.109 = (bf16[304,384]{1,0:T(8,128)(2,1)}, bf16[384,1152]{1,0:T(8,128)(2,1)}, bf16[16,4608]{1,0:T(8,128)(2,1)}) custom-call(bf16[3,288,128]{2,1,0:T(8,128)(2,1)} %bitcast.18, bf16[256,4608]{1,0:T(8,128)(2,1)} %out_proj.3, bf16[128,4608]{1,0:T(8,128)(2,1)} %decoder.1, bf16[288]{0:T(512)(128)(2,1)} %post.1, bf16[288]{0:T(512)(128)(2,1)} %pre.1), custom_call_target="tpu_custom_call" | custom-call | tf_op jit(solution)/shard_map/pallas_call | solution.py:267
  2.4 11.4 %collective-permute-start = (bf16[16,4608]{1,0:T(8,128)(2,1)}, bf16[16,4608]{1,0:T(8,128)(2,1)S(1)}, u32[]{:S(2)}, u32[]{:S(2)}) collective-permute-start(bf16[16,4608]{1,0:T(8,128)(2,1)} %get-tuple-element.18), channel_id=1, source_target_pairs={{387,0},{384,1},{385,2},{386,3},{391,4},{388,5},{389,6},{390,7},{3... | collective-permute-start | bytes 442376 | tf_op jit(solution)/shard_map/ppermute | solution.py:282
  13.8 4.9 %collective-permute-start.3 = (bf16[384,1152]{1,0:T(8,128)(2,1)}, bf16[384,1152]{1,0:T(8,128)(2,1)S(1)}, u32[]{:S(2)}, u32[]{:S(2)}) collective-permute-start(bf16[384,1152]{1,0:T(8,128)(2,1)} %get-tuple-element.23), channel_id=1, source_target_pairs={{0,8},{4,12},{8,0},{12,4},{1,9},{5,13},{9,1},{13,5},{2,10},{6,14},... | collective-permute-start | bytes 2654216 | tf_op jit(solution)/shard_map/ppermute | solution.py:283
  18.8 39.8 %all-gather = bf16[1216,384]{1,0:T(8,128)(2,1)S(1)} all-gather(bf16[304,384]{1,0:T(8,128)(2,1)} %get-tuple-element.16), channel_id=2, replica_groups=mesh['zl'=4,'y'=4,'c'=2,'x'=4,'zh'=4] {'zh'}, dimensions={0}, use_global_device_ids=true | all-gather | bytes 1167360 | tf_op jit(solution)/shard_map/all_gather | solution.py:284
  58.6 0.1 shard_map.110
  58.7 13.9 %all-gather.1 = bf16[64,4992]{1,0:T(8,128)(2,1)S(1)} all-gather(bf16[16,4992]{1,0:T(8,128)(2,1)S(1)} %pad_maximum_fusion), channel_id=3, replica_groups=mesh['zl'=4,'y'=4,'c'=2,'x'=4,'zh'=4] {'x'}, dimensions={0}, use_global_device_ids=true | all-gather | bytes 798720 | tf_op jit(solution)/shard_map/all_gather | solution.py:294
  72.5 2.1 %collective-permute-start.1 = (bf16[1152,384]{1,0:T(8,128)(2,1)S(1)}, bf16[1152,384]{1,0:T(8,128)(2,1)S(1)}, u32[]{:S(2)}, u32[]{:S(2)}) collective-permute-start(bf16[1152,384]{1,0:T(8,128)(2,1)S(1)} %get-tuple-element.22.wide_ref.own), channel_id=1, source_target_pairs={{0,4},{4,8},{8,12},{12,0},{1,5},{5,9},{9,13},{13,1},{2,6},{6,10},{... | collective-permute-start | bytes 2654216 | tf_op jit(solution)/shard_map/ppermute | solution.py:296
  74.6 5.0 %collective-permute-start.2 = (bf16[1152,384]{1,0:T(8,128)(2,1)S(1)}, bf16[1152,384]{1,0:T(8,128)(2,1)S(1)}, u32[]{:S(2)}, u32[]{:S(2)}) collective-permute-start(bf16[1152,384]{1,0:T(8,128)(2,1)S(1)} %get-tuple-element.22.wide_ref.own), channel_id=1, source_target_pairs={{0,12},{4,0},{8,4},{12,8},{1,13},{5,1},{9,5},{13,9},{2,14},{6,2},{... | collective-permute-start | bytes 2654216 | tf_op jit(solution)/shard_map/ppermute | solution.py:297
  79.6 1.3 shard_map.111
  80.9 0.0 copy-start.1
  80.9 0.0 copy-start.3
  81.0 0.6 shard_map.112
  81.6 2.2 %collective-permute-start.4 = (bf16[384,384]{1,0:T(8,128)(2,1)S(1)}, bf16[384,384]{1,0:T(8,128)(2,1)S(1)}, u32[]{:S(2)}, u32[]{:S(2)}) collective-permute-start(bf16[384,384]{1,0:T(8,128)(2,1)S(1)} %shard_map.112), channel_id=1, source_target_pairs={{0,8},{4,12},{8,0},{12,4},{1,9},{5,13},{9,1},{13,5},{2,10},{6,14},... | collective-permute-start | bytes 884744 | tf_op jit(solution)/shard_map/ppermute | solution.py:318
  83.8 8.6 %all_to_all.10 = bf16[8,64,128]{2,1,0:T(8,128)(2,1)S(1)} all-to-all(bf16[8,64,128]{2,1,0:T(8,128)(2,1)S(1)} %shard_map.111), channel_id=1, replica_groups=mesh['zl'=4,'y'=4,'c'=2,'x'=4,'zh'=4] {'c','y'}, dimensions={0} | all-to-all | bytes 262144 | tf_op jit(solution)/shard_map/all_to_all | solution.py:312
  92.3 2.9 %collective-permute-start.5 = (bf16[8,4,16,128]{3,2,1,0:T(8,128)(2,1)S(1)}, bf16[8,4,16,128]{3,2,1,0:T(8,128)(2,1)S(1)}, u32[]{:S(2)}, u32[]{:S(2)}) collective-permute-start(bf16[8,4,16,128]{3,2,1,0:T(8,128)(2,1)S(1)} %bitcast.11), channel_id=1, source_target_pairs={{0,128},{128,256},{256,384},{384,0},{1,129},{129,257},{257,385},{3... | collective-permute-start | bytes 393224 | tf_op jit(solution)/shard_map/ppermute | solution.py:320
  95.3 4.7 %collective-permute-start.6 = (bf16[8,4,16,128]{3,2,1,0:T(8,128)(2,1)S(1)}, bf16[8,4,16,128]{3,2,1,0:T(8,128)(2,1)S(1)}, u32[]{:S(2)}, u32[]{:S(2)}) collective-permute-start(bf16[8,4,16,128]{3,2,1,0:T(8,128)(2,1)S(1)} %bitcast.12), channel_id=1, source_target_pairs={{0,384},{128,0},{256,128},{384,256},{1,385},{129,1},{257,129},{385... | collective-permute-start | bytes 393224 | tf_op jit(solution)/shard_map/ppermute | solution.py:320
  100.0 1.9 %collective-permute-start.7 = (bf16[8,4,16,128]{3,2,1,0:T(8,128)(2,1)S(1)}, bf16[8,4,16,128]{3,2,1,0:T(8,128)(2,1)S(1)}, u32[]{:S(2)}, u32[]{:S(2)}) collective-permute-start(bf16[8,4,16,128]{3,2,1,0:T(8,128)(2,1)S(1)} %bitcast.13), channel_id=1, source_target_pairs={{0,256},{128,384},{256,0},{384,128},{1,257},{129,385},{257,1},{385... | collective-permute-start | bytes 393224 | tf_op jit(solution)/shard_map/ppermute | solution.py:320
  102.0 0.0 copy-start.5
  102.0 0.0 copy-start.7
  102.0 2.6 %shard_map.113 = (bf16[384,128]{1,0:T(8,128)(2,1)S(1)}, f32[384,128]{1,0:T(8,128)S(1)}) custom-call(bf16[1152,384]{1,0:T(8,128)(2,1)S(1)} %get-tuple-element.22.wide_ref.own, bf16[1152,384]{1,0:T(8,128)(2,1)S(1)} %collective-permute-done.1.left, bf16[1152,384]{1,0:T(8,128)(2,1)S(1)} %collective-permute-done.2.right, ...), custom_call_target="tpu_custom_call" | custom-call | tf_op jit(solution)/shard_map/pallas_call | solution.py:322
  104.6 4.9 %collective-permute-done.7.m3 = bf16[8,4,16,128]{3,2,1,0:T(8,128)(2,1)S(1)} collective-permute-done((bf16[8,4,16,128]{3,2,1,0:T(8,128)(2,1)S(1)}, bf16[8,4,16,128]{3,2,1,0:T(8,128)(2,1)S(1)}, u32[]{:S(2)}, u32[]{:S(2)}) %collective-permute-start.7) | collective-permute-done | bytes 131104 | tf_op jit(solution)/shard_map/ppermute | solution.py:320
  109.5 1.0 shard_map.114
  110.5 21.4 %all_to_all.11.parts_ref = bf16[16,16,384]{2,1,0:T(8,128)(2,1)S(1)} all-to-all(bf16[16,16,384]{2,1,0:T(8,128)(2,1)S(1)} %shard_map.114), channel_id=1, replica_groups={{10,11,8,9,14,15,12,13,2,3,0,1,6,7,4,5},{26,27,24,25,30,31,28,29,18,19,..., dimensions={0} | all-to-all | bytes 393216 | tf_op jit(solution)/shard_map/all_to_all | solution.py:346
  131.9 0.6 shard_map.115
  (20 shorter events, 0.1 us)
Async XLA Ops:
  2.4 56.2 %collective-permute-start = (bf16[16,4608]{1,0:T(8,128)(2,1)}, bf16[16,4608]{1,0:T(8,128)(2,1)S(1)}, u32[]{:S(2)}, u32[]{:S(2)}) collective-permute-start(bf16[16,4608]{1,0:T(8,128)(2,1)} %get-tuple-element.18), channel_id=1, source_target_pairs={{387,0},{384,1},{385,2},{386,3},{391,4},{388,5},{389,6},{390,7},{3... | collective-permute-start | bytes 442376 | tf_op jit(solution)/shard_map/ppermute | solution.py:282
  13.8 67.1 %collective-permute-start.3 = (bf16[384,1152]{1,0:T(8,128)(2,1)}, bf16[384,1152]{1,0:T(8,128)(2,1)S(1)}, u32[]{:S(2)}, u32[]{:S(2)}) collective-permute-start(bf16[384,1152]{1,0:T(8,128)(2,1)} %get-tuple-element.23), channel_id=1, source_target_pairs={{0,8},{4,12},{8,0},{12,4},{1,9},{5,13},{9,1},{13,5},{2,10},{6,14},... | collective-permute-start | bytes 2654216 | tf_op jit(solution)/shard_map/ppermute | solution.py:283
  58.6 21.0 %copy-start.2 = (bf16[128,4608]{1,0:T(8,128)(2,1)S(1)}, bf16[128,4608]{1,0:T(8,128)(2,1)}, u32[]{:S(2)}) copy-start(bf16[128,4608]{1,0:T(8,128)(2,1)} %value_ref.1) | copy-start | bytes 3538948
  72.5 27.5 %collective-permute-start.1 = (bf16[1152,384]{1,0:T(8,128)(2,1)S(1)}, bf16[1152,384]{1,0:T(8,128)(2,1)S(1)}, u32[]{:S(2)}, u32[]{:S(2)}) collective-permute-start(bf16[1152,384]{1,0:T(8,128)(2,1)S(1)} %get-tuple-element.22.wide_ref.own), channel_id=1, source_target_pairs={{0,4},{4,8},{8,12},{12,0},{1,5},{5,9},{9,13},{13,1},{2,6},{6,10},{... | collective-permute-start | bytes 2654216 | tf_op jit(solution)/shard_map/ppermute | solution.py:296
  74.6 27.3 %collective-permute-start.2 = (bf16[1152,384]{1,0:T(8,128)(2,1)S(1)}, bf16[1152,384]{1,0:T(8,128)(2,1)S(1)}, u32[]{:S(2)}, u32[]{:S(2)}) collective-permute-start(bf16[1152,384]{1,0:T(8,128)(2,1)S(1)} %get-tuple-element.22.wide_ref.own), channel_id=1, source_target_pairs={{0,12},{4,0},{8,4},{12,8},{1,13},{5,1},{9,5},{13,9},{2,14},{6,2},{... | collective-permute-start | bytes 2654216 | tf_op jit(solution)/shard_map/ppermute | solution.py:297
  79.6 22.3 %copy-start = (bf16[256,4608]{1,0:T(8,128)(2,1)S(1)}, bf16[256,4608]{1,0:T(8,128)(2,1)}, u32[]{:S(2)}) copy-start(bf16[256,4608]{1,0:T(8,128)(2,1)} %out_proj.3) | copy-start | bytes 7077892
  80.9 21.0 %copy-start.1 = (bf16[128,4608]{1,0:T(8,128)(2,1)S(1)}, bf16[128,4608]{1,0:T(8,128)(2,1)}, u32[]{:S(2)}) copy-start(bf16[128,4608]{1,0:T(8,128)(2,1)} %decoder.1) | copy-start | bytes 3538948
  80.9 21.0 %copy-start.3 = (bf16[2,128,128]{2,1,0:T(8,128)(2,1)S(1)}, bf16[2,128,128]{2,1,0:T(8,128)(2,1)}, u32[]{:S(2)}) copy-start(bf16[2,128,128]{2,1,0:T(8,128)(2,1)} %patterns_ref.1) | copy-start | bytes 196612
  81.0 21.0 %copy-start.6 = (f32[128]{0:T(128)S(1)}, f32[128]{0:T(128)}, u32[]{:S(2)}) copy-start(f32[128]{0:T(128)} %param.12) | copy-start | bytes 1540
  81.6 20.3 %collective-permute-start.4 = (bf16[384,384]{1,0:T(8,128)(2,1)S(1)}, bf16[384,384]{1,0:T(8,128)(2,1)S(1)}, u32[]{:S(2)}, u32[]{:S(2)}) collective-permute-start(bf16[384,384]{1,0:T(8,128)(2,1)S(1)} %shard_map.112), channel_id=1, source_target_pairs={{0,8},{4,12},{8,0},{12,4},{1,9},{5,13},{9,1},{13,5},{2,10},{6,14},... | collective-permute-start | bytes 884744 | tf_op jit(solution)/shard_map/ppermute | solution.py:318
  92.3 12.3 %collective-permute-start.5 = (bf16[8,4,16,128]{3,2,1,0:T(8,128)(2,1)S(1)}, bf16[8,4,16,128]{3,2,1,0:T(8,128)(2,1)S(1)}, u32[]{:S(2)}, u32[]{:S(2)}) collective-permute-start(bf16[8,4,16,128]{3,2,1,0:T(8,128)(2,1)S(1)} %bitcast.11), channel_id=1, source_target_pairs={{0,128},{128,256},{256,384},{384,0},{1,129},{129,257},{257,385},{3... | collective-permute-start | bytes 393224 | tf_op jit(solution)/shard_map/ppermute | solution.py:320
  95.3 9.3 %collective-permute-start.6 = (bf16[8,4,16,128]{3,2,1,0:T(8,128)(2,1)S(1)}, bf16[8,4,16,128]{3,2,1,0:T(8,128)(2,1)S(1)}, u32[]{:S(2)}, u32[]{:S(2)}) collective-permute-start(bf16[8,4,16,128]{3,2,1,0:T(8,128)(2,1)S(1)} %bitcast.12), channel_id=1, source_target_pairs={{0,384},{128,0},{256,128},{384,256},{1,385},{129,1},{257,129},{385... | collective-permute-start | bytes 393224 | tf_op jit(solution)/shard_map/ppermute | solution.py:320
  100.0 9.5 %collective-permute-start.7 = (bf16[8,4,16,128]{3,2,1,0:T(8,128)(2,1)S(1)}, bf16[8,4,16,128]{3,2,1,0:T(8,128)(2,1)S(1)}, u32[]{:S(2)}, u32[]{:S(2)}) collective-permute-start(bf16[8,4,16,128]{3,2,1,0:T(8,128)(2,1)S(1)} %bitcast.13), channel_id=1, source_target_pairs={{0,256},{128,384},{256,0},{384,128},{1,257},{129,385},{257,1},{385... | collective-permute-start | bytes 393224 | tf_op jit(solution)/shard_map/ppermute | solution.py:320
  102.0 7.5 %copy-start.5 = (s32[128,2]{0,1:T(2,128)S(1)}, s32[128,2]{0,1:T(2,128)}, u32[]{:S(2)}) copy-start(s32[128,2]{0,1:T(2,128)} %param.20) | copy-start | bytes 3076
  102.0 7.5 %copy-start.7 = (f32[128]{0:T(128)S(1)}, f32[128]{0:T(128)}, u32[]{:S(2)}) copy-start(f32[128]{0:T(128)} %param.17) | copy-start | bytes 1540
  104.6 27.3 %copy-start.4 = (bf16[8,256]{1,0:T(8,128)(2,1)S(1)}, bf16[8,256]{1,0:T(8,128)(2,1)}, u32[]{:S(2)}) copy-start(bf16[8,256]{1,0:T(8,128)(2,1)} %acts_ref.1) | copy-start | bytes 12292

commit v8 on v7

--- a/solution.py
+++ b/solution.py
@@ -108,21 +108,18 @@
     return jnp.concatenate([tile[first + i : first + i + 1] for i in range(count)], axis=1)
 
 
-def fold_kernel(dec_ref, gains_ref, value_ref, out_ref, acc_ref):
-    step = pl.program_id(0)
-
-    @pl.when(step == 0)
-    def _():
-        acc_ref[...] = jnp.zeros_like(acc_ref)
-
-    chunk = value_ref.shape[1]
-    gain = gain_row(gains_ref[0], 8, chunk // gains_ref.shape[2])
-    dec = (dec_ref[...].reshape(-1, chunk).astype(F32) * gain).astype(BF16)
-    acc_ref[...] += dot(dec, value_ref[...], ((1,), (1,)))
-
-    @pl.when(step == pl.num_programs(0) - 1)
-    def _():
-        out_ref[...] = jnp.broadcast_to(acc_ref[...].astype(BF16)[None], out_ref.shape)
+def fold_kernel(near_ref, value_ref, out_ref):
+    senders, share, tall = near_ref.shape
+    width = value_ref.shape[1]
+    chunk, wide = width // senders, tall - width
+    total = None
+    for i in range(senders):
+        cols = slice(i * chunk, (i + 1) * chunk)
+        gain = gain_row(near_ref[i, 0:16, width:], 8, chunk // wide).astype(BF16)
+        dec = near_ref[:, :, cols].reshape(senders * share, chunk) * gain
+        part = dot(dec, value_ref[:, cols], ((1,), (1,)))
+        total = part if total is None else total + part
+    out_ref[...] = jnp.broadcast_to(total.astype(BF16)[None], out_ref.shape)
 
 
 def value_kernel(
@@ -297,17 +294,9 @@
     right = lax.ppermute(wide, "x", ring(nx, nx - 1))
     folded = pl.pallas_call(
         fold_kernel,
-        grid=(nx,),
-        in_specs=[
-            pl.BlockSpec((nx, share, chunk), lambda i: (0, 0, i)),
-            pl.BlockSpec((1, 16, rows), lambda i: (i, 0, width // rows)),
-            pl.BlockSpec((head, chunk), lambda i: (0, i)),
-        ],
-        out_specs=pl.BlockSpec((copies, nx * share, head), lambda i: (0, 0, 0)),
         out_shape=jax.ShapeDtypeStruct((copies, nx * share, head), BF16),
-        scratch_shapes=[pltpu.VMEM((nx * share, head), F32)],
-        compiler_params=PARAMS,
-    )(near, near, value_proj)
+        compiler_params=PARAMS,
+    )(near, value_proj)
     wide, folded = lax.optimization_barrier((wide, folded))
     folded = lax.all_to_all(folded, ("c", "y"), 0, 0)
     far = pl.pallas_call(

time: 135 us -> 134 us (level)
  the two profiles are of different devices: /device:TPU:24 before, /device:TPU:1 now
where the time goes in v8:
time: 134 us
  blocking collectives  86 us (64%)
  starting transfers between devices  34.1 us (25%)
  Pallas kernels  7.94 us (6%)
  waiting for transfers between devices  5.64 us (4%)
    all_gather x1, blocking collectives, shards(): columns = lax.all_gather(packed, 'zh', axis=0, tiled=False)  39.2 us
    all_to_all x1, blocking collectives, shards(): parts = lax.all_to_all(parts, TP, 0, 0, axis_index_groups=[group])  20.7 us
    all_to_all x1, blocking collectives, shards(): folded = lax.all_to_all(folded, ('c', 'y'), 0, 0)  14.4 us
    ppermute x1, starting transfers between devices, shards(): near = lax.ppermute(near, AXES, decoder_moves(sizes))  12 us
    all_gather x1, blocking collectives, shards(): lax.all_gather(jnp.concatenate([near, tail], axis=1), 'x', axis=0, tiled=...  11.7 us
    ppermute x3, starting transfers between devices, shards(): lax.ppermute(folded, 'zl', ring(nzl, k))  9.02 us
    ppermute x3, waiting for transfers between devices, shards(): lax.ppermute(folded, 'zl', ring(nzl, k))  5.63 us
    ppermute x1, starting transfers between devices, shards(): weights = lax.ppermute(weights, 'x', ring(nx, 2))  4.65 us
  transfers between devices with their start and end apart: 8, of which 2 were waited for; matrix products, arithmetic and copies ran while one was open for 0% of the time, Pallas kernels for 3%

profile of v8, /device:TPU:1, one launch (start us, length us, event | category | flops | bytes accessed | tf_op | source)
XLA Modules:
  0.0 134.0 jit_solution(12694903460195140239)
XLA Ops:
  0.0 2.4 %shard_map.109 = (bf16[304,384]{1,0:T(8,128)(2,1)}, bf16[384,1152]{1,0:T(8,128)(2,1)}, bf16[16,4608]{1,0:T(8,128)(2,1)}) custom-call(bf16[3,288,128]{2,1,0:T(8,128)(2,1)} %bitcast.17, bf16[256,4608]{1,0:T(8,128)(2,1)} %out_proj.3, bf16[128,4608]{1,0:T(8,128)(2,1)} %decoder.1, bf16[288]{0:T(512)(128)(2,1)} %post.1, bf16[288]{0:T(512)(128)(2,1)} %pre.1), custom_call_target="tpu_custom_call" | custom-call | tf_op jit(solution)/shard_map/pallas_call | solution.py:264
  2.4 12.0 %collective-permute-start = (bf16[16,4608]{1,0:T(8,128)(2,1)}, bf16[16,4608]{1,0:T(8,128)(2,1)S(1)}, u32[]{:S(2)}, u32[]{:S(2)}) collective-permute-start(bf16[16,4608]{1,0:T(8,128)(2,1)} %get-tuple-element.18), channel_id=1, source_target_pairs={{387,0},{384,1},{385,2},{386,3},{391,4},{388,5},{389,6},{390,7},{3... | collective-permute-start | bytes 442376 | tf_op jit(solution)/shard_map/ppermute | solution.py:279
  14.4 4.7 %collective-permute-start.3 = (bf16[384,1152]{1,0:T(8,128)(2,1)}, bf16[384,1152]{1,0:T(8,128)(2,1)S(1)}, u32[]{:S(2)}, u32[]{:S(2)}) collective-permute-start(bf16[384,1152]{1,0:T(8,128)(2,1)} %get-tuple-element.23), channel_id=1, source_target_pairs={{0,8},{4,12},{8,0},{12,4},{1,9},{5,13},{9,1},{13,5},{2,10},{6,14},... | collective-permute-start | bytes 2654216 | tf_op jit(solution)/shard_map/ppermute | solution.py:280
  19.0 39.2 %all-gather = bf16[1216,384]{1,0:T(8,128)(2,1)S(1)} all-gather(bf16[304,384]{1,0:T(8,128)(2,1)} %get-tuple-element.16), channel_id=2, replica_groups=mesh['zl'=4,'y'=4,'c'=2,'x'=4,'zh'=4] {'zh'}, dimensions={0}, use_global_device_ids=true | all-gather | bytes 1167360 | tf_op jit(solution)/shard_map/all_gather | solution.py:281
  58.2 0.1 shard_map.110
  58.4 11.7 %all-gather.1 = bf16[64,4992]{1,0:T(8,128)(2,1)S(1)} all-gather(bf16[16,4992]{1,0:T(8,128)(2,1)S(1)} %pad_maximum_fusion), channel_id=3, replica_groups=mesh['zl'=4,'y'=4,'c'=2,'x'=4,'zh'=4] {'x'}, dimensions={0}, use_global_device_ids=true | all-gather | bytes 798720 | tf_op jit(solution)/shard_map/all_gather | solution.py:291
  70.0 2.3 %collective-permute-start.1 = (bf16[1152,384]{1,0:T(8,128)(2,1)S(1)}, bf16[1152,384]{1,0:T(8,128)(2,1)S(1)}, u32[]{:S(2)}, u32[]{:S(2)}) collective-permute-start(bf16[1152,384]{1,0:T(8,128)(2,1)S(1)} %get-tuple-element.22.wide_ref.own), channel_id=1, source_target_pairs={{0,4},{4,8},{8,12},{12,0},{1,5},{5,9},{9,13},{13,1},{2,6},{6,10},{... | collective-permute-start | bytes 2654216 | tf_op jit(solution)/shard_map/ppermute | solution.py:293
  72.3 4.2 %collective-permute-start.2 = (bf16[1152,384]{1,0:T(8,128)(2,1)S(1)}, bf16[1152,384]{1,0:T(8,128)(2,1)S(1)}, u32[]{:S(2)}, u32[]{:S(2)}) collective-permute-start(bf16[1152,384]{1,0:T(8,128)(2,1)S(1)} %get-tuple-element.22.wide_ref.own), channel_id=1, source_target_pairs={{0,12},{4,0},{8,4},{12,8},{1,13},{5,1},{9,5},{13,9},{2,14},{6,2},{... | collective-permute-start | bytes 2654216 | tf_op jit(solution)/shard_map/ppermute | solution.py:294
  76.6 0.0 copy-start
  76.6 0.6 shard_map.111
  77.1 0.0 copy-start.3
  77.2 0.0 copy-start.6
  77.2 0.6 shard_map.112
  77.8 2.0 %collective-permute-start.4 = (bf16[384,384]{1,0:T(8,128)(2,1)S(1)}, bf16[384,384]{1,0:T(8,128)(2,1)S(1)}, u32[]{:S(2)}, u32[]{:S(2)}) collective-permute-start(bf16[384,384]{1,0:T(8,128)(2,1)S(1)} %shard_map.112), channel_id=1, source_target_pairs={{0,8},{4,12},{8,0},{12,4},{1,9},{5,13},{9,1},{13,5},{2,10},{6,14},... | collective-permute-start | bytes 884744 | tf_op jit(solution)/shard_map/ppermute | solution.py:307
  79.8 14.4 %all_to_all.10 = bf16[8,64,128]{2,1,0:T(8,128)(2,1)S(1)} all-to-all(bf16[8,64,128]{2,1,0:T(8,128)(2,1)S(1)} %shard_map.111), channel_id=1, replica_groups=mesh['zl'=4,'y'=4,'c'=2,'x'=4,'zh'=4] {'c','y'}, dimensions={0} | all-to-all | bytes 262144 | tf_op jit(solution)/shard_map/all_to_all | solution.py:301
  94.3 2.7 %collective-permute-start.5 = (bf16[8,4,16,128]{3,2,1,0:T(8,128)(2,1)S(1)}, bf16[8,4,16,128]{3,2,1,0:T(8,128)(2,1)S(1)}, u32[]{:S(2)}, u32[]{:S(2)}) collective-permute-start(bf16[8,4,16,128]{3,2,1,0:T(8,128)(2,1)S(1)} %bitcast.10), channel_id=1, source_target_pairs={{0,128},{128,256},{256,384},{384,0},{1,129},{129,257},{257,385},{3... | collective-permute-start | bytes 393224 | tf_op jit(solution)/shard_map/ppermute | solution.py:309
  97.0 4.4 %collective-permute-start.6 = (bf16[8,4,16,128]{3,2,1,0:T(8,128)(2,1)S(1)}, bf16[8,4,16,128]{3,2,1,0:T(8,128)(2,1)S(1)}, u32[]{:S(2)}, u32[]{:S(2)}) collective-permute-start(bf16[8,4,16,128]{3,2,1,0:T(8,128)(2,1)S(1)} %bitcast.11), channel_id=1, source_target_pairs={{0,384},{128,0},{256,128},{384,256},{1,385},{129,1},{257,129},{385... | collective-permute-start | bytes 393224 | tf_op jit(solution)/shard_map/ppermute | solution.py:309
  101.4 1.9 %collective-permute-start.7 = (bf16[8,4,16,128]{3,2,1,0:T(8,128)(2,1)S(1)}, bf16[8,4,16,128]{3,2,1,0:T(8,128)(2,1)S(1)}, u32[]{:S(2)}, u32[]{:S(2)}) collective-permute-start(bf16[8,4,16,128]{3,2,1,0:T(8,128)(2,1)S(1)} %bitcast.12), channel_id=1, source_target_pairs={{0,256},{128,384},{256,0},{384,128},{1,257},{129,385},{257,1},{385... | collective-permute-start | bytes 393224 | tf_op jit(solution)/shard_map/ppermute | solution.py:309
  103.4 2.6 %shard_map.113 = (bf16[384,128]{1,0:T(8,128)(2,1)S(1)}, f32[384,128]{1,0:T(8,128)S(1)}) custom-call(bf16[1152,384]{1,0:T(8,128)(2,1)S(1)} %get-tuple-element.22.wide_ref.own, bf16[1152,384]{1,0:T(8,128)(2,1)S(1)} %collective-permute-done.1.left, bf16[1152,384]{1,0:T(8,128)(2,1)S(1)} %collective-permute-done.2.right, ...), custom_call_target="tpu_custom_call" | custom-call | tf_op jit(solution)/shard_map/pallas_call | solution.py:311
  106.0 0.2 collective-permute-done.6.m2
  106.2 5.4 %collective-permute-done.7.m3 = bf16[8,4,16,128]{3,2,1,0:T(8,128)(2,1)S(1)} collective-permute-done((bf16[8,4,16,128]{3,2,1,0:T(8,128)(2,1)S(1)}, bf16[8,4,16,128]{3,2,1,0:T(8,128)(2,1)S(1)}, u32[]{:S(2)}, u32[]{:S(2)}) %collective-permute-start.7) | collective-permute-done | bytes 131104 | tf_op jit(solution)/shard_map/ppermute | solution.py:309
  111.6 1.0 shard_map.114
  112.7 20.7 %all_to_all.11.parts_ref = bf16[16,16,384]{2,1,0:T(8,128)(2,1)S(1)} all-to-all(bf16[16,16,384]{2,1,0:T(8,128)(2,1)S(1)} %shard_map.114), channel_id=1, replica_groups={{10,11,8,9,14,15,12,13,2,3,0,1,6,7,4,5},{26,27,24,25,30,31,28,29,18,19,..., dimensions={0} | all-to-all | bytes 393216 | tf_op jit(solution)/shard_map/all_to_all | solution.py:335
  133.4 0.6 shard_map.115
  (20 shorter events, 0.1 us)
Async XLA Ops:
  2.4 55.9 %collective-permute-start = (bf16[16,4608]{1,0:T(8,128)(2,1)}, bf16[16,4608]{1,0:T(8,128)(2,1)S(1)}, u32[]{:S(2)}, u32[]{:S(2)}) collective-permute-start(bf16[16,4608]{1,0:T(8,128)(2,1)} %get-tuple-element.18), channel_id=1, source_target_pairs={{387,0},{384,1},{385,2},{386,3},{391,4},{388,5},{389,6},{390,7},{3... | collective-permute-start | bytes 442376 | tf_op jit(solution)/shard_map/ppermute | solution.py:279
  14.4 62.8 %collective-permute-start.3 = (bf16[384,1152]{1,0:T(8,128)(2,1)}, bf16[384,1152]{1,0:T(8,128)(2,1)S(1)}, u32[]{:S(2)}, u32[]{:S(2)}) collective-permute-start(bf16[384,1152]{1,0:T(8,128)(2,1)} %get-tuple-element.23), channel_id=1, source_target_pairs={{0,8},{4,12},{8,0},{12,4},{1,9},{5,13},{9,1},{13,5},{2,10},{6,14},... | collective-permute-start | bytes 2654216 | tf_op jit(solution)/shard_map/ppermute | solution.py:280
  58.2 18.3 %copy-start.2 = (bf16[128,4608]{1,0:T(8,128)(2,1)S(1)}, bf16[128,4608]{1,0:T(8,128)(2,1)}, u32[]{:S(2)}) copy-start(bf16[128,4608]{1,0:T(8,128)(2,1)} %value_ref.1) | copy-start | bytes 3538948
  70.0 31.3 %collective-permute-start.1 = (bf16[1152,384]{1,0:T(8,128)(2,1)S(1)}, bf16[1152,384]{1,0:T(8,128)(2,1)S(1)}, u32[]{:S(2)}, u32[]{:S(2)}) collective-permute-start(bf16[1152,384]{1,0:T(8,128)(2,1)S(1)} %get-tuple-element.22.wide_ref.own), channel_id=1, source_target_pairs={{0,4},{4,8},{8,12},{12,0},{1,5},{5,9},{9,13},{13,1},{2,6},{6,10},{... | collective-permute-start | bytes 2654216 | tf_op jit(solution)/shard_map/ppermute | solution.py:293
  72.3 31.0 %collective-permute-start.2 = (bf16[1152,384]{1,0:T(8,128)(2,1)S(1)}, bf16[1152,384]{1,0:T(8,128)(2,1)S(1)}, u32[]{:S(2)}, u32[]{:S(2)}) collective-permute-start(bf16[1152,384]{1,0:T(8,128)(2,1)S(1)} %get-tuple-element.22.wide_ref.own), channel_id=1, source_target_pairs={{0,12},{4,0},{8,4},{12,8},{1,13},{5,1},{9,5},{13,9},{2,14},{6,2},{... | collective-permute-start | bytes 2654216 | tf_op jit(solution)/shard_map/ppermute | solution.py:294
  76.6 26.8 %copy-start = (bf16[256,4608]{1,0:T(8,128)(2,1)S(1)}, bf16[256,4608]{1,0:T(8,128)(2,1)}, u32[]{:S(2)}) copy-start(bf16[256,4608]{1,0:T(8,128)(2,1)} %out_proj.3) | copy-start | bytes 7077892
  77.1 26.2 %copy-start.1 = (bf16[128,4608]{1,0:T(8,128)(2,1)S(1)}, bf16[128,4608]{1,0:T(8,128)(2,1)}, u32[]{:S(2)}) copy-start(bf16[128,4608]{1,0:T(8,128)(2,1)} %decoder.1) | copy-start | bytes 3538948
  77.1 26.2 %copy-start.3 = (bf16[2,128,128]{2,1,0:T(8,128)(2,1)S(1)}, bf16[2,128,128]{2,1,0:T(8,128)(2,1)}, u32[]{:S(2)}) copy-start(bf16[2,128,128]{2,1,0:T(8,128)(2,1)} %patterns_ref.1) | copy-start | bytes 196612
  77.2 26.2 %copy-start.6 = (f32[128]{0:T(128)S(1)}, f32[128]{0:T(128)}, u32[]{:S(2)}) copy-start(f32[128]{0:T(128)} %param.12) | copy-start | bytes 1540
  77.8 25.5 %collective-permute-start.4 = (bf16[384,384]{1,0:T(8,128)(2,1)S(1)}, bf16[384,384]{1,0:T(8,128)(2,1)S(1)}, u32[]{:S(2)}, u32[]{:S(2)}) collective-permute-start(bf16[384,384]{1,0:T(8,128)(2,1)S(1)} %shard_map.112), channel_id=1, source_target_pairs={{0,8},{4,12},{8,0},{12,4},{1,9},{5,13},{9,1},{13,5},{2,10},{6,14},... | collective-permute-start | bytes 884744 | tf_op jit(solution)/shard_map/ppermute | solution.py:307
  94.3 11.7 %collective-permute-start.5 = (bf16[8,4,16,128]{3,2,1,0:T(8,128)(2,1)S(1)}, bf16[8,4,16,128]{3,2,1,0:T(8,128)(2,1)S(1)}, u32[]{:S(2)}, u32[]{:S(2)}) collective-permute-start(bf16[8,4,16,128]{3,2,1,0:T(8,128)(2,1)S(1)} %bitcast.10), channel_id=1, source_target_pairs={{0,128},{128,256},{256,384},{384,0},{1,129},{129,257},{257,385},{3... | collective-permute-start | bytes 393224 | tf_op jit(solution)/shard_map/ppermute | solution.py:309
  97.0 9.3 %collective-permute-start.6 = (bf16[8,4,16,128]{3,2,1,0:T(8,128)(2,1)S(1)}, bf16[8,4,16,128]{3,2,1,0:T(8,128)(2,1)S(1)}, u32[]{:S(2)}, u32[]{:S(2)}) collective-permute-start(bf16[8,4,16,128]{3,2,1,0:T(8,128)(2,1)S(1)} %bitcast.11), channel_id=1, source_target_pairs={{0,384},{128,0},{256,128},{384,256},{1,385},{129,1},{257,129},{385... | collective-permute-start | bytes 393224 | tf_op jit(solution)/shard_map/ppermute | solution.py:309
  101.4 10.2 %collective-permute-start.7 = (bf16[8,4,16,128]{3,2,1,0:T(8,128)(2,1)S(1)}, bf16[8,4,16,128]{3,2,1,0:T(8,128)(2,1)S(1)}, u32[]{:S(2)}, u32[]{:S(2)}) collective-permute-start(bf16[8,4,16,128]{3,2,1,0:T(8,128)(2,1)S(1)} %bitcast.12), channel_id=1, source_target_pairs={{0,256},{128,384},{256,0},{384,128},{1,257},{129,385},{257,1},{385... | collective-permute-start | bytes 393224 | tf_op jit(solution)/shard_map/ppermute | solution.py:309
  103.4 8.3 %copy-start.5 = (s32[128,2]{0,1:T(2,128)S(1)}, s32[128,2]{0,1:T(2,128)}, u32[]{:S(2)}) copy-start(s32[128,2]{0,1:T(2,128)} %param.20) | copy-start | bytes 3076
  103.4 8.2 %copy-start.7 = (f32[128]{0:T(128)S(1)}, f32[128]{0:T(128)}, u32[]{:S(2)}) copy-start(f32[128]{0:T(128)} %param.17) | copy-start | bytes 1540
  106.0 27.4 %copy-start.4 = (bf16[8,256]{1,0:T(8,128)(2,1)S(1)}, bf16[8,256]{1,0:T(8,128)(2,1)}, u32[]{:S(2)}) copy-start(bf16[8,256]{1,0:T(8,128)(2,1)} %acts_ref.1) | copy-start | bytes 12292
